TPU v7x, 256 devices: a whole 4x4x8 slice. The times are simulated.
256 devices in a mesh: section: 4 (over z_lo), ctx: 64 (over z_hi, x, y, core).
Axes of the slice: x: 4, y: 4, z: 8 (z_hi: 2, z_lo: 4; z = z_hi * 4 + z_lo), core: 2. Of those that a mesh axis runs over, the one named last changes fastest.
Arguments:
- queries: bfloat16 [512, 4096], P('section', 'ctx'), may hold values from -160 to 160
- keys: bfloat16 [32768, 4096], P(('section', 'ctx')), may hold values from -16 to 16
- values: bfloat16 [32768, 4096], P(('section', 'ctx')), may hold values from -6 to 6
- out_grad: bfloat16 [512, 4096], P('section', 'ctx'), may hold values from -12 to 12
- key_mask: int32 [32768], P(('section', 'ctx')), may hold values 0 or 1
- query_mask: int32 [512], P('section'), may hold values 0 or 1
Outputs:
- grad_queries: bfloat16 [512, 4096], P('section', 'ctx')
- grad_keys: bfloat16 [32768, 4096], P(('section', 'ctx'))
- grad_values: bfloat16 [32768, 4096], P(('section', 'ctx'))
All inputs are finite; a program needn't handle non-finite values. No bound on the sum of `key_mask` or of `query_mask` on one device may be relied on, other than what follows from the above.
Results may differ from a plain program's by a relative error of at most 0.019.
Values may be sent and summed in bfloat16 or wider, within the bound.
No kernel may reach another device: no remote copies, remote signals or barrier semaphores. Data moves between devices by JAX's collectives and lax.ppermute only.
A program may use at most 128 MiB of HBM per device.

v0:
```python
import math

import jax
import jax.numpy as jnp
from jax import lax
from jax.sharding import PartitionSpec as P

HD = 64


masked_bias = -1000000000.0


def block_view(key_rows, value_rows, mask_rows):
    total_rows = key_rows.shape[0]
    block_rows = math.gcd(total_rows, 2048)
    blocks = total_rows // block_rows
    head_count = key_rows.shape[1] // HD
    key_blocks = key_rows.reshape(blocks, block_rows, head_count, HD)
    value_blocks = value_rows.reshape(blocks, block_rows, head_count, HD)
    bias_blocks = (
        jnp.where(mask_rows == 1, 0.0, masked_bias).astype(jnp.float32).reshape(blocks, block_rows)
    )
    return (key_blocks, value_blocks, bias_blocks)


def score_block(query_heads, key_block, bias_row, factor):
    product = jnp.einsum("qhd,khd->qhk", query_heads, key_block, preferred_element_type=jnp.float32)
    return product * factor + bias_row[None, None, :]


def running_stats(query_heads, key_blocks, bias_blocks, factor):
    start_stats = (
        jnp.full(query_heads.shape[:2], -1e30, jnp.float32),
        jnp.zeros(query_heads.shape[:2], jnp.float32),
    )

    def running_one_block(running, inputs):
        highest, summed = running
        key_block, bias_row = inputs
        logits = score_block(query_heads, key_block, bias_row, factor)
        new_highest = jnp.maximum(highest, jnp.max(logits, axis=2))
        summed = summed * jnp.exp(highest - new_highest) + jnp.sum(
            jnp.exp(logits - new_highest[:, :, None]), axis=2
        )
        return ((new_highest, summed), None)

    (highest, summed), unused = lax.scan(running_one_block, start_stats, (key_blocks, bias_blocks))
    return (highest, summed)


def output_pass(query_heads, key_blocks, value_blocks, bias_blocks, log_total, factor):

    def output_one_block(running, inputs):
        key_block, value_block, bias_row = inputs
        logits = score_block(query_heads, key_block, bias_row, factor)
        weights_low = jnp.exp(logits - log_total[:, :, None]).astype(jnp.bfloat16)
        running = running + jnp.einsum(
            "qhk,khd->qhd", weights_low, value_block, preferred_element_type=jnp.float32
        )
        return (running, None)

    start_output = jnp.zeros(query_heads.shape, jnp.float32)
    attended, unused = lax.scan(
        output_one_block, start_output, (key_blocks, value_blocks, bias_blocks)
    )
    return attended


def backward_pass(
    query_heads, grad_heads, key_blocks, value_blocks, bias_blocks, log_total, row_inner, factor
):

    def backward_one_block(running, inputs):
        key_block, value_block, bias_row = inputs
        logits = score_block(query_heads, key_block, bias_row, factor)
        weights = jnp.exp(logits - log_total[:, :, None])
        weights_low = weights.astype(jnp.bfloat16)
        grad_probs = jnp.einsum(
            "qhd,khd->qhk", grad_heads, value_block, preferred_element_type=jnp.float32
        )
        grad_logits = (weights * (grad_probs - row_inner[:, :, None])).astype(jnp.bfloat16)
        grad_value = jnp.einsum(
            "qhk,qhd->khd", weights_low, grad_heads, preferred_element_type=jnp.float32
        )
        grad_key = (
            jnp.einsum("qhk,qhd->khd", grad_logits, query_heads, preferred_element_type=jnp.float32)
            * factor
        )
        running = running + jnp.einsum(
            "qhk,khd->qhd", grad_logits, key_block, preferred_element_type=jnp.float32
        )
        return (running, (grad_key, grad_value))

    start_grad = jnp.zeros(query_heads.shape, jnp.float32)
    grad_query, (key_grads, value_grads) = lax.scan(
        backward_one_block, start_grad, (key_blocks, value_blocks, bias_blocks)
    )
    total_rows = key_grads.shape[0] * key_grads.shape[1]
    width = key_grads.shape[2] * key_grads.shape[3]
    return (
        grad_query * factor,
        key_grads.reshape(total_rows, width),
        value_grads.reshape(total_rows, width),
    )


def per_device(queries, keys, values, out_grad, key_mask, query_mask):
    factor = 1.0 / math.sqrt(HD)
    grad_rows = out_grad * query_mask[:, None].astype(jnp.bfloat16)
    head_keys, head_values = (
        lax.all_to_all(keys, "ctx", split_axis=1, concat_axis=0, tiled=True),
        lax.all_to_all(values, "ctx", split_axis=1, concat_axis=0, tiled=True),
    )
    group_mask = lax.all_gather(key_mask, "ctx", axis=0, tiled=True)
    width = head_keys.shape[1]
    head_count = width // HD
    all_keys, all_values, all_mask = (
        lax.all_gather(head_keys, "section", axis=0, tiled=True),
        lax.all_gather(head_values, "section", axis=0, tiled=True),
        lax.all_gather(group_mask, "section", axis=0, tiled=True),
    )
    key_blocks, value_blocks, bias_blocks = block_view(all_keys, all_values, all_mask)
    query_heads = queries.reshape(queries.shape[0], head_count, HD)
    grad_heads = grad_rows.reshape(grad_rows.shape[0], head_count, HD)
    highest, summed = running_stats(query_heads, key_blocks, bias_blocks, factor)
    log_total = highest + jnp.log(summed)
    attended = output_pass(query_heads, key_blocks, value_blocks, bias_blocks, log_total, factor)
    row_inner = jnp.sum(grad_heads.astype(jnp.float32) * attended, axis=2)
    grad_query, key_grads, value_grads = backward_pass(
        query_heads, grad_heads, key_blocks, value_blocks, bias_blocks, log_total, row_inner, factor
    )
    joined = jnp.concatenate((key_grads, value_grads), axis=1)
    shares = lax.psum_scatter(
        joined.astype(jnp.bfloat16), "section", scatter_dimension=0, tiled=True
    ).astype(jnp.float32)
    key_share = shares[:, :width].astype(jnp.bfloat16)
    value_share = shares[:, width:].astype(jnp.bfloat16)
    grad_queries = grad_query.reshape(queries.shape[0], width).astype(jnp.bfloat16)
    grad_keys, grad_values = (
        lax.all_to_all(key_share, "ctx", split_axis=0, concat_axis=1, tiled=True),
        lax.all_to_all(value_share, "ctx", split_axis=0, concat_axis=1, tiled=True),
    )
    return (grad_queries, grad_keys, grad_values)


def solution(mesh):
    placed = (
        P("section", "ctx"),
        P(("section", "ctx"), None),
        P(("section", "ctx"), None),
        P("section", "ctx"),
        P(("section", "ctx")),
        P("section"),
    )
    return jax.shard_map(
        per_device,
        mesh=mesh,
        in_specs=placed,
        out_specs=(P("section", "ctx"), P(("section", "ctx"), None), P(("section", "ctx"), None)),
        check_vma=False,
    )
```

profile of v0, /device:TPU:1, one launch (start us, length us, event | category | flops | bytes accessed | tf_op | source)
XLA Modules:
  0.0 688.9 jit_solution(4994626883550804577)
XLA Ops:
  8.9 38.8 %all_to_all.76 = bf16[128,64,64]{0,2,1:T(8,128)(2,1)S(1)} all-to-all(bf16[128,64,64]{0,2,1:T(8,128)(2,1)S(1)} %bitcast.272), channel_id=1, replica_groups=mesh['section'=4,'ctx'=64] {'ctx'}, dimensions={1} | all-to-all | bytes 2097152 | tf_op jit(solution)/shard_map/all_to_all | solution.py:112
  50.2 12.4 %all-to-all-start.1 = ((bf16[128,64,64]{0,2,1:T(8,128)(2,1)}), bf16[128,64,64]{0,2,1:T(8,128)(2,1)S(1)}, u32[]{:S(2)}, u32[]{:S(2)}) async-start(bf16[128,64,64]{0,2,1:T(8,128)(2,1)} %bitcast.5), calls=%async_computation.1 | async-start | bytes 2097152 | tf_op jit(solution)/shard_map/all_to_all | solution.py:113
  62.8 130.7 %all-gather = s32[64,1,128]{2,1,0:T(1,128)S(1)} all-gather(s32[1,1,128]{2,1,0:T(1,128)S(1)} %bitcast.283), channel_id=1, replica_groups=mesh['section'=4,'ctx'=64] {'ctx'}, dimensions={0}, use_global_device_ids=true | all-gather | bytes 33280 | tf_op jit(solution)/shard_map/all_gather | solution.py:115
  193.5 34.3 %all_gather.14 = s32[32768]{0:T(1024)S(1)} all-gather(s32[8192]{0:T(1024)S(1)} %bitcast.277), channel_id=1, replica_groups=mesh['section'=4,'ctx'=64] {'section'}, dimensions={0}, use_global_device_ids=true | all-gather | bytes 163840 | tf_op jit(solution)/shard_map/all_gather | solution.py:121
  229.1 4.6 copy.61
  233.7 4.3 copy.49
  237.9 29.5 %while.39 = (s32[]{:T(128)}, f32[128,1]{0,1:T(1,128)S(1)}, f32[128,1]{0,1:T(1,128)S(1)}, bf16[16,2048,1,64]{1,3,2,0:T(8,128)(2,1)}, bf16[128,1,64]{0,2,1:T(8,128...) while((s32[]{:T(128)}, f32[128,1]{0,1:T(1,128)S(1)}, f32[128,1]{0,1:T(1,128)S(1)}, ...), condition=%wide.region_3.4_spmd.clone, body=%wide.region_0.3_spmd.clone.sunk | while | flops 34865792 | bytes 2407024 | solution.py:48
  267.4 44.2 %all-gather.6.cloned.1.call-done = bf16[32768,64]{0,1:T(8,128)(2,1)} async-done(((bf16[8192,64]{0,1:T(8,128)(2,1)}), bf16[32768,64]{0,1:T(8,128)(2,1)}) %all-gather.6.cloned.1.call-update) | async-done | bytes 4194320 | tf_op jit(solution)/shard_map/all_gather | solution.py:120
  311.7 4.6 copy.62
  316.3 4.2 copy.50
  320.5 27.9 %while.40 = (s32[]{:T(128)}, f32[128,1,64]{0,2,1:T(8,128)S(1)}, bf16[16,2048,1,64]{1,3,2,0:T(8,128)(2,1)}, bf16[16,2048,1,64]{1,3,2,0:T(8,128)(2,1)}, bf16[128,1...) while((s32[]{:T(128)}, f32[128,1,64]{0,2,1:T(8,128)S(1)}, ...), condition=%wide.region_5.6_spmd.clone, body=%wide.region_4.5_spmd.clone.sunk | while | flops 68173824 | bytes 632946 | solution.py:64
  320.5 1.7 fusion.88
  322.3 1.7 fusion.88
  324.0 1.7 fusion.88
  325.8 1.7 fusion.88
  327.5 1.7 fusion.88
  329.2 1.7 fusion.88
  334.5 1.7 fusion.88
  336.2 1.7 fusion.88
  337.9 1.7 fusion.88
  339.7 1.7 fusion.88
  341.4 1.7 fusion.88
  343.2 1.7 fusion.88
  348.4 96.0 %while.41 = (s32[]{:T(128)}, f32[128,1,64]{0,2,1:T(8,128)S(1)}, bf16[16,2048,1,64]{1,3,2,0:T(8,128)(2,1)}, bf16[16,2048,1,64]{1,3,2,0:T(8,128)(2,1)}, bf16[16,20...) while((s32[]{:T(128)}, f32[128,1,64]{0,2,1:T(8,128)S(1)}, ...), condition=%wide.region_8.9_spmd.clone, body=%wide.region_7.8_spmd.clone.sunk | while | flops 169754624 | bytes 6710439 | solution.py:96
  444.4 4.8 copy.64
  449.2 2.3 copy.63
  451.5 7.4 %pad_maximum_fusion = bf16[32768,128]{0,1:T(8,128)(2,1)} fusion(bf16[32768,64]{0,1:T(8,128)(2,1)} %bitcast.264, bf16[32768,64]{0,1:T(8,128)(2,1)} %bitcast.265), kind=kLoop, calls=%fused_computation.67 | loop fusion | flops 16777216 | bytes 16777216 | tf_op jit(solution)/shard_map/concatenate | solution.py:133
  458.9 149.9 %reduce-scatter.2.cloned.1.call-done = bf16[8192,128]{0,1:T(8,128)(2,1)} async-done(((bf16[32768,128]{0,1:T(8,128)(2,1)}), bf16[8192,128]{0,1:T(8,128)(2,1)}) %reduce-scatter.2.cloned.1.call-update) | async-done | bytes 2097168 | tf_op jit(solution)/shard_map/reduce_scatter | solution.py:134
  611.8 11.9 %all-to-all-start.3 = ((bf16[64,128,64]{1,2,0:T(8,128)(2,1)}), bf16[64,128,64]{1,2,0:T(8,128)(2,1)S(1)}, u32[]{:S(2)}, u32[]{:S(2)}) async-start(bf16[64,128,64]{1,2,0:T(8,128)(2,1)} %bitcast.194), calls=%async_computation.4 | async-start | bytes 2097152 | tf_op jit(solution)/shard_map/all_to_all | solution.py:142
  625.0 21.5 %all-to-all-done.3 = bf16[64,128,64]{1,2,0:T(8,128)(2,1)S(1)} async-done(((bf16[64,128,64]{1,2,0:T(8,128)(2,1)}), bf16[64,128,64]{1,2,0:T(8,128)(2,1)S(1)}, u32[]{:S(2)}, u32[]{:S(2)}) %all-to-all-start.3) | async-done | bytes 1048608 | tf_op jit(solution)/shard_map/all_to_all | solution.py:142
  646.5 13.4 %all-to-all-start.2 = ((bf16[64,128,64]{1,2,0:T(8,128)(2,1)}), bf16[64,128,64]{1,2,0:T(8,128)(2,1)S(1)}, u32[]{:S(2)}, u32[]{:S(2)}) async-start(bf16[64,128,64]{1,2,0:T(8,128)(2,1)} %bitcast.195), calls=%async_computation.3 | async-start | bytes 2097152 | tf_op jit(solution)/shard_map/all_to_all | solution.py:141
  661.8 19.2 %all-to-all-done.2 = bf16[64,128,64]{1,2,0:T(8,128)(2,1)S(1)} async-done(((bf16[64,128,64]{1,2,0:T(8,128)(2,1)}), bf16[64,128,64]{1,2,0:T(8,128)(2,1)S(1)}, u32[]{:S(2)}, u32[]{:S(2)}) %all-to-all-start.2) | async-done | bytes 1048608 | tf_op jit(solution)/shard_map/all_to_all | solution.py:141
  (253 shorter events, 144.5 us)
Async XLA Ops:
  7.2 41.7 %copy-start.2 = (bf16[128,4096]{1,0:T(8,128)(2,1)S(1)}, bf16[128,4096]{1,0:T(8,128)(2,1)}, u32[]{:S(2)}) copy-start(bf16[128,4096]{1,0:T(8,128)(2,1)} %param.14) | copy-start | bytes 3145732
  7.2 221.9 %all-gather.4.cloned.1.call-start = ((), (), s32[]{:S(2)}) async-start(), calls=%async_computation.5 | async-start | bytes 5242880 | tf_op jit(solution)/shard_map/all_gather | solution.py:119
  47.8 15.0 %copy-start.5 = (s32[128]{0:T(128)S(1)}, s32[128]{0:T(128)}, u32[]{:S(2)}) copy-start(s32[128]{0:T(128)} %param.17) | copy-start | bytes 1540
  47.8 15.0 %copy-start.4 = (s32[128]{0:T(128)S(1)}, s32[128]{0:T(128)}, u32[]{:S(2)}) copy-start(s32[128]{0:T(128)} %param.16) | copy-start | bytes 1540
  50.2 177.6 %all-to-all-start.1 = ((bf16[128,64,64]{0,2,1:T(8,128)(2,1)}), bf16[128,64,64]{0,2,1:T(8,128)(2,1)S(1)}, u32[]{:S(2)}, u32[]{:S(2)}) async-start(bf16[128,64,64]{0,2,1:T(8,128)(2,1)} %bitcast.5), calls=%async_computation.1 | async-start | bytes 2097152 | tf_op jit(solution)/shard_map/all_to_all | solution.py:113
  62.6 249.1 %all-gather.6.cloned.1.call-start = ((), (), s32[]{:S(2)}) async-start(), calls=%async_computation.6 | async-start | bytes 5242880 | tf_op jit(solution)/shard_map/all_gather | solution.py:120
  229.0 379.9 %reduce-scatter.2.cloned.1.call-start = ((), (), s32[]{:S(2)}) async-start(), calls=%async_computation.7 | async-start | bytes 10485760 | tf_op jit(solution)/shard_map/reduce_scatter | solution.py:134
  233.6 4.3 copy-start.1
  320.5 27.9 %copy-start.3 = (bf16[128,64]{0,1:T(8,128)(2,1)S(1)}, bf16[128,64]{0,1:T(8,128)(2,1)}, u32[]{:S(2)}) copy-start(bf16[128,64]{0,1:T(8,128)(2,1)} %param.15) | copy-start | bytes 49156
  444.4 4.9 copy-start
  611.8 34.7 %all-to-all-start.3 = ((bf16[64,128,64]{1,2,0:T(8,128)(2,1)}), bf16[64,128,64]{1,2,0:T(8,128)(2,1)S(1)}, u32[]{:S(2)}, u32[]{:S(2)}) async-start(bf16[64,128,64]{1,2,0:T(8,128)(2,1)} %bitcast.194), calls=%async_computation.4 | async-start | bytes 2097152 | tf_op jit(solution)/shard_map/all_to_all | solution.py:142
  646.5 34.5 %all-to-all-start.2 = ((bf16[64,128,64]{1,2,0:T(8,128)(2,1)}), bf16[64,128,64]{1,2,0:T(8,128)(2,1)S(1)}, u32[]{:S(2)}, u32[]{:S(2)}) async-start(bf16[64,128,64]{1,2,0:T(8,128)(2,1)} %bitcast.195), calls=%async_computation.3 | async-start | bytes 2097152 | tf_op jit(solution)/shard_map/all_to_all | solution.py:141
Sparse Core Ops, SparseCore 0:
  49.0 106.6 all-gather.3
  229.1 82.5 all-gather.5
  459.1 149.7 reduce-scatter.1
where the time goes:
time: 701 us; the launch traced here: 689 us
  waiting for transfers between devices  235 us (34%)
  blocking collectives  204 us (29%)
  matrix products  146 us (21%)
  starting transfers between devices  37.8 us (5%)
  local copies, waits for them, and re-layouts  37.5 us (5%)
  between operations  13.9 us (2%)
  other arithmetic  13.2 us (2%)
    reduce_scatter x1, waiting for transfers between devices, per_device(): lax.psum_scatter(joined.astype(jnp.bfloat16), 'section', scatter_dimensio...  150 us
    all_gather x1, blocking collectives, per_device(): group_mask = lax.all_gather(key_mask, 'ctx', axis=0, tiled=True)  131 us
    dot_general x32, matrix products, score_block(): jnp.einsum('qhd,khd->qhk', query_heads, key_block, preferred_element_type...  46.8 us
    all_gather x1, waiting for transfers between devices, per_device(): lax.all_gather(head_values, 'section', axis=0, tiled=True)  44.2 us
    all_to_all x1, blocking collectives, per_device(): lax.all_to_all(keys, 'ctx', split_axis=1, concat_axis=0, tiled=True)  38.8 us
    all_gather x1, blocking collectives, per_device(): lax.all_gather(group_mask, 'section', axis=0, tiled=True)  34.3 us
    unnamed x23, local copies, waits for them, and re-layouts  32.1 us
    dot_general x16, matrix products, output_one_block(): jnp.einsum('qhk,khd->qhd', weights_low, value_block, preferred_element_ty...  27.1 us
  transfers between devices with their start and end apart: 6, of which 4 were waited for; matrix products, arithmetic and copies ran while one was open for 6% of the time, Pallas kernels for 0%

commit v1 on v0

v1 whole, which is shorter than its diff:
```python
import functools
import math

import jax
import jax.numpy as jnp
from jax import lax
from jax.experimental import pallas as pl
from jax.experimental.pallas import tpu as pltpu
from jax.sharding import Mesh
from jax.sharding import PartitionSpec as P

HD = 64
LANES = 128
TOKENS = 512
ROWS = 128
EXTRA = 16
FACTOR = 1.0 / math.sqrt(HD)
MASKED_BIAS = -1000000000.0
AXES = ("s", "h", "x", "y", "c")
PLANE = ("x", "y", "c")
COLUMN = ("s", "h")
PEERS = 32
LAYERS = 8
f32 = jnp.float32
bf16 = jnp.bfloat16
NT = (((1,), (1,)), ((), ()))
NN = (((1,), (0,)), ((), ()))


def dot(a, b, dims=NN):
    return lax.dot_general(a, b, dims, preferred_element_type=f32)


def pack_kernel(k_ref, v_ref, m_ref, kp_ref, vp_ref):
    half = k_ref.shape[1] // 2
    for src, dst in ((k_ref, kp_ref), (v_ref, vp_ref)):
        for j in range(0, PEERS, 2):
            low = src[:, j * HD : j * HD + LANES]
            high = src[:, half + j * HD : half + j * HD + LANES]
            dst[j, :ROWS, :] = jnp.concatenate([low[:, :HD], high[:, :HD]], axis=1)
            dst[j + 1, :ROWS, :] = jnp.concatenate([low[:, HD:], high[:, HD:]], axis=1)
    mask = jnp.broadcast_to(m_ref[...].astype(f32), (EXTRA, LANES)).astype(bf16)
    for j in range(PEERS):
        kp_ref[j, ROWS:, :] = mask


def unpack_kernel(k_ref, v_ref, ko_ref, vo_ref):
    half = ko_ref.shape[1] // 2
    for src, dst in ((k_ref, ko_ref), (v_ref, vo_ref)):
        for j in range(0, PEERS, 2):
            a = src[j]
            b = src[j + 1]
            dst[:, j * HD : j * HD + LANES] = jnp.concatenate([a[:, :HD], b[:, :HD]], axis=1)
            dst[:, half + j * HD : half + j * HD + LANES] = jnp.concatenate(
                [a[:, HD:], b[:, HD:]], axis=1
            )


def spread_tokens(t_ref, q_s, d_s, qt_s, dt_s):
    lane = lax.broadcasted_iota(jnp.int32, (ROWS, LANES), 1)
    for block in range(TOKENS // ROWS):
        for head in range(2):
            both = t_ref[2 * block + head].astype(f32)
            turned = pltpu.roll(both, HD, 1)
            mine = (lane < HD) if head == 0 else (lane >= HD)
            q, d = (both, turned) if head == 0 else (turned, both)
            q = jnp.where(mine, q * FACTOR, 0.0)
            d = jnp.where(mine, d, 0.0)
            at = pl.ds(block * ROWS, ROWS)
            if q_s is not None:
                q_s[head, at, :] = q.astype(bf16)
                d_s[head, at, :] = d.astype(bf16)
            qt_s[head, :, at] = q.T.astype(bf16)
            dt_s[head, :, at] = d.T.astype(bf16)


def bias_of(k_ref, b):
    row = k_ref[b, ROWS : ROWS + EXTRA, :].astype(f32)
    square = jnp.broadcast_to(row[:1, :], (LANES, LANES)).T
    bias = jnp.where(square == 1.0, 0.0, MASKED_BIAS)
    return jnp.concatenate([bias] * (TOKENS // LANES), axis=1)


def stats_kernel(t_ref, k_ref, v_ref, o_ref, qt_s, dt_s, m_s, z_s, s_s):
    step = pl.program_id(0)

    @pl.when(step == 0)
    def _():
        spread_tokens(t_ref, None, None, qt_s, dt_s)
        m_s[...] = jnp.full(m_s.shape, -3e38, f32)
        z_s[...] = jnp.zeros(z_s.shape, f32)
        s_s[...] = jnp.zeros(s_s.shape, f32)

    for b in range(k_ref.shape[0]):
        bias = bias_of(k_ref, b)
        keys = k_ref[b, :ROWS, :]
        values = v_ref[b]
        for head in range(2):
            logits = dot(keys, qt_s[head]) + bias
            probs = dot(values, dt_s[head])
            split = (ROWS // 8, 8, TOKENS)
            logits = logits.reshape(split)
            old = m_s[head]
            new = jnp.maximum(old, jnp.max(logits, axis=0))
            scale = jnp.exp(old - new)
            weights = jnp.exp(logits - new[None])
            m_s[head] = new
            z_s[head] = z_s[head] * scale + jnp.sum(weights, axis=0)
            s_s[head] = s_s[head] * scale + jnp.sum(weights * probs.reshape(split), axis=0)

    @pl.when(step == pl.num_programs(0) - 1)
    def _():
        o_ref[...] = jnp.zeros(o_ref.shape, f32)
        for head in range(2):
            m8 = m_s[head]
            m = jnp.max(m8, axis=0, keepdims=True)
            scale = jnp.exp(m8 - m)
            z = jnp.sum(z_s[head] * scale, axis=0, keepdims=True)
            s = jnp.sum(s_s[head] * scale, axis=0, keepdims=True)
            for layer in range(LAYERS):
                o_ref[layer, head : head + 1, :] = m
                o_ref[layer, 2 + head : 3 + head, :] = z
                o_ref[layer, 4 + head : 5 + head, :] = s


def grads_kernel(
    t_ref, a_ref, k_ref, v_ref, gk_ref, gv_ref, gq_ref, q_s, d_s, qt_s, dt_s, l_s, r_s, acc_s
):
    step = pl.program_id(0)

    @pl.when(step == 0)
    def _():
        spread_tokens(t_ref, q_s, d_s, qt_s, dt_s)
        acc_s[...] = jnp.zeros(acc_s.shape, f32)
        for head in range(2):
            ms = [a_ref[i, head : head + 1, :] for i in range(LAYERS)]
            m = functools.reduce(jnp.maximum, ms)
            z = jnp.zeros_like(m)
            s = jnp.zeros_like(m)
            for i in range(LAYERS):
                scale = jnp.exp(ms[i] - m)
                z = z + scale * a_ref[i, 2 + head : 3 + head, :]
                s = s + scale * a_ref[i, 4 + head : 5 + head, :]
            l_s[head] = jnp.broadcast_to(m + jnp.log(z), (8, TOKENS))
            r_s[head] = jnp.broadcast_to(s / z, (8, TOKENS))

    for b in range(k_ref.shape[0]):
        bias = bias_of(k_ref, b)
        keys = k_ref[b, :ROWS, :]
        values = v_ref[b]
        keys_t = keys.astype(f32).T.astype(bf16)
        gk = jnp.zeros((ROWS, LANES), f32)
        gv = jnp.zeros((ROWS, LANES), f32)
        for head in range(2):
            logits = dot(keys, qt_s[head]) + bias
            probs = dot(values, dt_s[head])
            split = (ROWS // 8, 8, TOKENS)
            weights = jnp.exp(logits.reshape(split) - l_s[head][None])
            grad = weights * (probs.reshape(split) - r_s[head][None])
            weights = weights.reshape(ROWS, TOKENS).astype(bf16)
            grad = grad.reshape(ROWS, TOKENS).astype(bf16)
            gv = gv + dot(weights, d_s[head])
            gk = gk + dot(grad, q_s[head])
            acc_s[head] += dot(keys_t[head * HD : (head + 1) * HD, :], grad)
        gk_ref[b] = gk.astype(bf16)
        gv_ref[b] = gv.astype(bf16)

    @pl.when(step == pl.num_programs(0) - 1)
    def _():
        for block in range(TOKENS // ROWS):
            for head in range(2):
                part = acc_s[head, :, block * ROWS : (block + 1) * ROWS] * FACTOR
                gq_ref[2 * block + head] = part.astype(bf16)


def per_device(queries, keys, values, out_grad, key_mask, query_mask):
    vmem = pl.BlockSpec(memory_space=pltpu.VMEM)
    params = pltpu.CompilerParams(vmem_limit_bytes=48 * 1024 * 1024)
    packed_keys, packed_values = pl.pallas_call(
        pack_kernel,
        in_specs=[vmem] * 3,
        out_specs=[vmem] * 2,
        out_shape=[
            jax.ShapeDtypeStruct((PEERS, ROWS + EXTRA, LANES), bf16),
            jax.ShapeDtypeStruct((PEERS, ROWS, LANES), bf16),
        ],
        compiler_params=params,
    )(keys, values, key_mask.reshape(1, ROWS))

    grad_rows = out_grad * query_mask[:, None].astype(bf16)
    own_tokens = jnp.concatenate([queries, grad_rows], axis=1)
    copies = jnp.broadcast_to(own_tokens[None], (LAYERS,) + own_tokens.shape)
    exchange = functools.partial(lax.all_to_all, split_axis=0, concat_axis=0, tiled=True)
    tokens = exchange(copies, COLUMN)
    all_keys = exchange(packed_keys, PLANE)
    all_values = exchange(packed_values, PLANE)

    group = 4
    whole = lambda *shape: pl.BlockSpec(shape, lambda i: (0,) * len(shape))
    key_spec = pl.BlockSpec((group, ROWS + EXTRA, LANES), lambda i: (i, 0, 0))
    row_spec = pl.BlockSpec((group, ROWS, LANES), lambda i: (i, 0, 0))
    scratch = lambda *shape, dtype=bf16: pltpu.VMEM(shape, dtype)
    stats = pl.pallas_call(
        stats_kernel,
        grid=(PEERS // group,),
        in_specs=[whole(LAYERS, ROWS, LANES), key_spec, row_spec],
        out_specs=whole(LAYERS, 8, TOKENS),
        out_shape=jax.ShapeDtypeStruct((LAYERS, 8, TOKENS), f32),
        scratch_shapes=[
            scratch(2, LANES, TOKENS),
            scratch(2, LANES, TOKENS),
            scratch(2, 8, TOKENS, dtype=f32),
            scratch(2, 8, TOKENS, dtype=f32),
            scratch(2, 8, TOKENS, dtype=f32),
        ],
        compiler_params=params,
    )(tokens, all_keys, all_values)
    all_stats = exchange(stats, COLUMN)
    key_grads, value_grads, query_parts = pl.pallas_call(
        grads_kernel,
        grid=(PEERS // group,),
        in_specs=[whole(LAYERS, ROWS, LANES), whole(LAYERS, 8, TOKENS), key_spec, row_spec],
        out_specs=[row_spec, row_spec, whole(LAYERS, HD, ROWS)],
        out_shape=[
            jax.ShapeDtypeStruct((PEERS, ROWS, LANES), bf16),
            jax.ShapeDtypeStruct((PEERS, ROWS, LANES), bf16),
            jax.ShapeDtypeStruct((LAYERS, HD, ROWS), bf16),
        ],
        scratch_shapes=[
            scratch(2, TOKENS, LANES),
            scratch(2, TOKENS, LANES),
            scratch(2, LANES, TOKENS),
            scratch(2, LANES, TOKENS),
            scratch(2, 8, TOKENS, dtype=f32),
            scratch(2, 8, TOKENS, dtype=f32),
            scratch(2, HD, TOKENS, dtype=f32),
        ],
        compiler_params=params,
    )(tokens, all_stats, all_keys, all_values)
    own_values = exchange(value_grads, PLANE)
    own_keys = exchange(key_grads, PLANE)
    own_queries = exchange(query_parts, COLUMN)
    grad_queries = jnp.sum(own_queries.astype(f32), axis=0).T.astype(bf16)
    grad_keys, grad_values = pl.pallas_call(
        unpack_kernel,
        in_specs=[vmem] * 2,
        out_specs=[vmem] * 2,
        out_shape=[
            jax.ShapeDtypeStruct(keys.shape, bf16),
            jax.ShapeDtypeStruct(values.shape, bf16),
        ],
        compiler_params=params,
    )(own_keys, own_values)
    return grad_queries, grad_keys, grad_values


def solution(mesh):
    fine = Mesh(mesh.devices.reshape(4, 2, 4, 4, 2), AXES)
    ctx = ("h",) + PLANE
    rows = ("s",) + ctx
    head_spec = P("s", ctx)
    row_spec = P(rows, None)
    return jax.shard_map(
        per_device,
        mesh=fine,
        in_specs=(head_spec, row_spec, row_spec, head_spec, P(rows), P("s")),
        out_specs=(head_spec, row_spec, row_spec),
        check_vma=False,
    )
```

time: 701 us -> 162 us (0.23); the launches traced: 689 us -> 161 us
  waiting for transfers between devices: 235 us -> 19.7 us
  matrix products: 146 us -> 0 us
  blocking collectives: 204 us -> 93.2 us
  local copies, waits for them, and re-layouts: 37.5 us -> 3.96 us
  Pallas kernels: 0 us -> 28.3 us
  starting transfers between devices: 37.8 us -> 13 us
  between operations: 13.9 us -> 0.67 us
  other arithmetic: 13.2 us -> 2.73 us
    all_gather x2 -> x0, blocking collectives: 165 us -> none  [the longest x1 131 us: per_device(): group_mask = lax.all_gather(key_mask, 'ctx', axis=0, tiled=True)]
    reduce_scatter x1 -> x0, waiting for transfers between devices: 150 us -> none  [per_device(): lax.psum_scatter(joined.astype(jnp.bfloat16), 'section', scatter_dimensio...]
    dot_general x112 -> x0, matrix products: 146 us -> none  [the longest x32 46.8 us: score_block(): jnp.einsum('qhd,khd->qhk', query_heads, key_block, preferred_element_type...]
    all_to_all x1 -> x5, blocking collectives: 38.8 us -> 93.2 us  [the longest x1 26.5 us: per_device(): all_values = exchange(packed_values, PLANE)]
    all_gather x2 -> x0, waiting for transfers between devices: 44.3 us -> none  [the longest x1 44.2 us: per_device(): lax.all_gather(head_values, 'section', axis=0, tiled=True)]
    unnamed x23 -> x6, local copies, waits for them, and re-layouts: 32.1 us -> 3.1 us
    pallas_call x0 -> x4, Pallas kernels: none -> 28.3 us  [the longest x1 18.8 us: per_device(): pl.pallas_call(grads_kernel, grid=(PEERS // group,), in_specs=[whole(LAYE...]
    all_to_all x3 -> x2, starting transfers between devices: 37.7 us -> 13 us  [the longest x1 9.01 us: per_device(): tokens = exchange(copies, COLUMN)]
  transfers between devices with their start and end apart: 6 -> 2, of which waited for: 4 -> 2; matrix products, arithmetic and copies ran while one was open for 6% -> 0% of each run, Pallas kernels for 0% -> 0%
where the time goes in v1:
time: 162 us; the launch traced here: 161 us
  blocking collectives  93.2 us (58%)
  Pallas kernels  28.3 us (17%)
  waiting for transfers between devices  19.7 us (12%)
  starting transfers between devices  13 us (8%)
  local copies, waits for them, and re-layouts  3.96 us (2%)
  other arithmetic  2.73 us (2%)
    all_to_all x1, blocking collectives, per_device(): all_values = exchange(packed_values, PLANE)  26.5 us
    all_to_all x1, blocking collectives, per_device(): own_keys = exchange(key_grads, PLANE)  22.8 us
    all_to_all x1, blocking collectives, per_device(): all_keys = exchange(packed_keys, PLANE)  22.7 us
    pallas_call x1, Pallas kernels, per_device(): pl.pallas_call(grads_kernel, grid=(PEERS // group,), in_specs=[whole(LAYE...  18.8 us
    all_to_all x1, waiting for transfers between devices, per_device(): own_values = exchange(value_grads, PLANE)  16.3 us
    all_to_all x1, blocking collectives, per_device(): all_stats = exchange(stats, COLUMN)  11.1 us
    all_to_all x1, blocking collectives, per_device(): own_queries = exchange(query_parts, COLUMN)  10.1 us
    all_to_all x1, starting transfers between devices, per_device(): tokens = exchange(copies, COLUMN)  9.01 us
  transfers between devices with their start and end apart: 2, of which 2 were waited for; matrix products, arithmetic and copies ran while one was open for 0% of the time, Pallas kernels for 0%

profile of v1, /device:TPU:1, one launch (start us, length us, event | category | flops | bytes accessed | tf_op | source)
XLA Modules:
  0.0 161.5 jit_solution(17404272621666740772)
XLA Ops:
  0.6 0.7 convert_element_type.9
  1.3 0.7 broadcast_multiply_fusion
  2.0 0.7 pad_maximum_fusion
  2.7 0.1 copy.9
  2.8 0.7 broadcast_in_dim.2
  3.6 9.0 %all-to-all-start = ((bf16[8,128,128]{2,1,0:T(8,128)(2,1)}), bf16[8,128,128]{2,1,0:T(8,128)(2,1)S(1)}, u32[]{:S(2)}, u32[]{:S(2)}) async-start(bf16[8,128,128]{2,1,0:T(8,128)(2,1)} %broadcast_in_dim.2), calls=%async_computation | async-start | bytes 524288 | tf_op jit(solution)/shard_map/all_to_all | solution.py:194
  12.6 0.0 copy-start
  12.6 1.2 copy-done
  13.8 0.0 copy-start.1
  13.8 1.2 copy-done.1
  15.1 0.0 copy-start.2
  15.1 0.7 copy-done.2
  15.7 0.6 shard_map.85
  16.3 3.4 %all-to-all-done.t_ref = bf16[8,128,128]{2,1,0:T(8,128)(2,1)S(1)} async-done(((bf16[8,128,128]{2,1,0:T(8,128)(2,1)}), bf16[8,128,128]{2,1,0:T(8,128)(2,1)S(1)}, u32[]{:S(2)}, u32[]{:S(2)}) %all-to-all-start) | async-done | bytes 262176 | tf_op jit(solution)/shard_map/all_to_all | solution.py:194
  19.7 26.5 %all_to_all.35.v_ref = bf16[32,128,128]{2,1,0:T(8,128)(2,1)S(1)} all-to-all(bf16[32,128,128]{2,1,0:T(8,128)(2,1)S(1)} %get-tuple-element.11), channel_id=1, replica_groups=mesh['s'=4,'h'=2,'x'=4,'y'=4,'c'=2] {'x','y','c'}, dimensions={0} | all-to-all | bytes 2097152 | tf_op jit(solution)/shard_map/all_to_all | solution.py:196
  46.2 22.7 %all_to_all.36.k_ref = bf16[32,144,128]{2,1,0:T(8,128)(2,1)S(1)} all-to-all(bf16[32,144,128]{2,1,0:T(8,128)(2,1)S(1)} %get-tuple-element.10), channel_id=1, replica_groups=mesh['s'=4,'h'=2,'x'=4,'y'=4,'c'=2] {'x','y','c'}, dimensions={0} | all-to-all | bytes 2359296 | tf_op jit(solution)/shard_map/all_to_all | solution.py:195
  68.9 6.9 %shard_map.86 = f32[8,8,512]{2,1,0:T(8,128)S(1)} custom-call(bf16[8,128,128]{2,1,0:T(8,128)(2,1)S(1)} %all-to-all-done.t_ref, bf16[32,144,128]{2,1,0:T(8,128)(2,1)S(1)} %all_to_all.36.k_ref, bf16[32,128,128]{2,1,0:T(8,128)(2,1)S(1)} %all_to_all.35.v_ref), custom_call_target="tpu_custom_call" | custom-call | tf_op jit(solution)/shard_map/pallas_call | solution.py:203
  75.8 11.1 %all_to_all.37.a_ref = f32[8,8,512]{2,1,0:T(8,128)S(1)} all-to-all(f32[8,8,512]{2,1,0:T(8,128)S(1)} %shard_map.86), channel_id=1, replica_groups=mesh['s'=4,'h'=2,'x'=4,'y'=4,'c'=2] {'s','h'}, dimensions={0} | all-to-all | bytes 262144 | tf_op jit(solution)/shard_map/all_to_all | solution.py:218
  86.9 18.8 %shard_map.87 = (bf16[32,128,128]{2,1,0:T(8,128)(2,1)S(1)}, bf16[32,128,128]{2,1,0:T(8,128)(2,1)}, bf16[8,64,128]{2,1,0:T(8,128)(2,1)S(1)}) custom-call(bf16[8,128,128]{2,1,0:T(8,128)(2,1)S(1)} %all-to-all-done.t_ref, f32[8,8,512]{2,1,0:T(8,128)S(1)} %all_to_all.37.a_ref, bf16[32,144,128]{2,1,0:T(8,128)(2,1)S(1)} %all_to_all.36.k_ref, ...), custom_call_target="tpu_custom_call" | custom-call | tf_op jit(solution)/shard_map/pallas_call | solution.py:219
  105.7 10.1 %all_to_all.38 = bf16[8,64,128]{2,1,0:T(8,128)(2,1)S(1)} all-to-all(bf16[8,64,128]{2,1,0:T(8,128)(2,1)S(1)} %get-tuple-element.12), channel_id=1, replica_groups=mesh['s'=4,'h'=2,'x'=4,'y'=4,'c'=2] {'s','h'}, dimensions={0} | all-to-all | bytes 262144 | tf_op jit(solution)/shard_map/all_to_all | solution.py:242
  115.8 22.8 %all_to_all.39.k_ref = bf16[32,128,128]{2,1,0:T(8,128)(2,1)S(1)} all-to-all(bf16[32,128,128]{2,1,0:T(8,128)(2,1)S(1)} %get-tuple-element.13), channel_id=1, replica_groups=mesh['s'=4,'h'=2,'x'=4,'y'=4,'c'=2] {'x','y','c'}, dimensions={0} | all-to-all | bytes 2097152 | tf_op jit(solution)/shard_map/all_to_all | solution.py:241
  138.7 4.0 %all-to-all-start.6 = ((bf16[32,128,128]{2,1,0:T(8,128)(2,1)}), bf16[32,128,128]{2,1,0:T(8,128)(2,1)S(1)}, u32[]{:S(2)}, u32[]{:S(2)}) async-start(bf16[32,128,128]{2,1,0:T(8,128)(2,1)} %get-tuple-element.14), calls=%async_computation.6 | async-start | bytes 2097152 | tf_op jit(solution)/shard_map/all_to_all | solution.py:240
  142.6 0.6 reduce_sum.12
  143.3 16.3 %all-to-all-done.6.v_ref = bf16[32,128,128]{2,1,0:T(8,128)(2,1)S(1)} async-done(((bf16[32,128,128]{2,1,0:T(8,128)(2,1)}), bf16[32,128,128]{2,1,0:T(8,128)(2,1)S(1)}, u32[]{:S(2)}, u32[]{:S(2)}) %all-to-all-start.6) | async-done | bytes 1048608 | tf_op jit(solution)/shard_map/all_to_all | solution.py:240
  159.5 1.9 %shard_map.88 = (bf16[128,4096]{1,0:T(8,128)(2,1)}, bf16[128,4096]{1,0:T(8,128)(2,1)}) custom-call(bf16[32,128,128]{2,1,0:T(8,128)(2,1)S(1)} %all_to_all.39.k_ref, bf16[32,128,128]{2,1,0:T(8,128)(2,1)S(1)} %all-to-all-done.6.v_ref), custom_call_target="tpu_custom_call" | custom-call | tf_op jit(solution)/shard_map/pallas_call | solution.py:244
Async XLA Ops:
  3.6 16.1 %all-to-all-start = ((bf16[8,128,128]{2,1,0:T(8,128)(2,1)}), bf16[8,128,128]{2,1,0:T(8,128)(2,1)S(1)}, u32[]{:S(2)}, u32[]{:S(2)}) async-start(bf16[8,128,128]{2,1,0:T(8,128)(2,1)} %broadcast_in_dim.2), calls=%async_computation | async-start | bytes 524288 | tf_op jit(solution)/shard_map/all_to_all | solution.py:194
  12.6 1.2 copy-start
  13.8 1.2 copy-start.1
  15.1 0.7 copy-start.2
  138.7 20.9 %all-to-all-start.6 = ((bf16[32,128,128]{2,1,0:T(8,128)(2,1)}), bf16[32,128,128]{2,1,0:T(8,128)(2,1)S(1)}, u32[]{:S(2)}, u32[]{:S(2)}) async-start(bf16[32,128,128]{2,1,0:T(8,128)(2,1)} %get-tuple-element.14), calls=%async_computation.6 | async-start | bytes 2097152 | tf_op jit(solution)/shard_map/all_to_all | solution.py:240

commit v2 on v1

--- a/solution.py
+++ b/solution.py
@@ -18,7 +18,7 @@
 MASKED_BIAS = -1000000000.0
 AXES = ("s", "h", "x", "y", "c")
 PLANE = ("x", "y", "c")
-COLUMN = ("s", "h")
+COLUMN = ("h", "s")
 PEERS = 32
 LAYERS = 8
 f32 = jnp.float32
@@ -31,25 +31,34 @@
     return lax.dot_general(a, b, dims, preferred_element_type=f32)
 
 
-def pack_kernel(k_ref, v_ref, m_ref, kp_ref, vp_ref):
+def column_of(row):
+    return jnp.broadcast_to(row, (LANES, LANES)).T
+
+
+def pack_kernel(k_ref, v_ref, m_ref, q_ref, d_ref, qm_ref, kv_ref, t_ref):
     half = k_ref.shape[1] // 2
-    for src, dst in ((k_ref, kp_ref), (v_ref, vp_ref)):
+    for src, base in ((k_ref, 0), (v_ref, ROWS)):
+        at = pl.ds(base, ROWS)
         for j in range(0, PEERS, 2):
             low = src[:, j * HD : j * HD + LANES]
             high = src[:, half + j * HD : half + j * HD + LANES]
-            dst[j, :ROWS, :] = jnp.concatenate([low[:, :HD], high[:, :HD]], axis=1)
-            dst[j + 1, :ROWS, :] = jnp.concatenate([low[:, HD:], high[:, HD:]], axis=1)
+            kv_ref[j, at, :] = jnp.concatenate([low[:, :HD], high[:, :HD]], axis=1)
+            kv_ref[j + 1, at, :] = jnp.concatenate([low[:, HD:], high[:, HD:]], axis=1)
     mask = jnp.broadcast_to(m_ref[...].astype(f32), (EXTRA, LANES)).astype(bf16)
     for j in range(PEERS):
-        kp_ref[j, ROWS:, :] = mask
-
-
-def unpack_kernel(k_ref, v_ref, ko_ref, vo_ref):
+        kv_ref[j, 2 * ROWS :, :] = mask
+    rows = column_of(qm_ref[...].astype(f32))
+    grad_rows = d_ref[...].astype(f32) * rows[:, :HD]
+    t_ref[...] = jnp.concatenate([q_ref[...].astype(f32), grad_rows], axis=1).astype(bf16)
+
+
+def unpack_kernel(g_ref, ko_ref, vo_ref):
     half = ko_ref.shape[1] // 2
-    for src, dst in ((k_ref, ko_ref), (v_ref, vo_ref)):
+    for dst, base in ((ko_ref, 0), (vo_ref, ROWS)):
+        at = pl.ds(base, ROWS)
         for j in range(0, PEERS, 2):
-            a = src[j]
-            b = src[j + 1]
+            a = g_ref[j, at, :]
+            b = g_ref[j + 1, at, :]
             dst[:, j * HD : j * HD + LANES] = jnp.concatenate([a[:, :HD], b[:, :HD]], axis=1)
             dst[:, half + j * HD : half + j * HD + LANES] = jnp.concatenate(
                 [a[:, HD:], b[:, HD:]], axis=1
@@ -60,7 +69,7 @@
     lane = lax.broadcasted_iota(jnp.int32, (ROWS, LANES), 1)
     for block in range(TOKENS // ROWS):
         for head in range(2):
-            both = t_ref[2 * block + head].astype(f32)
+            both = t_ref[4 * head + block].astype(f32)
             turned = pltpu.roll(both, HD, 1)
             mine = (lane < HD) if head == 0 else (lane >= HD)
             q, d = (both, turned) if head == 0 else (turned, both)
@@ -75,13 +84,13 @@
 
 
 def bias_of(k_ref, b):
-    row = k_ref[b, ROWS : ROWS + EXTRA, :].astype(f32)
-    square = jnp.broadcast_to(row[:1, :], (LANES, LANES)).T
+    row = k_ref[b, 2 * ROWS :, :].astype(f32)
+    square = column_of(row[:1, :])
     bias = jnp.where(square == 1.0, 0.0, MASKED_BIAS)
     return jnp.concatenate([bias] * (TOKENS // LANES), axis=1)
 
 
-def stats_kernel(t_ref, k_ref, v_ref, o_ref, qt_s, dt_s, m_s, z_s, s_s):
+def stats_kernel(t_ref, k_ref, o_ref, qt_s, dt_s, m_s, z_s, s_s):
     step = pl.program_id(0)
 
     @pl.when(step == 0)
@@ -94,7 +103,7 @@
     for b in range(k_ref.shape[0]):
         bias = bias_of(k_ref, b)
         keys = k_ref[b, :ROWS, :]
-        values = v_ref[b]
+        values = k_ref[b, ROWS : 2 * ROWS, :]
         for head in range(2):
             logits = dot(keys, qt_s[head]) + bias
             probs = dot(values, dt_s[head])
@@ -124,7 +133,7 @@
 
 
 def grads_kernel(
-    t_ref, a_ref, k_ref, v_ref, gk_ref, gv_ref, gq_ref, q_s, d_s, qt_s, dt_s, l_s, r_s, acc_s
+    t_ref, a_ref, k_ref, g_ref, gq_ref, q_s, d_s, qt_s, dt_s, l_s, r_s, acc_s
 ):
     step = pl.program_id(0)
 
@@ -147,7 +156,7 @@
     for b in range(k_ref.shape[0]):
         bias = bias_of(k_ref, b)
         keys = k_ref[b, :ROWS, :]
-        values = v_ref[b]
+        values = k_ref[b, ROWS : 2 * ROWS, :]
         keys_t = keys.astype(f32).T.astype(bf16)
         gk = jnp.zeros((ROWS, LANES), f32)
         gv = jnp.zeros((ROWS, LANES), f32)
@@ -162,48 +171,44 @@
             gv = gv + dot(weights, d_s[head])
             gk = gk + dot(grad, q_s[head])
             acc_s[head] += dot(keys_t[head * HD : (head + 1) * HD, :], grad)
-        gk_ref[b] = gk.astype(bf16)
-        gv_ref[b] = gv.astype(bf16)
+        g_ref[b, :ROWS, :] = gk.astype(bf16)
+        g_ref[b, ROWS:, :] = gv.astype(bf16)
 
     @pl.when(step == pl.num_programs(0) - 1)
     def _():
         for block in range(TOKENS // ROWS):
             for head in range(2):
                 part = acc_s[head, :, block * ROWS : (block + 1) * ROWS] * FACTOR
-                gq_ref[2 * block + head] = part.astype(bf16)
+                gq_ref[4 * head + block] = part
 
 
 def per_device(queries, keys, values, out_grad, key_mask, query_mask):
     vmem = pl.BlockSpec(memory_space=pltpu.VMEM)
     params = pltpu.CompilerParams(vmem_limit_bytes=48 * 1024 * 1024)
-    packed_keys, packed_values = pl.pallas_call(
+    sent_rows = 2 * ROWS + EXTRA
+    packed, own_tokens = pl.pallas_call(
         pack_kernel,
-        in_specs=[vmem] * 3,
+        in_specs=[vmem] * 6,
         out_specs=[vmem] * 2,
         out_shape=[
-            jax.ShapeDtypeStruct((PEERS, ROWS + EXTRA, LANES), bf16),
-            jax.ShapeDtypeStruct((PEERS, ROWS, LANES), bf16),
-        ],
-        compiler_params=params,
-    )(keys, values, key_mask.reshape(1, ROWS))
-
-    grad_rows = out_grad * query_mask[:, None].astype(bf16)
-    own_tokens = jnp.concatenate([queries, grad_rows], axis=1)
-    copies = jnp.broadcast_to(own_tokens[None], (LAYERS,) + own_tokens.shape)
+            jax.ShapeDtypeStruct((PEERS, sent_rows, LANES), bf16),
+            jax.ShapeDtypeStruct((ROWS, LANES), bf16),
+        ],
+        compiler_params=params,
+    )(keys, values, key_mask.reshape(1, ROWS), queries, out_grad, query_mask.reshape(1, ROWS))
     exchange = functools.partial(lax.all_to_all, split_axis=0, concat_axis=0, tiled=True)
-    tokens = exchange(copies, COLUMN)
-    all_keys = exchange(packed_keys, PLANE)
-    all_values = exchange(packed_values, PLANE)
+    tokens = lax.all_gather(own_tokens, COLUMN, axis=0, tiled=False)
+    rows = exchange(packed, PLANE)
 
     group = 4
     whole = lambda *shape: pl.BlockSpec(shape, lambda i: (0,) * len(shape))
-    key_spec = pl.BlockSpec((group, ROWS + EXTRA, LANES), lambda i: (i, 0, 0))
-    row_spec = pl.BlockSpec((group, ROWS, LANES), lambda i: (i, 0, 0))
+    in_spec = pl.BlockSpec((group, sent_rows, LANES), lambda i: (i, 0, 0))
+    out_spec = pl.BlockSpec((group, 2 * ROWS, LANES), lambda i: (i, 0, 0))
     scratch = lambda *shape, dtype=bf16: pltpu.VMEM(shape, dtype)
     stats = pl.pallas_call(
         stats_kernel,
         grid=(PEERS // group,),
-        in_specs=[whole(LAYERS, ROWS, LANES), key_spec, row_spec],
+        in_specs=[whole(LAYERS, ROWS, LANES), in_spec],
         out_specs=whole(LAYERS, 8, TOKENS),
         out_shape=jax.ShapeDtypeStruct((LAYERS, 8, TOKENS), f32),
         scratch_shapes=[
@@ -214,17 +219,16 @@
             scratch(2, 8, TOKENS, dtype=f32),
         ],
         compiler_params=params,
-    )(tokens, all_keys, all_values)
+    )(tokens, rows)
     all_stats = exchange(stats, COLUMN)
-    key_grads, value_grads, query_parts = pl.pallas_call(
+    grads, query_parts = pl.pallas_call(
         grads_kernel,
         grid=(PEERS // group,),
-        in_specs=[whole(LAYERS, ROWS, LANES), whole(LAYERS, 8, TOKENS), key_spec, row_spec],
-        out_specs=[row_spec, row_spec, whole(LAYERS, HD, ROWS)],
+        in_specs=[whole(LAYERS, ROWS, LANES), whole(LAYERS, 8, TOKENS), in_spec],
+        out_specs=[out_spec, whole(LAYERS, HD, ROWS)],
         out_shape=[
-            jax.ShapeDtypeStruct((PEERS, ROWS, LANES), bf16),
-            jax.ShapeDtypeStruct((PEERS, ROWS, LANES), bf16),
-            jax.ShapeDtypeStruct((LAYERS, HD, ROWS), bf16),
+            jax.ShapeDtypeStruct((PEERS, 2 * ROWS, LANES), bf16),
+            jax.ShapeDtypeStruct((LAYERS, HD, ROWS), f32),
         ],
         scratch_shapes=[
             scratch(2, TOKENS, LANES),
@@ -236,21 +240,22 @@
             scratch(2, HD, TOKENS, dtype=f32),
         ],
         compiler_params=params,
-    )(tokens, all_stats, all_keys, all_values)
-    own_values = exchange(value_grads, PLANE)
-    own_keys = exchange(key_grads, PLANE)
-    own_queries = exchange(query_parts, COLUMN)
-    grad_queries = jnp.sum(own_queries.astype(f32), axis=0).T.astype(bf16)
+    )(tokens, all_stats, rows)
+    own_queries = lax.psum_scatter(
+        query_parts.reshape(LAYERS * HD, ROWS), COLUMN, scatter_dimension=0, tiled=True
+    )
+    own_rows = exchange(grads, PLANE)
+    grad_queries = own_queries.T.astype(bf16)
     grad_keys, grad_values = pl.pallas_call(
         unpack_kernel,
-        in_specs=[vmem] * 2,
+        in_specs=[vmem],
         out_specs=[vmem] * 2,
         out_shape=[
             jax.ShapeDtypeStruct(keys.shape, bf16),
             jax.ShapeDtypeStruct(values.shape, bf16),
         ],
         compiler_params=params,
-    )(own_keys, own_values)
+    )(own_rows)
     return grad_queries, grad_keys, grad_values
 
 

time: 162 us -> 149 us (0.920)
  the two profiles are of different devices: /device:TPU:1 before, /device:TPU:2 now
where the time goes in v2:
time: 149 us; the launch traced here: 148 us
  blocking collectives  45.1 us (30%)
  waiting for transfers between devices  36.8 us (25%)
  Pallas kernels  28.3 us (19%)
  starting transfers between devices  14.2 us (10%)
  between operations  14.1 us (9%)
  local copies, waits for them, and re-layouts  8.11 us (5%)
    reduce_scatter x1, waiting for transfers between devices, per_device(): lax.psum_scatter(query_parts.reshape(LAYERS * HD, ROWS), COLUMN, scatter_...  36.1 us
    all_gather x1, blocking collectives, per_device(): tokens = lax.all_gather(own_tokens, COLUMN, axis=0, tiled=False)  28.5 us
    pallas_call x1, Pallas kernels, per_device(): pl.pallas_call(grads_kernel, grid=(PEERS // group,), in_specs=[whole(LAYE...  18.8 us
    all_to_all x1, blocking collectives, per_device(): all_stats = exchange(stats, COLUMN)  16.6 us
    unnamed x14, local copies, waits for them, and re-layouts  8.11 us
    all_to_all x1, starting transfers between devices, per_device(): rows = exchange(packed, PLANE)  7.62 us
    pallas_call x1, Pallas kernels, per_device(): pl.pallas_call(stats_kernel, grid=(PEERS // group,), in_specs=[whole(LAYE...  6.9 us
    all_to_all x1, starting transfers between devices, per_device(): own_rows = exchange(grads, PLANE)  6.57 us
  transfers between devices with their start and end apart: 3, of which 1 were waited for; matrix products, arithmetic and copies ran while one was open for 1% of the time, Pallas kernels for 0%

profile of v2, /device:TPU:2, one launch (start us, length us, event | category | flops | bytes accessed | tf_op | source)
XLA Modules:
  0.0 148.0 jit_solution(10312639209530193639)
XLA Ops:
  7.2 0.8 copy.9.q_ref
  8.0 0.8 copy.10.d_ref
  8.8 0.0 copy-start.2
  8.8 1.2 copy-done.2
  10.1 0.0 copy-start.3
  10.1 1.2 copy-done.3
  11.3 0.0 copy-start.4
  11.3 0.7 copy-done.4
  11.9 0.0 copy-start.5
  11.9 0.7 copy-done.5
  12.6 0.6 shard_map.85
  13.2 0.0 copy-start
  13.3 1.4 copy-done
  14.6 7.6 %all-to-all-start = ((bf16[32,272,128]{2,1,0:T(8,128)(2,1)}), bf16[32,272,128]{2,1,0:T(8,128)(2,1)S(1)}, u32[]{:S(2)}, u32[]{:S(2)}) async-start(bf16[32,272,128]{2,1,0:T(8,128)(2,1)} %copy-done), calls=%async_computation | async-start | bytes 4456448 | tf_op jit(solution)/shard_map/all_to_all | solution.py:201
  22.3 28.5 %all-gather = bf16[1024,128]{1,0:T(8,128)(2,1)S(1)} all-gather(bf16[128,128]{1,0:T(8,128)(2,1)S(1)} %get-tuple-element.9), channel_id=2, replica_groups=mesh['s'=4,'h'=2,'x'=4,'y'=4,'c'=2] {'h','s'}, dimensions={0}, use_global_device_ids=true | all-gather | bytes 294912 | tf_op jit(solution)/shard_map/all_gather | solution.py:200
  50.7 0.0 all-to-all-done.k_ref
  50.7 6.9 %shard_map.86 = f32[8,8,512]{2,1,0:T(8,128)S(1)} custom-call(bf16[8,128,128]{2,1,0:T(8,128)(2,1)S(1)} %bitcast.6, bf16[32,272,128]{2,1,0:T(8,128)(2,1)S(1)} %all-to-all-done.k_ref), custom_call_target="tpu_custom_call" | custom-call | tf_op jit(solution)/shard_map/pallas_call | solution.py:208
  57.6 16.6 %all_to_all.15.a_ref = f32[8,8,512]{2,1,0:T(8,128)S(1)} all-to-all(f32[8,8,512]{2,1,0:T(8,128)S(1)} %shard_map.86), channel_id=1, replica_groups=mesh['s'=4,'h'=2,'x'=4,'y'=4,'c'=2] {'h','s'}, dimensions={0} | all-to-all | bytes 262144 | tf_op jit(solution)/shard_map/all_to_all | solution.py:223
  74.3 18.8 %shard_map.87 = (bf16[32,256,128]{2,1,0:T(8,128)(2,1)S(1)}, f32[8,64,128]{2,1,0:T(8,128)}) custom-call(bf16[8,128,128]{2,1,0:T(8,128)(2,1)S(1)} %bitcast.7, f32[8,8,512]{2,1,0:T(8,128)S(1)} %all_to_all.15.a_ref, bf16[32,272,128]{2,1,0:T(8,128)(2,1)S(1)} %all-to-all-done.k_ref), custom_call_target="tpu_custom_call" | custom-call | tf_op jit(solution)/shard_map/pallas_call | solution.py:224
  93.1 0.0 copy-start.1
  93.1 1.3 copy-done.1
  94.4 6.6 %all-to-all-start.2 = ((bf16[32,256,128]{2,1,0:T(8,128)(2,1)}), bf16[32,256,128]{2,1,0:T(8,128)(2,1)S(1)}, u32[]{:S(2)}, u32[]{:S(2)}) async-start(bf16[32,256,128]{2,1,0:T(8,128)(2,1)} %copy-done.1), calls=%async_computation.3 | async-start | bytes 4194304 | tf_op jit(solution)/shard_map/all_to_all | solution.py:247
  101.0 0.0 reduce-scatter.2.cloned.1.call-start
  101.1 0.7 reduce-scatter.2.cloned.1.call-update
  101.7 36.1 %reduce-scatter.2.cloned.1.call-done = f32[64,128]{1,0:T(8,128)} async-done(((f32[512,128]{1,0:T(8,128)}), f32[64,128]{1,0:T(8,128)}) %reduce-scatter.2.cloned.1.call-update) | async-done | bytes 32784 | tf_op jit(solution)/shard_map/reduce_scatter | solution.py:244
  137.9 1.4 convert_bitcast_fusion
  139.2 0.0 all-to-all-done.2.g_ref
  139.2 1.9 %shard_map.88 = (bf16[128,4096]{1,0:T(8,128)(2,1)}, bf16[128,4096]{1,0:T(8,128)(2,1)}) custom-call(bf16[32,256,128]{2,1,0:T(8,128)(2,1)S(1)} %all-to-all-done.2.g_ref), custom_call_target="tpu_custom_call" | custom-call | tf_op jit(solution)/shard_map/pallas_call | solution.py:249
Async XLA Ops:
  8.8 1.2 copy-start.2
  10.1 1.2 copy-start.3
  11.3 0.7 copy-start.4
  11.9 0.7 copy-start.5
  13.2 1.4 copy-start
  14.6 36.1 %all-to-all-start = ((bf16[32,272,128]{2,1,0:T(8,128)(2,1)}), bf16[32,272,128]{2,1,0:T(8,128)(2,1)S(1)}, u32[]{:S(2)}, u32[]{:S(2)}) async-start(bf16[32,272,128]{2,1,0:T(8,128)(2,1)} %copy-done), calls=%async_computation | async-start | bytes 4456448 | tf_op jit(solution)/shard_map/all_to_all | solution.py:201
  93.1 1.3 copy-start.1
  94.4 44.8 %all-to-all-start.2 = ((bf16[32,256,128]{2,1,0:T(8,128)(2,1)}), bf16[32,256,128]{2,1,0:T(8,128)(2,1)S(1)}, u32[]{:S(2)}, u32[]{:S(2)}) async-start(bf16[32,256,128]{2,1,0:T(8,128)(2,1)} %copy-done.1), calls=%async_computation.3 | async-start | bytes 4194304 | tf_op jit(solution)/shard_map/all_to_all | solution.py:247
  101.0 36.9 %reduce-scatter.2.cloned.1.call-start = ((), (), s32[]{:S(2)}) async-start(), calls=%async_computation.4 | async-start | bytes 294912 | tf_op jit(solution)/shard_map/reduce_scatter | solution.py:244
Sparse Core Ops, SparseCore 0:
  104.9 32.9 reduce-scatter.1

commit v3 on v2

v3 whole, which is shorter than its diff:
```python
import functools
import math

import jax
import jax.numpy as jnp
from jax import lax
from jax.experimental import pallas as pl
from jax.experimental.pallas import tpu as pltpu
from jax.sharding import Mesh
from jax.sharding import PartitionSpec as P

HD = 64
LANES = 128
TOKENS = 512
ROWS = 128
EXTRA = 16
STATS_JOINED = 4
GRADS_JOINED = 8
MIB = 1024 * 1024
FACTOR = 1.0 / math.sqrt(HD)
MASKED_BIAS = -1000000000.0
AXES = ("s", "h", "x", "y", "c")
PLANE = ("x", "y", "c")
COLUMN = ("h", "s")
PEERS = 32
LAYERS = 8
f32 = jnp.float32
bf16 = jnp.bfloat16
NT = (((1,), (1,)), ((), ()))
NN = (((1,), (0,)), ((), ()))


def dot(a, b, dims=NN):
    return lax.dot_general(a, b, dims, preferred_element_type=f32)


def column_of(row):
    return jnp.broadcast_to(row, (LANES, LANES)).T


def pack_kernel(k_ref, v_ref, m_ref, q_ref, d_ref, qm_ref, kv_ref, t_ref, *scratch):
    k_s, v_s, m_s, q_s, d_s, qm_s, kv_s, t_s, in_sems, small_sems, out_sems = scratch
    steps = in_sems.shape[0]
    half = k_ref.shape[1] // 2
    width = half // steps
    copy = pltpu.make_async_copy
    small = ((m_ref, m_s), (q_ref, q_s), (d_ref, d_s), (qm_ref, qm_s))
    small = [copy(src, dst, small_sems.at[i]) for i, (src, dst) in enumerate(small)]
    loads = []
    for step in range(steps):
        for i, (src, dst) in enumerate(((k_ref, k_s), (v_ref, v_s))):
            for side in range(2):
                at = pl.ds(side * half + step * width, width)
                sem = in_sems.at[step, 2 * i + side]
                loads.append(copy(src.at[:, at], dst.at[:, at], sem))
    for load in small + loads:
        load.start()
    for load in small:
        load.wait()
    t_s[:HD, :] = (q_s[...].astype(f32) * FACTOR).astype(bf16)
    t_s[HD:, :] = (d_s[...].astype(f32) * qm_s[...].astype(f32)).astype(bf16)
    stores = [copy(t_s, t_ref, out_sems.at[steps])]
    stores[0].start()
    mask = jnp.broadcast_to(m_s[...].astype(f32), (EXTRA, LANES)).astype(bf16)
    for step in range(steps):
        for load in loads[4 * step : 4 * step + 4]:
            load.wait()
        first = step * width // HD
        for j in range(first, first + width // HD, 2):
            for src, base in ((k_s, 0), (v_s, ROWS)):
                at = pl.ds(base, ROWS)
                low = src[:, j * HD : j * HD + LANES]
                high = src[:, half + j * HD : half + j * HD + LANES]
                kv_s[j, at, :] = jnp.concatenate([low[:, :HD], high[:, :HD]], axis=1)
                kv_s[j + 1, at, :] = jnp.concatenate([low[:, HD:], high[:, HD:]], axis=1)
            kv_s[j, 2 * ROWS :, :] = mask
            kv_s[j + 1, 2 * ROWS :, :] = mask
        at = pl.ds(first, width // HD)
        store = copy(kv_s.at[at], kv_ref.at[at], out_sems.at[step])
        store.start()
        stores.append(store)
    for store in stores:
        store.wait()


def unpack_kernel(g_ref, ko_ref, vo_ref, k_s, v_s, sems):
    steps = sems.shape[0]
    half = ko_ref.shape[1] // 2
    width = half // steps
    stores = []
    for step in range(steps):
        first = step * width // HD
        for i, (dst, out, base) in enumerate(((k_s, ko_ref, 0), (v_s, vo_ref, ROWS))):
            at = pl.ds(base, ROWS)
            for j in range(first, first + width // HD, 2):
                a = g_ref[j, at, :]
                b = g_ref[j + 1, at, :]
                low = jnp.concatenate([a[:, :HD], b[:, :HD]], axis=1)
                high = jnp.concatenate([a[:, HD:], b[:, HD:]], axis=1)
                dst[:, j * HD : j * HD + LANES] = low
                dst[:, half + j * HD : half + j * HD + LANES] = high
            for side in range(2):
                at = pl.ds(side * half + step * width, width)
                sem = sems.at[step, 2 * i + side]
                store = pltpu.make_async_copy(dst.at[:, at], out.at[:, at], sem)
                store.start()
                stores.append(store)
    for store in stores:
        store.wait()


def layer_index():
    return lax.axis_index("h") * 4 + lax.axis_index("s")


def spread_tokens(t_refs, t_s, q_s, d_s, qt_s, dt_s):
    layer = layer_index()
    for r in range(LAYERS):
        t_s[lax.rem(layer + LAYERS - r, LAYERS)] = t_refs[r][...]
    qt_s[...] = jnp.zeros(qt_s.shape, bf16)
    dt_s[...] = jnp.zeros(dt_s.shape, bf16)
    for block in range(TOKENS // ROWS):
        at = pl.ds(block * ROWS, ROWS)
        for head in range(2):
            mine = pl.ds(head * HD, HD)
            qt_s[head, mine, at] = t_s[4 * head + block, :HD, :]
            dt_s[head, mine, at] = t_s[4 * head + block, HD:, :]
            if q_s is not None:
                q_s[head, at, :] = qt_s[head, :, at].astype(f32).T.astype(bf16)
                d_s[head, at, :] = dt_s[head, :, at].astype(f32).T.astype(bf16)


def bias_of(k_ref, first, count):
    parts = []
    for b in range(first, first + count):
        row = k_ref[b, 2 * ROWS :, :].astype(f32)
        square = column_of(row[:1, :])
        bias = jnp.where(square == 1.0, 0.0, MASKED_BIAS)
        parts.append(jnp.concatenate([bias] * (TOKENS // LANES), axis=1))
    return jnp.concatenate(parts, axis=0)


def block_of(k_ref, first, count, base):
    return k_ref[first : first + count, base : base + ROWS, :].reshape(count * ROWS, LANES)


def stats_kernel(*refs):
    t_refs, (k_ref, o_ref, t_s, qt_s, dt_s, m_s, z_s, s_s) = refs[:LAYERS], refs[LAYERS:]
    step = pl.program_id(0)

    @pl.when(step == 0)
    def _():
        spread_tokens(t_refs, t_s, None, None, qt_s, dt_s)
        m_s[...] = jnp.full(m_s.shape, -3e38, f32)
        z_s[...] = jnp.zeros(z_s.shape, f32)
        s_s[...] = jnp.zeros(s_s.shape, f32)

    count = STATS_JOINED
    split = (count * ROWS // 8, 8, TOKENS)
    for b in range(0, k_ref.shape[0], count):
        bias = bias_of(k_ref, b, count)
        keys = block_of(k_ref, b, count, 0)
        values = block_of(k_ref, b, count, ROWS)
        for head in range(2):
            logits = dot(keys, qt_s[head]) + bias
            probs = dot(values, dt_s[head])
            logits = logits.reshape(split)
            old = m_s[head]
            new = jnp.maximum(old, jnp.max(logits, axis=0))
            scale = jnp.exp(old - new)
            weights = jnp.exp(logits - new[None])
            m_s[head] = new
            z_s[head] = z_s[head] * scale + jnp.sum(weights, axis=0)
            s_s[head] = s_s[head] * scale + jnp.sum(weights * probs.reshape(split), axis=0)

    @pl.when(step == pl.num_programs(0) - 1)
    def _():
        o_ref[...] = jnp.zeros(o_ref.shape, f32)
        for head in range(2):
            m8 = m_s[head]
            m = jnp.max(m8, axis=0, keepdims=True)
            scale = jnp.exp(m8 - m)
            z = jnp.sum(z_s[head] * scale, axis=0, keepdims=True)
            s = jnp.sum(s_s[head] * scale, axis=0, keepdims=True)
            for layer in range(LAYERS):
                o_ref[layer, head : head + 1, :] = m
                o_ref[layer, 2 + head : 3 + head, :] = z
                o_ref[layer, 4 + head : 5 + head, :] = s


def grads_kernel(*refs):
    t_refs, (a_ref, k_ref, g_ref), refs = refs[:LAYERS], refs[LAYERS : LAYERS + 3], refs[LAYERS + 3 :]
    gq_refs, (t_s, q_s, d_s, qt_s, dt_s, l_s, r_s, acc_s, part_s) = refs[:LAYERS], refs[LAYERS:]
    step = pl.program_id(0)

    @pl.when(step == 0)
    def _():
        spread_tokens(t_refs, t_s, q_s, d_s, qt_s, dt_s)
        acc_s[...] = jnp.zeros(acc_s.shape, f32)
        for head in range(2):
            ms = [a_ref[i, head : head + 1, :] for i in range(LAYERS)]
            m = functools.reduce(jnp.maximum, ms)
            z = jnp.zeros_like(m)
            s = jnp.zeros_like(m)
            for i in range(LAYERS):
                scale = jnp.exp(ms[i] - m)
                z = z + scale * a_ref[i, 2 + head : 3 + head, :]
                s = s + scale * a_ref[i, 4 + head : 5 + head, :]
            l_s[head] = jnp.broadcast_to(m + jnp.log(z), (8, TOKENS))
            r_s[head] = jnp.broadcast_to(s / z, (8, TOKENS))

    count = GRADS_JOINED
    split = (count * ROWS // 8, 8, TOKENS)
    for b in range(0, k_ref.shape[0], count):
        bias = bias_of(k_ref, b, count)
        keys = block_of(k_ref, b, count, 0)
        values = block_of(k_ref, b, count, ROWS)
        keys_t = keys.astype(f32).T.astype(bf16)
        gk = jnp.zeros(keys.shape, f32)
        gv = jnp.zeros(keys.shape, f32)
        for head in range(2):
            logits = dot(keys, qt_s[head]) + bias
            probs = dot(values, dt_s[head])
            weights = jnp.exp(logits.reshape(split) - l_s[head][None])
            grad = weights * (probs.reshape(split) - r_s[head][None])
            weights = weights.reshape(count * ROWS, TOKENS).astype(bf16)
            grad = grad.reshape(count * ROWS, TOKENS).astype(bf16)
            gv = gv + dot(weights, d_s[head])
            gk = gk + dot(grad, q_s[head])
            acc_s[head] += dot(keys_t[head * HD : (head + 1) * HD, :], grad)
        shape = (count, ROWS, LANES)
        g_ref[b : b + count, :ROWS, :] = gk.astype(bf16).reshape(shape)
        g_ref[b : b + count, ROWS:, :] = gv.astype(bf16).reshape(shape)

    @pl.when(step == pl.num_programs(0) - 1)
    def _():
        for block in range(TOKENS // ROWS):
            for head in range(2):
                part = acc_s[head, :, block * ROWS : (block + 1) * ROWS] * FACTOR
                part_s[4 * head + block] = part.astype(bf16)
        for r in range(LAYERS):
            gq_refs[r][...] = part_s[lax.rem(layer_index() + r, LAYERS)]


def permuted(array, distance):
    place = lambda z: (z % 4) * 2 + z // 4
    pairs = [(place(z), place((z + distance) % LAYERS)) for z in range(LAYERS)]
    return lax.ppermute(array, ("s", "h"), pairs)


def permuted_parts(arrays):
    return [arrays[0]] + [permuted(arrays[r], r) for r in range(1, LAYERS)]


def per_device(queries, keys, values, out_grad, key_mask, query_mask):
    vmem = pl.BlockSpec(memory_space=pltpu.VMEM)
    hbm = pl.BlockSpec(memory_space=pl.ANY)
    limit = lambda mib: pltpu.CompilerParams(vmem_limit_bytes=mib * MIB)
    whole = lambda *shape: pl.BlockSpec(shape, lambda i: (0,) * len(shape))
    scratch = lambda *shape, dtype=bf16: pltpu.VMEM(shape, dtype)
    dma = pltpu.SemaphoreType.DMA
    i32 = jnp.int32
    sent_rows = 2 * ROWS + EXTRA
    steps = 8
    packed, own_tokens = pl.pallas_call(
        pack_kernel,
        in_specs=[hbm] * 6,
        out_specs=[hbm] * 2,
        out_shape=[
            pltpu.HBM((PEERS, sent_rows, LANES), bf16),
            pltpu.HBM((2 * HD, ROWS), bf16),
        ],
        scratch_shapes=[
            scratch(*keys.shape),
            scratch(*values.shape),
            scratch(1, ROWS, dtype=i32),
            scratch(HD, ROWS),
            scratch(HD, ROWS),
            scratch(1, ROWS, dtype=i32),
            scratch(PEERS, sent_rows, LANES),
            scratch(2 * HD, ROWS),
            dma((steps, 4)),
            dma((4,)),
            dma((steps + 1,)),
        ],
        compiler_params=limit(60),
    )(
        keys,
        values,
        key_mask.reshape(1, ROWS),
        queries.T,
        out_grad.T,
        query_mask.reshape(1, ROWS),
    )
    exchange = functools.partial(lax.all_to_all, split_axis=0, concat_axis=0, tiled=True)
    rows = exchange(packed, PLANE)
    tokens = permuted_parts([own_tokens] * LAYERS)

    group = 8
    in_spec = pl.BlockSpec((group, sent_rows, LANES), lambda i: (i, 0, 0))
    out_spec = pl.BlockSpec((group, 2 * ROWS, LANES), lambda i: (i, 0, 0))
    token_specs = [whole(2 * HD, ROWS)] * LAYERS
    stats = pl.pallas_call(
        stats_kernel,
        grid=(PEERS // group,),
        in_specs=token_specs + [in_spec],
        out_specs=whole(LAYERS, 8, TOKENS),
        out_shape=pltpu.HBM((LAYERS, 8, TOKENS), f32),
        scratch_shapes=[
            scratch(LAYERS, 2 * HD, ROWS),
            scratch(2, LANES, TOKENS),
            scratch(2, LANES, TOKENS),
            scratch(2, 8, TOKENS, dtype=f32),
            scratch(2, 8, TOKENS, dtype=f32),
            scratch(2, 8, TOKENS, dtype=f32),
        ],
        compiler_params=limit(40),
    )(*tokens, rows)
    all_stats = exchange(stats, COLUMN)
    grads, *query_parts = pl.pallas_call(
        grads_kernel,
        grid=(PEERS // group,),
        in_specs=token_specs + [whole(LAYERS, 8, TOKENS), in_spec],
        out_specs=[out_spec] + [whole(HD, ROWS)] * LAYERS,
        out_shape=[pltpu.HBM((PEERS, 2 * ROWS, LANES), bf16)]
        + [pltpu.HBM((HD, ROWS), bf16)] * LAYERS,
        scratch_shapes=[
            scratch(LAYERS, 2 * HD, ROWS),
            scratch(2, TOKENS, LANES),
            scratch(2, TOKENS, LANES),
            scratch(2, LANES, TOKENS),
            scratch(2, LANES, TOKENS),
            scratch(2, 8, TOKENS, dtype=f32),
            scratch(2, 8, TOKENS, dtype=f32),
            scratch(2, HD, TOKENS, dtype=f32),
            scratch(LAYERS, HD, ROWS),
        ],
        compiler_params=limit(40),
    )(*tokens, all_stats, rows)
    own_rows = exchange(grads, PLANE)
    own_parts = permuted_parts(query_parts)
    total = functools.reduce(jnp.add, [part.astype(f32) for part in own_parts])
    grad_queries = total.astype(bf16).T
    grad_keys, grad_values = pl.pallas_call(
        unpack_kernel,
        in_specs=[vmem],
        out_specs=[hbm] * 2,
        out_shape=[pltpu.HBM(keys.shape, bf16), pltpu.HBM(values.shape, bf16)],
        scratch_shapes=[scratch(*keys.shape), scratch(*values.shape), dma((steps, 4))],
        compiler_params=limit(16),
    )(own_rows)
    return grad_queries, grad_keys, grad_values


def solution(mesh):
    fine = Mesh(mesh.devices.reshape(4, 2, 4, 4, 2), AXES)
    ctx = ("h",) + PLANE
    rows = ("s",) + ctx
    head_spec = P("s", ctx)
    row_spec = P(rows, None)
    return jax.shard_map(
        per_device,
        mesh=fine,
        in_specs=(head_spec, row_spec, row_spec, head_spec, P(rows), P("s")),
        out_specs=(head_spec, row_spec, row_spec),
        check_vma=False,
    )
```

time: 149 us -> 115 us (0.77)
  the two profiles are of different devices: /device:TPU:2 before, /device:TPU:1 now
where the time goes in v3:
time: 115 us; the launch traced here: 114 us
  starting transfers between devices  40.1 us (35%)
  waiting for transfers between devices  32.1 us (28%)
  Pallas kernels  24.6 us (21%)
  blocking collectives  16.1 us (14%)
    ppermute x14, starting transfers between devices, permuted(): return lax.ppermute(array, ('s', 'h'), pairs)  25.3 us
    all_to_all x1, blocking collectives, per_device(): all_stats = exchange(stats, COLUMN)  16.1 us
    all_to_all x1, waiting for transfers between devices, per_device(): own_rows = exchange(grads, PLANE)  14.8 us
    pallas_call x1, Pallas kernels, per_device(): pl.pallas_call(grads_kernel, grid=(PEERS // group,), in_specs=token_specs...  12.3 us
    all_to_all x1, waiting for transfers between devices, per_device(): rows = exchange(packed, PLANE)  11.2 us
    all_to_all x1, starting transfers between devices, per_device(): rows = exchange(packed, PLANE)  8.6 us
    pallas_call x1, Pallas kernels, per_device(): pl.pallas_call(stats_kernel, grid=(PEERS // group,), in_specs=token_specs...  6.98 us
    all_to_all x1, starting transfers between devices, per_device(): own_rows = exchange(grads, PLANE)  6.17 us
  transfers between devices with their start and end apart: 16, of which 7 were waited for; matrix products, arithmetic and copies ran while one was open for 1% of the time, Pallas kernels for 0%

profile of v3, /device:TPU:1, one launch (start us, length us, event | category | flops | bytes accessed | tf_op | source)
XLA Modules:
  0.0 114.5 jit_solution(15254429704191023557)
XLA Ops:
  0.6 3.7 %shard_map.85 = (bf16[32,272,128]{2,1,0:T(8,128)(2,1)}, bf16[128,128]{1,0:T(8,128)(2,1)}) custom-call(bf16[128,4096]{1,0:T(8,128)(2,1)} %k_ref.1, bf16[128,4096]{1,0:T(8,128)(2,1)} %v_ref.1, s32[1,128]{1,0:T(1,128)} %bitcast.8, bf16[64,128]{1,0:T(8,128)(2,1)} %bitcast.6, bf16[64,128]{1,0:T(8,128)(2,1)} %bitcast.7, s32[1,128]{1,0:T(1,128)} %bitcast.9), custom_call_target="tpu_custom_call" | custom-call | tf_op jit(solution)/shard_map/pallas_call | solution.py:265
  4.3 0.0 copy-start
  4.4 8.6 %all-to-all-start = ((bf16[32,272,128]{2,1,0:T(8,128)(2,1)}), bf16[32,272,128]{2,1,0:T(8,128)(2,1)S(1)}, u32[]{:S(2)}, u32[]{:S(2)}) async-start(bf16[32,272,128]{2,1,0:T(8,128)(2,1)} %get-tuple-element.17), calls=%async_computation | async-start | bytes 4456448 | tf_op jit(solution)/shard_map/all_to_all | solution.py:296
  13.0 5.7 %collective-permute-start.6 = (bf16[128,128]{1,0:T(8,128)(2,1)S(1)}, bf16[128,128]{1,0:T(8,128)(2,1)S(1)}, u32[]{:S(2)}, u32[]{:S(2)}) collective-permute-start(bf16[128,128]{1,0:T(8,128)(2,1)S(1)} %copy-done), channel_id=1, source_target_pairs={{0,224},{64,0},{128,64},{192,128},{32,192},{96,32},{160,96},{224,1... | collective-permute-start | bytes 98312 | tf_op jit(solution)/shard_map/ppermute | solution.py:248
  18.6 1.2 %collective-permute-start.5 = (bf16[128,128]{1,0:T(8,128)(2,1)S(1)}, bf16[128,128]{1,0:T(8,128)(2,1)S(1)}, u32[]{:S(2)}, u32[]{:S(2)}) collective-permute-start(bf16[128,128]{1,0:T(8,128)(2,1)S(1)} %copy-done), channel_id=1, source_target_pairs={{0,160},{64,224},{128,0},{192,64},{32,128},{96,192},{160,32},{224,... | collective-permute-start | bytes 98312 | tf_op jit(solution)/shard_map/ppermute | solution.py:248
  19.8 0.4 collective-permute-start.4
  20.2 4.5 %collective-permute-start.3 = (bf16[128,128]{1,0:T(8,128)(2,1)S(1)}, bf16[128,128]{1,0:T(8,128)(2,1)S(1)}, u32[]{:S(2)}, u32[]{:S(2)}) collective-permute-start(bf16[128,128]{1,0:T(8,128)(2,1)S(1)} %copy-done), channel_id=1, source_target_pairs={{0,32},{64,96},{128,160},{192,224},{32,0},{96,64},{160,128},{224,1... | collective-permute-start | bytes 98312 | tf_op jit(solution)/shard_map/ppermute | solution.py:248
  24.7 2.2 %collective-permute-start.1 = (bf16[128,128]{1,0:T(8,128)(2,1)S(1)}, bf16[128,128]{1,0:T(8,128)(2,1)S(1)}, u32[]{:S(2)}, u32[]{:S(2)}) collective-permute-start(bf16[128,128]{1,0:T(8,128)(2,1)S(1)} %copy-done), channel_id=1, source_target_pairs={{0,128},{64,192},{128,32},{192,96},{32,160},{96,224},{160,0},{224,... | collective-permute-start | bytes 98312 | tf_op jit(solution)/shard_map/ppermute | solution.py:248
  26.9 1.4 %collective-permute-start = (bf16[128,128]{1,0:T(8,128)(2,1)S(1)}, bf16[128,128]{1,0:T(8,128)(2,1)S(1)}, u32[]{:S(2)}, u32[]{:S(2)}) collective-permute-start(bf16[128,128]{1,0:T(8,128)(2,1)S(1)} %copy-done), channel_id=1, source_target_pairs={{0,64},{64,128},{128,192},{192,32},{32,96},{96,160},{160,224},{224... | collective-permute-start | bytes 98312 | tf_op jit(solution)/shard_map/ppermute | solution.py:248
  28.3 2.5 %collective-permute-done.2.refs_3_ = bf16[128,128]{1,0:T(8,128)(2,1)S(1)} collective-permute-done((bf16[128,128]{1,0:T(8,128)(2,1)S(1)}, bf16[128,128]{1,0:T(8,128)(2,1)S(1)}, u32[]{:S(2)}, u32[]{:S(2)}) %collective-permute-start.2) | collective-permute-done | bytes 32800 | tf_op jit(solution)/shard_map/ppermute | solution.py:248
  30.8 0.6 collective-permute-done.1.refs_2_
  31.4 11.2 %all-to-all-done.refs_8_.refs_9_ = bf16[32,272,128]{2,1,0:T(8,128)(2,1)S(1)} async-done(((bf16[32,272,128]{2,1,0:T(8,128)(2,1)}), bf16[32,272,128]{2,1,0:T(8,128)(2,1)S(1)}, u32[]{:S(2)}, u32[]{:S(2)}) %all-to-all-start) | async-done | bytes 2228256 | tf_op jit(solution)/shard_map/all_to_all | solution.py:296
  42.7 7.0 %shard_map.86 = f32[8,8,512]{2,1,0:T(8,128)} custom-call(bf16[128,128]{1,0:T(8,128)(2,1)S(1)} %copy-done, bf16[128,128]{1,0:T(8,128)(2,1)S(1)} %collective-permute-done.refs_1_, bf16[128,128]{1,0:T(8,128)(2,1)S(1)} %collective-permute-done.1.refs_2_, bf16[128,128]{1,0:T(8,128)(2,1)S(1)} %collective-permute-done.2.refs_3_, ...), custom_call_target="tpu_custom_call" | custom-call | tf_op jit(solution)/shard_map/pallas_call | solution.py:303
  49.7 16.1 %all_to_all.15.refs_8_ = f32[8,8,512]{2,1,0:T(8,128)S(1)} all-to-all(f32[8,8,512]{2,1,0:T(8,128)} %shard_map.86), channel_id=1, replica_groups=mesh['s'=4,'h'=2,'x'=4,'y'=4,'c'=2] {'h','s'}, dimensions={0} | all-to-all | bytes 262144 | tf_op jit(solution)/shard_map/all_to_all | solution.py:319
  65.7 12.3 %shard_map.87 = (bf16[32,256,128]{2,1,0:T(8,128)(2,1)}, bf16[64,128]{1,0:T(8,128)(2,1)}, bf16[64,128]{1,0:T(8,128)(2,1)}, bf16[64,128]{1,0:T(8,128)(2,1)}, bf16[...) custom-call(bf16[128,128]{1,0:T(8,128)(2,1)S(1)} %copy-done, ...), custom_call_target="tpu_custom_call" | custom-call | tf_op jit(solution)/shard_map/pallas_call | solution.py:320
  78.0 0.0 copy-start.8
  78.0 0.0 copy-start.7
  78.1 0.0 copy-start.1
  78.1 6.2 %all-to-all-start.2 = ((bf16[32,256,128]{2,1,0:T(8,128)(2,1)}), bf16[32,256,128]{2,1,0:T(8,128)(2,1)S(1)}, u32[]{:S(2)}, u32[]{:S(2)}) async-start(bf16[32,256,128]{2,1,0:T(8,128)(2,1)} %get-tuple-element.26), calls=%async_computation.2 | async-start | bytes 4194304 | tf_op jit(solution)/shard_map/all_to_all | solution.py:340
  84.3 0.5 collective-permute-start.7
  84.8 0.1 collective-permute-start.8
  84.9 2.1 %collective-permute-start.9 = (bf16[64,128]{1,0:T(8,128)(2,1)S(1)}, bf16[64,128]{1,0:T(8,128)(2,1)S(1)}, u32[]{:S(2)}, u32[]{:S(2)}) collective-permute-start(bf16[64,128]{1,0:T(8,128)(2,1)S(1)} %copy-done.6), channel_id=1, source_target_pairs={{0,192},{64,32},{128,96},{192,160},{32,224},{96,0},{160,64},{224,1... | collective-permute-start | bytes 49160 | tf_op jit(solution)/shard_map/ppermute | solution.py:248
  87.0 3.3 %collective-permute-start.10 = (bf16[64,128]{1,0:T(8,128)(2,1)S(1)}, bf16[64,128]{1,0:T(8,128)(2,1)S(1)}, u32[]{:S(2)}, u32[]{:S(2)}) collective-permute-start(bf16[64,128]{1,0:T(8,128)(2,1)S(1)} %copy-done.5), channel_id=1, source_target_pairs={{0,32},{64,96},{128,160},{192,224},{32,0},{96,64},{160,128},{224,1... | collective-permute-start | bytes 49160 | tf_op jit(solution)/shard_map/ppermute | solution.py:248
  90.3 1.6 %collective-permute-start.11 = (bf16[64,128]{1,0:T(8,128)(2,1)S(1)}, bf16[64,128]{1,0:T(8,128)(2,1)S(1)}, u32[]{:S(2)}, u32[]{:S(2)}) collective-permute-start(bf16[64,128]{1,0:T(8,128)(2,1)S(1)} %copy-done.4), channel_id=1, source_target_pairs={{0,96},{64,160},{128,224},{192,0},{32,64},{96,128},{160,192},{224,... | collective-permute-start | bytes 49160 | tf_op jit(solution)/shard_map/ppermute | solution.py:248
  91.9 2.0 %collective-permute-start.12 = (bf16[64,128]{1,0:T(8,128)(2,1)S(1)}, bf16[64,128]{1,0:T(8,128)(2,1)S(1)}, u32[]{:S(2)}, u32[]{:S(2)}) collective-permute-start(bf16[64,128]{1,0:T(8,128)(2,1)S(1)} %copy-done.3), channel_id=1, source_target_pairs={{0,160},{64,224},{128,0},{192,64},{32,128},{96,192},{160,32},{224,... | collective-permute-start | bytes 49160 | tf_op jit(solution)/shard_map/ppermute | solution.py:248
  93.9 0.4 collective-permute-start.13
  94.3 0.6 collective-permute-done.11
  95.0 1.8 %collective-permute-done.12 = bf16[64,128]{1,0:T(8,128)(2,1)S(1)} collective-permute-done((bf16[64,128]{1,0:T(8,128)(2,1)S(1)}, bf16[64,128]{1,0:T(8,128)(2,1)S(1)}, u32[]{:S(2)}, u32[]{:S(2)}) %collective-permute-start.12) | collective-permute-done | bytes 16416 | tf_op jit(solution)/shard_map/ppermute | solution.py:248
  96.8 0.5 collective-permute-done.13
  97.3 0.6 fusion
  97.9 14.8 %all-to-all-done.2.g_ref = bf16[32,256,128]{2,1,0:T(8,128)(2,1)S(1)} async-done(((bf16[32,256,128]{2,1,0:T(8,128)(2,1)}), bf16[32,256,128]{2,1,0:T(8,128)(2,1)S(1)}, u32[]{:S(2)}, u32[]{:S(2)}) %all-to-all-start.2) | async-done | bytes 2097184 | tf_op jit(solution)/shard_map/all_to_all | solution.py:340
  112.7 1.7 %shard_map.88 = (bf16[128,4096]{1,0:T(8,128)(2,1)}, bf16[128,4096]{1,0:T(8,128)(2,1)}) custom-call(bf16[32,256,128]{2,1,0:T(8,128)(2,1)S(1)} %all-to-all-done.2.g_ref), custom_call_target="tpu_custom_call" | custom-call | tf_op jit(solution)/shard_map/pallas_call | solution.py:344
  (24 shorter events, 0.1 us)
Async XLA Ops:
  4.3 8.6 %copy-start = (bf16[128,128]{1,0:T(8,128)(2,1)S(1)}, bf16[128,128]{1,0:T(8,128)(2,1)}, u32[]{:S(2)}) copy-start(bf16[128,128]{1,0:T(8,128)(2,1)} %get-tuple-element.16.refs_0_) | copy-start | bytes 98308
  4.4 38.3 %all-to-all-start = ((bf16[32,272,128]{2,1,0:T(8,128)(2,1)}), bf16[32,272,128]{2,1,0:T(8,128)(2,1)S(1)}, u32[]{:S(2)}, u32[]{:S(2)}) async-start(bf16[32,272,128]{2,1,0:T(8,128)(2,1)} %get-tuple-element.17), calls=%async_computation | async-start | bytes 4456448 | tf_op jit(solution)/shard_map/all_to_all | solution.py:296
  13.0 11.8 %collective-permute-start.6 = (bf16[128,128]{1,0:T(8,128)(2,1)S(1)}, bf16[128,128]{1,0:T(8,128)(2,1)S(1)}, u32[]{:S(2)}, u32[]{:S(2)}) collective-permute-start(bf16[128,128]{1,0:T(8,128)(2,1)S(1)} %copy-done), channel_id=1, source_target_pairs={{0,224},{64,0},{128,64},{192,128},{32,192},{96,32},{160,96},{224,1... | collective-permute-start | bytes 98312 | tf_op jit(solution)/shard_map/ppermute | solution.py:248
  18.6 8.3 %collective-permute-start.5 = (bf16[128,128]{1,0:T(8,128)(2,1)S(1)}, bf16[128,128]{1,0:T(8,128)(2,1)S(1)}, u32[]{:S(2)}, u32[]{:S(2)}) collective-permute-start(bf16[128,128]{1,0:T(8,128)(2,1)S(1)} %copy-done), channel_id=1, source_target_pairs={{0,160},{64,224},{128,0},{192,64},{32,128},{96,192},{160,32},{224,... | collective-permute-start | bytes 98312 | tf_op jit(solution)/shard_map/ppermute | solution.py:248
  19.8 8.5 %collective-permute-start.4 = (bf16[128,128]{1,0:T(8,128)(2,1)S(1)}, bf16[128,128]{1,0:T(8,128)(2,1)S(1)}, u32[]{:S(2)}, u32[]{:S(2)}) collective-permute-start(bf16[128,128]{1,0:T(8,128)(2,1)S(1)} %copy-done), channel_id=1, source_target_pairs={{0,96},{64,160},{128,224},{192,0},{32,64},{96,128},{160,192},{224,... | collective-permute-start | bytes 98312 | tf_op jit(solution)/shard_map/ppermute | solution.py:248
  20.2 8.0 %collective-permute-start.3 = (bf16[128,128]{1,0:T(8,128)(2,1)S(1)}, bf16[128,128]{1,0:T(8,128)(2,1)S(1)}, u32[]{:S(2)}, u32[]{:S(2)}) collective-permute-start(bf16[128,128]{1,0:T(8,128)(2,1)S(1)} %copy-done), channel_id=1, source_target_pairs={{0,32},{64,96},{128,160},{192,224},{32,0},{96,64},{160,128},{224,1... | collective-permute-start | bytes 98312 | tf_op jit(solution)/shard_map/ppermute | solution.py:248
  24.7 6.1 %collective-permute-start.2 = (bf16[128,128]{1,0:T(8,128)(2,1)S(1)}, bf16[128,128]{1,0:T(8,128)(2,1)S(1)}, u32[]{:S(2)}, u32[]{:S(2)}) collective-permute-start(bf16[128,128]{1,0:T(8,128)(2,1)S(1)} %copy-done), channel_id=1, source_target_pairs={{0,192},{64,32},{128,96},{192,160},{32,224},{96,0},{160,64},{224,1... | collective-permute-start | bytes 98312 | tf_op jit(solution)/shard_map/ppermute | solution.py:248
  24.7 6.7 %collective-permute-start.1 = (bf16[128,128]{1,0:T(8,128)(2,1)S(1)}, bf16[128,128]{1,0:T(8,128)(2,1)S(1)}, u32[]{:S(2)}, u32[]{:S(2)}) collective-permute-start(bf16[128,128]{1,0:T(8,128)(2,1)S(1)} %copy-done), channel_id=1, source_target_pairs={{0,128},{64,192},{128,32},{192,96},{32,160},{96,224},{160,0},{224,... | collective-permute-start | bytes 98312 | tf_op jit(solution)/shard_map/ppermute | solution.py:248
  26.9 4.5 %collective-permute-start = (bf16[128,128]{1,0:T(8,128)(2,1)S(1)}, bf16[128,128]{1,0:T(8,128)(2,1)S(1)}, u32[]{:S(2)}, u32[]{:S(2)}) collective-permute-start(bf16[128,128]{1,0:T(8,128)(2,1)S(1)} %copy-done), channel_id=1, source_target_pairs={{0,64},{64,128},{128,192},{192,32},{32,96},{96,160},{160,224},{224... | collective-permute-start | bytes 98312 | tf_op jit(solution)/shard_map/ppermute | solution.py:248
  78.0 6.3 %copy-start.8 = (bf16[64,128]{1,0:T(8,128)(2,1)S(1)}, bf16[64,128]{1,0:T(8,128)(2,1)}, u32[]{:S(2)}) copy-start(bf16[64,128]{1,0:T(8,128)(2,1)} %get-tuple-element.19) | copy-start | bytes 49156
  78.0 6.8 %copy-start.7 = (bf16[64,128]{1,0:T(8,128)(2,1)S(1)}, bf16[64,128]{1,0:T(8,128)(2,1)}, u32[]{:S(2)}) copy-start(bf16[64,128]{1,0:T(8,128)(2,1)} %get-tuple-element.20) | copy-start | bytes 49156
  78.0 6.9 %copy-start.6 = (bf16[64,128]{1,0:T(8,128)(2,1)S(1)}, bf16[64,128]{1,0:T(8,128)(2,1)}, u32[]{:S(2)}) copy-start(bf16[64,128]{1,0:T(8,128)(2,1)} %get-tuple-element.21) | copy-start | bytes 49156
  78.0 9.0 %copy-start.5 = (bf16[64,128]{1,0:T(8,128)(2,1)S(1)}, bf16[64,128]{1,0:T(8,128)(2,1)}, u32[]{:S(2)}) copy-start(bf16[64,128]{1,0:T(8,128)(2,1)} %get-tuple-element.22) | copy-start | bytes 49156
  78.0 12.3 %copy-start.4 = (bf16[64,128]{1,0:T(8,128)(2,1)S(1)}, bf16[64,128]{1,0:T(8,128)(2,1)}, u32[]{:S(2)}) copy-start(bf16[64,128]{1,0:T(8,128)(2,1)} %get-tuple-element.23) | copy-start | bytes 49156
  78.1 13.8 %copy-start.3 = (bf16[64,128]{1,0:T(8,128)(2,1)S(1)}, bf16[64,128]{1,0:T(8,128)(2,1)}, u32[]{:S(2)}) copy-start(bf16[64,128]{1,0:T(8,128)(2,1)} %get-tuple-element.24) | copy-start | bytes 49156
  78.1 15.8 %copy-start.2 = (bf16[64,128]{1,0:T(8,128)(2,1)S(1)}, bf16[64,128]{1,0:T(8,128)(2,1)}, u32[]{:S(2)}) copy-start(bf16[64,128]{1,0:T(8,128)(2,1)} %get-tuple-element.25) | copy-start | bytes 49156
  78.1 19.2 %copy-start.1 = (bf16[64,128]{1,0:T(8,128)(2,1)S(1)}, bf16[64,128]{1,0:T(8,128)(2,1)}, u32[]{:S(2)}) copy-start(bf16[64,128]{1,0:T(8,128)(2,1)} %get-tuple-element.18) | copy-start | bytes 49156
  78.1 34.6 %all-to-all-start.2 = ((bf16[32,256,128]{2,1,0:T(8,128)(2,1)}), bf16[32,256,128]{2,1,0:T(8,128)(2,1)S(1)}, u32[]{:S(2)}, u32[]{:S(2)}) async-start(bf16[32,256,128]{2,1,0:T(8,128)(2,1)} %get-tuple-element.26), calls=%async_computation.2 | async-start | bytes 4194304 | tf_op jit(solution)/shard_map/all_to_all | solution.py:340
  84.3 7.6 %collective-permute-start.7 = (bf16[64,128]{1,0:T(8,128)(2,1)S(1)}, bf16[64,128]{1,0:T(8,128)(2,1)S(1)}, u32[]{:S(2)}, u32[]{:S(2)}) collective-permute-start(bf16[64,128]{1,0:T(8,128)(2,1)S(1)} %copy-done.8), channel_id=1, source_target_pairs={{0,64},{64,128},{128,192},{192,32},{32,96},{96,160},{160,224},{224... | collective-permute-start | bytes 49160 | tf_op jit(solution)/shard_map/ppermute | solution.py:248
  84.8 9.1 %collective-permute-start.8 = (bf16[64,128]{1,0:T(8,128)(2,1)S(1)}, bf16[64,128]{1,0:T(8,128)(2,1)S(1)}, u32[]{:S(2)}, u32[]{:S(2)}) collective-permute-start(bf16[64,128]{1,0:T(8,128)(2,1)S(1)} %copy-done.7), channel_id=1, source_target_pairs={{0,128},{64,192},{128,32},{192,96},{32,160},{96,224},{160,0},{224,... | collective-permute-start | bytes 49160 | tf_op jit(solution)/shard_map/ppermute | solution.py:248
  84.9 9.4 %collective-permute-start.9 = (bf16[64,128]{1,0:T(8,128)(2,1)S(1)}, bf16[64,128]{1,0:T(8,128)(2,1)S(1)}, u32[]{:S(2)}, u32[]{:S(2)}) collective-permute-start(bf16[64,128]{1,0:T(8,128)(2,1)S(1)} %copy-done.6), channel_id=1, source_target_pairs={{0,192},{64,32},{128,96},{192,160},{32,224},{96,0},{160,64},{224,1... | collective-permute-start | bytes 49160 | tf_op jit(solution)/shard_map/ppermute | solution.py:248
  87.0 7.3 %collective-permute-start.10 = (bf16[64,128]{1,0:T(8,128)(2,1)S(1)}, bf16[64,128]{1,0:T(8,128)(2,1)S(1)}, u32[]{:S(2)}, u32[]{:S(2)}) collective-permute-start(bf16[64,128]{1,0:T(8,128)(2,1)S(1)} %copy-done.5), channel_id=1, source_target_pairs={{0,32},{64,96},{128,160},{192,224},{32,0},{96,64},{160,128},{224,1... | collective-permute-start | bytes 49160 | tf_op jit(solution)/shard_map/ppermute | solution.py:248
  90.3 4.7 %collective-permute-start.11 = (bf16[64,128]{1,0:T(8,128)(2,1)S(1)}, bf16[64,128]{1,0:T(8,128)(2,1)S(1)}, u32[]{:S(2)}, u32[]{:S(2)}) collective-permute-start(bf16[64,128]{1,0:T(8,128)(2,1)S(1)} %copy-done.4), channel_id=1, source_target_pairs={{0,96},{64,160},{128,224},{192,0},{32,64},{96,128},{160,192},{224,... | collective-permute-start | bytes 49160 | tf_op jit(solution)/shard_map/ppermute | solution.py:248
  91.9 4.9 %collective-permute-start.12 = (bf16[64,128]{1,0:T(8,128)(2,1)S(1)}, bf16[64,128]{1,0:T(8,128)(2,1)S(1)}, u32[]{:S(2)}, u32[]{:S(2)}) collective-permute-start(bf16[64,128]{1,0:T(8,128)(2,1)S(1)} %copy-done.3), channel_id=1, source_target_pairs={{0,160},{64,224},{128,0},{192,64},{32,128},{96,192},{160,32},{224,... | collective-permute-start | bytes 49160 | tf_op jit(solution)/shard_map/ppermute | solution.py:248
  93.9 3.4 %collective-permute-start.13 = (bf16[64,128]{1,0:T(8,128)(2,1)S(1)}, bf16[64,128]{1,0:T(8,128)(2,1)S(1)}, u32[]{:S(2)}, u32[]{:S(2)}) collective-permute-start(bf16[64,128]{1,0:T(8,128)(2,1)S(1)} %copy-done.2), channel_id=1, source_target_pairs={{0,224},{64,0},{128,64},{192,128},{32,192},{96,32},{160,96},{224,1... | collective-permute-start | bytes 49160 | tf_op jit(solution)/shard_map/ppermute | solution.py:248

commit v4 on v3

v4 whole, which is shorter than its diff:
```python
import functools
import math

import jax
import jax.numpy as jnp
from jax import lax
from jax.experimental import pallas as pl
from jax.experimental.pallas import tpu as pltpu
from jax.sharding import Mesh
from jax.sharding import PartitionSpec as P

HD = 64
LANES = 128
TOKENS = 512
ROWS = 128
EXTRA = 16
JOINED = 4
MIB = 1024 * 1024
FACTOR = 1.0 / math.sqrt(HD)
MASKED_BIAS = -1000000000.0
AXES = ("s", "h", "x", "y", "c")
PLANE = ("x", "y", "c")
COLUMN = ("h", "s")
PEERS = 32
LAYERS = 8
f32 = jnp.float32
bf16 = jnp.bfloat16
NT = (((1,), (1,)), ((), ()))
NN = (((1,), (0,)), ((), ()))


def dot(a, b, dims=NN):
    return lax.dot_general(a, b, dims, preferred_element_type=f32)


def column_of(row):
    return jnp.broadcast_to(row, (LANES, LANES)).T


def pack_kernel(k_ref, v_ref, m_ref, q_ref, d_ref, qm_ref, kv_ref, t_ref, *scratch):
    k_s, v_s, m_s, q_s, d_s, qm_s, kv_s, t_s, in_sems, small_sems, out_sems = scratch
    steps = in_sems.shape[0]
    half = k_ref.shape[1] // 2
    width = half // steps
    copy = pltpu.make_async_copy
    small = ((m_ref, m_s), (q_ref, q_s), (d_ref, d_s), (qm_ref, qm_s))
    small = [copy(src, dst, small_sems.at[i]) for i, (src, dst) in enumerate(small)]
    loads = []
    for step in range(steps):
        for i, (src, dst) in enumerate(((k_ref, k_s), (v_ref, v_s))):
            for side in range(2):
                at = pl.ds(side * half + step * width, width)
                sem = in_sems.at[step, 2 * i + side]
                loads.append(copy(src.at[:, at], dst.at[:, at], sem))
    for load in small + loads:
        load.start()
    for load in small:
        load.wait()
    t_s[:HD, :] = (q_s[...].astype(f32) * FACTOR).astype(bf16)
    t_s[HD:, :] = (d_s[...].astype(f32) * qm_s[...].astype(f32)).astype(bf16)
    stores = [copy(t_s, t_ref, out_sems.at[steps])]
    stores[0].start()
    mask = jnp.broadcast_to(m_s[...].astype(f32), (EXTRA, LANES)).astype(bf16)
    for step in range(steps):
        for load in loads[4 * step : 4 * step + 4]:
            load.wait()
        first = step * width // HD
        for j in range(first, first + width // HD, 2):
            for src, base in ((k_s, 0), (v_s, ROWS)):
                at = pl.ds(base, ROWS)
                low = src[:, j * HD : j * HD + LANES]
                high = src[:, half + j * HD : half + j * HD + LANES]
                kv_s[j, at, :] = jnp.concatenate([low[:, :HD], high[:, :HD]], axis=1)
                kv_s[j + 1, at, :] = jnp.concatenate([low[:, HD:], high[:, HD:]], axis=1)
            kv_s[j, 2 * ROWS :, :] = mask
            kv_s[j + 1, 2 * ROWS :, :] = mask
        at = pl.ds(first, width // HD)
        store = copy(kv_s.at[at], kv_ref.at[at], out_sems.at[step])
        store.start()
        stores.append(store)
    for store in stores:
        store.wait()


def unpack_kernel(g_ref, ko_ref, vo_ref, k_s, v_s, sems):
    steps = sems.shape[0]
    half = ko_ref.shape[1] // 2
    width = half // steps
    stores = []
    for step in range(steps):
        first = step * width // HD
        for i, (dst, out, base) in enumerate(((k_s, ko_ref, 0), (v_s, vo_ref, ROWS))):
            at = pl.ds(base, ROWS)
            for j in range(first, first + width // HD, 2):
                a = g_ref[j, at, :]
                b = g_ref[j + 1, at, :]
                low = jnp.concatenate([a[:, :HD], b[:, :HD]], axis=1)
                high = jnp.concatenate([a[:, HD:], b[:, HD:]], axis=1)
                dst[:, j * HD : j * HD + LANES] = low
                dst[:, half + j * HD : half + j * HD + LANES] = high
            for side in range(2):
                at = pl.ds(side * half + step * width, width)
                sem = sems.at[step, 2 * i + side]
                store = pltpu.make_async_copy(dst.at[:, at], out.at[:, at], sem)
                store.start()
                stores.append(store)
    for store in stores:
        store.wait()


def layer_index():
    return lax.axis_index("h") * 4 + lax.axis_index("s")


def spread_kernel(*refs):
    t_refs, (q_ref, d_ref, qt_ref, dt_ref, t_s) = refs[:LAYERS], refs[LAYERS:]
    layer = layer_index()
    for r in range(LAYERS):
        t_s[lax.rem(layer + LAYERS - r, LAYERS)] = t_refs[r][...]
    qt_ref[...] = jnp.zeros(qt_ref.shape, bf16)
    dt_ref[...] = jnp.zeros(dt_ref.shape, bf16)
    for block in range(TOKENS // ROWS):
        at = pl.ds(block * ROWS, ROWS)
        for head in range(2):
            mine = pl.ds(head * HD, HD)
            qt_ref[head, mine, at] = t_s[4 * head + block, :HD, :]
            dt_ref[head, mine, at] = t_s[4 * head + block, HD:, :]
            q_ref[head, at, :] = qt_ref[head, :, at].astype(f32).T.astype(bf16)
            d_ref[head, at, :] = dt_ref[head, :, at].astype(f32).T.astype(bf16)


def bias_of(k_ref, first):
    parts = []
    for i in range(JOINED):
        row = k_ref[first + i, 2 * ROWS :, :].astype(f32)
        square = column_of(row[:1, :])
        bias = jnp.where(square == 1.0, 0.0, MASKED_BIAS)
        parts.append(jnp.concatenate([bias] * (TOKENS // LANES), axis=1))
    return jnp.concatenate(parts, axis=0)


def block_of(k_ref, first, count, base):
    return k_ref[pl.ds(first, count), base : base + ROWS, :].reshape(count * ROWS, LANES)


SPLIT = (JOINED * ROWS // 8, 8, TOKENS)
FLAT = (JOINED * ROWS, TOKENS)


def stats_kernel(k_ref, qt_ref, dt_ref, o_ref, p_ref, b_ref, m_s, z_s, s_s):
    m_s[...] = jnp.full(m_s.shape, -3e38, f32)
    z_s[...] = jnp.zeros(z_s.shape, f32)
    s_s[...] = jnp.zeros(s_s.shape, f32)

    def one_pair(pair, carry):
        for b in (2 * pair, 2 * pair + 1):
            first = b * JOINED
            bias = bias_of(k_ref, first)
            keys = block_of(k_ref, first, JOINED, 0)
            values = block_of(k_ref, first, JOINED, ROWS)
            for head in range(2):
                logits = (dot(keys, qt_ref[head]) + bias).reshape(SPLIT)
                probs = dot(values, dt_ref[head]).reshape(SPLIT)
                old = m_s[head]
                new = jnp.maximum(old, jnp.max(logits, axis=0))
                scale = jnp.exp(old - new)
                weights = jnp.exp(logits - new[None])
                m_s[head] = new
                b_ref[head, b] = new
                z_s[head] = z_s[head] * scale + jnp.sum(weights, axis=0)
                s_s[head] = s_s[head] * scale + jnp.sum(weights * probs, axis=0)
                p_ref[head, b] = weights.reshape(FLAT).astype(bf16)
        return carry

    lax.fori_loop(0, PEERS // JOINED // 2, one_pair, 0)
    o_ref[...] = jnp.zeros(o_ref.shape, f32)
    for head in range(2):
        m = jnp.max(m_s[head], axis=0, keepdims=True)
        scale = jnp.exp(m_s[head] - m)
        z = jnp.sum(z_s[head] * scale, axis=0, keepdims=True)
        s = jnp.sum(s_s[head] * scale, axis=0, keepdims=True)
        for layer in range(LAYERS):
            o_ref[layer, head : head + 1, :] = m
            o_ref[layer, 2 + head : 3 + head, :] = z
            o_ref[layer, 4 + head : 5 + head, :] = s


def grads_kernel(*refs):
    a_ref, k_ref, q_ref, d_ref, dt_ref, p_ref, b_ref, g_ref = refs[:8]
    gq_refs, (l_s, r_s, acc_s, part_s, g_s, sems) = refs[8 : 8 + LAYERS], refs[8 + LAYERS :]
    acc_s[...] = jnp.zeros(acc_s.shape, f32)
    for head in range(2):
        ms = [a_ref[i, head : head + 1, :] for i in range(LAYERS)]
        m = functools.reduce(jnp.maximum, ms)
        z = jnp.zeros_like(m)
        s = jnp.zeros_like(m)
        for i in range(LAYERS):
            scale = jnp.exp(ms[i] - m)
            z = z + scale * a_ref[i, 2 + head : 3 + head, :]
            s = s + scale * a_ref[i, 4 + head : 5 + head, :]
        l_s[head] = jnp.broadcast_to(m + jnp.log(z), (8, TOKENS))
        r_s[head] = jnp.broadcast_to(s / z, (8, TOKENS))

    count = 2 * JOINED
    flat = (count * ROWS, TOKENS)

    def store_of(pair):
        at = pl.ds(pair * count, count)
        return pltpu.make_async_copy(g_s.at[at], g_ref.at[at], sems.at[pair])

    def one_pair(pair, carry):
        first = pair * count
        keys_t = block_of(k_ref, first, count, 0).astype(f32).T.astype(bf16)
        values = block_of(k_ref, first, count, ROWS)
        gk = jnp.zeros(values.shape, f32)
        gv = jnp.zeros(values.shape, f32)
        for head in range(2):
            blocks = pl.ds(2 * pair, 2)
            scale = jnp.exp(b_ref[head, blocks] - l_s[head][None])
            probs = dot(values, dt_ref[head]).reshape((2,) + SPLIT)
            weights = p_ref[head, blocks].astype(f32).reshape((2,) + SPLIT) * scale[:, None]
            grad = weights * (probs - r_s[head])
            weights = weights.reshape(flat).astype(bf16)
            grad = grad.reshape(flat).astype(bf16)
            gv = gv + dot(weights, d_ref[head])
            gk = gk + dot(grad, q_ref[head])
            acc_s[head] += dot(keys_t[head * HD : (head + 1) * HD, :], grad)
        shape = (count, ROWS, LANES)
        g_s[pl.ds(first, count), :ROWS, :] = gk.astype(bf16).reshape(shape)
        g_s[pl.ds(first, count), ROWS:, :] = gv.astype(bf16).reshape(shape)
        store_of(pair).start()
        return carry

    pairs = PEERS // count
    lax.fori_loop(0, pairs, one_pair, 0)
    for block in range(TOKENS // ROWS):
        for head in range(2):
            part = acc_s[head, :, block * ROWS : (block + 1) * ROWS] * FACTOR
            part_s[4 * head + block] = part.astype(bf16)
    for r in range(LAYERS):
        gq_refs[r][...] = part_s[lax.rem(layer_index() + r, LAYERS)]
    for pair in range(pairs):
        store_of(pair).wait()


def permuted(array, distance):
    place = lambda z: (z % 4) * 2 + z // 4
    pairs = [(place(z), place((z + distance) % LAYERS)) for z in range(LAYERS)]
    return lax.ppermute(array, ("s", "h"), pairs)


def permuted_parts(arrays):
    return [arrays[0]] + [permuted(arrays[r], r) for r in range(1, LAYERS)]


def per_device(queries, keys, values, out_grad, key_mask, query_mask):
    vmem = pl.BlockSpec(memory_space=pltpu.VMEM)
    hbm = pl.BlockSpec(memory_space=pl.ANY)
    limit = lambda mib: pltpu.CompilerParams(vmem_limit_bytes=mib * MIB)
    whole = lambda *shape: pl.BlockSpec(shape, lambda i: (0,) * len(shape))
    scratch = lambda *shape, dtype=bf16: pltpu.VMEM(shape, dtype)
    dma = pltpu.SemaphoreType.DMA
    i32 = jnp.int32
    sent_rows = 2 * ROWS + EXTRA
    steps = 2
    packed, own_tokens = pl.pallas_call(
        pack_kernel,
        in_specs=[hbm] * 6,
        out_specs=[hbm] * 2,
        out_shape=[
            pltpu.HBM((PEERS, sent_rows, LANES), bf16),
            pltpu.HBM((2 * HD, ROWS), bf16),
        ],
        scratch_shapes=[
            scratch(*keys.shape),
            scratch(*values.shape),
            scratch(1, ROWS, dtype=i32),
            scratch(HD, ROWS),
            scratch(HD, ROWS),
            scratch(1, ROWS, dtype=i32),
            scratch(PEERS, sent_rows, LANES),
            scratch(2 * HD, ROWS),
            dma((steps, 4)),
            dma((4,)),
            dma((steps + 1,)),
        ],
        compiler_params=limit(60),
    )(
        keys,
        values,
        key_mask.reshape(1, ROWS),
        queries.T,
        out_grad.T,
        query_mask.reshape(1, ROWS),
    )
    exchange = functools.partial(lax.all_to_all, split_axis=0, concat_axis=0, tiled=True)
    rows = exchange(packed, PLANE)
    tokens = permuted_parts([own_tokens] * LAYERS)

    blocks = PEERS // JOINED
    shape = jax.ShapeDtypeStruct
    q, d, qt, dt = pl.pallas_call(
        spread_kernel,
        in_specs=[vmem] * LAYERS,
        out_specs=[vmem] * 4,
        out_shape=[shape((2, TOKENS, LANES), bf16)] * 2 + [shape((2, LANES, TOKENS), bf16)] * 2,
        scratch_shapes=[scratch(LAYERS, 2 * HD, ROWS)],
        compiler_params=limit(8),
    )(*tokens)
    stats, weights, maxima = pl.pallas_call(
        stats_kernel,
        in_specs=[vmem] * 3,
        out_specs=[vmem] * 3,
        out_shape=[
            shape((LAYERS, 8, TOKENS), f32),
            shape((2, blocks) + FLAT, bf16),
            shape((2, blocks, 8, TOKENS), f32),
        ],
        scratch_shapes=[
            scratch(2, 8, TOKENS, dtype=f32),
            scratch(2, 8, TOKENS, dtype=f32),
            scratch(2, 8, TOKENS, dtype=f32),
        ],
        compiler_params=limit(24),
    )(rows, qt, dt)
    all_stats = exchange(stats, COLUMN)
    grads, *query_parts = pl.pallas_call(
        grads_kernel,
        in_specs=[vmem] * 7,
        out_specs=[hbm] + [vmem] * LAYERS,
        out_shape=[pltpu.HBM((PEERS, 2 * ROWS, LANES), bf16)] + [shape((HD, ROWS), bf16)] * LAYERS,
        scratch_shapes=[
            scratch(2, 8, TOKENS, dtype=f32),
            scratch(2, 8, TOKENS, dtype=f32),
            scratch(2, HD, TOKENS, dtype=f32),
            scratch(LAYERS, HD, ROWS),
            scratch(PEERS, 2 * ROWS, LANES),
            dma((blocks // 2,)),
        ],
        compiler_params=limit(32),
    )(all_stats, rows, q, d, dt, weights, maxima)
    own_rows = exchange(grads, PLANE)
    own_parts = permuted_parts(query_parts)
    total = functools.reduce(jnp.add, [part.astype(f32) for part in own_parts])
    grad_queries = total.astype(bf16).T
    grad_keys, grad_values = pl.pallas_call(
        unpack_kernel,
        in_specs=[vmem],
        out_specs=[hbm] * 2,
        out_shape=[pltpu.HBM(keys.shape, bf16), pltpu.HBM(values.shape, bf16)],
        scratch_shapes=[scratch(*keys.shape), scratch(*values.shape), dma((steps, 4))],
        compiler_params=limit(16),
    )(own_rows)
    return grad_queries, grad_keys, grad_values


def solution(mesh):
    fine = Mesh(mesh.devices.reshape(4, 2, 4, 4, 2), AXES)
    ctx = ("h",) + PLANE
    rows = ("s",) + ctx
    head_spec = P("s", ctx)
    row_spec = P(rows, None)
    return jax.shard_map(
        per_device,
        mesh=fine,
        in_specs=(head_spec, row_spec, row_spec, head_spec, P(rows), P("s")),
        out_specs=(head_spec, row_spec, row_spec),
        check_vma=False,
    )
```

time: 115 us -> 111 us (0.965)
  Pallas kernels: 24.6 us -> 21 us
    pallas_call x2 -> x3, Pallas kernels: 19.3 us -> 16.2 us  [the longest x1 9.49 us: per_device(): pl.pallas_call(grads_kernel, in_specs=[vmem] * 7, out_specs=[hbm] + [vmem...]
where the time goes in v4:
time: 111 us; the launch traced here: 110 us
  starting transfers between devices  39.8 us (36%)
  waiting for transfers between devices  32 us (29%)
  Pallas kernels  21 us (19%)
  blocking collectives  15.9 us (14%)
    ppermute x14, starting transfers between devices, permuted(): return lax.ppermute(array, ('s', 'h'), pairs)  25.1 us
    all_to_all x1, blocking collectives, per_device(): all_stats = exchange(stats, COLUMN)  15.9 us
    all_to_all x1, waiting for transfers between devices, per_device(): own_rows = exchange(grads, PLANE)  15 us
    all_to_all x1, waiting for transfers between devices, per_device(): rows = exchange(packed, PLANE)  11 us
    pallas_call x1, Pallas kernels, per_device(): pl.pallas_call(grads_kernel, in_specs=[vmem] * 7, out_specs=[hbm] + [vmem...  9.49 us
    all_to_all x1, starting transfers between devices, per_device(): rows = exchange(packed, PLANE)  8.6 us
    pallas_call x1, Pallas kernels, per_device(): pl.pallas_call(stats_kernel, in_specs=[vmem] * 3, out_specs=[vmem] * 3, o...  6.47 us
    ppermute x14, waiting for transfers between devices, permuted(): return lax.ppermute(array, ('s', 'h'), pairs)  6.09 us
  transfers between devices with their start and end apart: 16, of which 7 were waited for; matrix products, arithmetic and copies ran while one was open for 1% of the time, Pallas kernels for 0%

profile of v4, /device:TPU:1, one launch (start us, length us, event | category | flops | bytes accessed | tf_op | source)
XLA Modules:
  0.0 110.2 jit_solution(830557617774430915)
XLA Ops:
  0.6 3.2 %shard_map.85 = (bf16[32,272,128]{2,1,0:T(8,128)(2,1)}, bf16[128,128]{1,0:T(8,128)(2,1)}) custom-call(bf16[128,4096]{1,0:T(8,128)(2,1)} %k_ref.1, bf16[128,4096]{1,0:T(8,128)(2,1)} %v_ref.1, s32[1,128]{1,0:T(1,128)} %bitcast.8, bf16[64,128]{1,0:T(8,128)(2,1)} %bitcast.6, bf16[64,128]{1,0:T(8,128)(2,1)} %bitcast.7, s32[1,128]{1,0:T(1,128)} %bitcast.9), custom_call_target="tpu_custom_call" | custom-call | tf_op jit(solution)/shard_map/pallas_call | solution.py:266
  3.8 0.0 copy-start
  3.8 8.6 %all-to-all-start = ((bf16[32,272,128]{2,1,0:T(8,128)(2,1)}), bf16[32,272,128]{2,1,0:T(8,128)(2,1)S(1)}, u32[]{:S(2)}, u32[]{:S(2)}) async-start(bf16[32,272,128]{2,1,0:T(8,128)(2,1)} %get-tuple-element.23), calls=%async_computation | async-start | bytes 4456448 | tf_op jit(solution)/shard_map/all_to_all | solution.py:297
  12.4 5.7 %collective-permute-start.6 = (bf16[128,128]{1,0:T(8,128)(2,1)S(1)}, bf16[128,128]{1,0:T(8,128)(2,1)S(1)}, u32[]{:S(2)}, u32[]{:S(2)}) collective-permute-start(bf16[128,128]{1,0:T(8,128)(2,1)S(1)} %copy-done), channel_id=1, source_target_pairs={{0,224},{64,0},{128,64},{192,128},{32,192},{96,32},{160,96},{224,1... | collective-permute-start | bytes 98312 | tf_op jit(solution)/shard_map/ppermute | solution.py:249
  18.1 1.2 %collective-permute-start.5 = (bf16[128,128]{1,0:T(8,128)(2,1)S(1)}, bf16[128,128]{1,0:T(8,128)(2,1)S(1)}, u32[]{:S(2)}, u32[]{:S(2)}) collective-permute-start(bf16[128,128]{1,0:T(8,128)(2,1)S(1)} %copy-done), channel_id=1, source_target_pairs={{0,160},{64,224},{128,0},{192,64},{32,128},{96,192},{160,32},{224,... | collective-permute-start | bytes 98312 | tf_op jit(solution)/shard_map/ppermute | solution.py:249
  19.3 0.4 collective-permute-start.4
  19.7 4.5 %collective-permute-start.3 = (bf16[128,128]{1,0:T(8,128)(2,1)S(1)}, bf16[128,128]{1,0:T(8,128)(2,1)S(1)}, u32[]{:S(2)}, u32[]{:S(2)}) collective-permute-start(bf16[128,128]{1,0:T(8,128)(2,1)S(1)} %copy-done), channel_id=1, source_target_pairs={{0,32},{64,96},{128,160},{192,224},{32,0},{96,64},{160,128},{224,1... | collective-permute-start | bytes 98312 | tf_op jit(solution)/shard_map/ppermute | solution.py:249
  24.2 0.0 collective-permute-start.2
  24.2 0.0 collective-permute-done.6.refs_7_
  24.2 2.2 %collective-permute-start.1 = (bf16[128,128]{1,0:T(8,128)(2,1)S(1)}, bf16[128,128]{1,0:T(8,128)(2,1)S(1)}, u32[]{:S(2)}, u32[]{:S(2)}) collective-permute-start(bf16[128,128]{1,0:T(8,128)(2,1)S(1)} %copy-done), channel_id=1, source_target_pairs={{0,128},{64,192},{128,32},{192,96},{32,160},{96,224},{160,0},{224,... | collective-permute-start | bytes 98312 | tf_op jit(solution)/shard_map/ppermute | solution.py:249
  26.4 1.4 %collective-permute-start = (bf16[128,128]{1,0:T(8,128)(2,1)S(1)}, bf16[128,128]{1,0:T(8,128)(2,1)S(1)}, u32[]{:S(2)}, u32[]{:S(2)}) collective-permute-start(bf16[128,128]{1,0:T(8,128)(2,1)S(1)} %copy-done), channel_id=1, source_target_pairs={{0,64},{64,128},{128,192},{192,32},{32,96},{96,160},{160,224},{224... | collective-permute-start | bytes 98312 | tf_op jit(solution)/shard_map/ppermute | solution.py:249
  27.7 2.5 %collective-permute-done.2.refs_3_ = bf16[128,128]{1,0:T(8,128)(2,1)S(1)} collective-permute-done((bf16[128,128]{1,0:T(8,128)(2,1)S(1)}, bf16[128,128]{1,0:T(8,128)(2,1)S(1)}, u32[]{:S(2)}, u32[]{:S(2)}) %collective-permute-start.2) | collective-permute-done | bytes 32800 | tf_op jit(solution)/shard_map/ppermute | solution.py:249
  30.3 0.6 collective-permute-done.1.refs_2_
  30.9 0.3 shard_map.86
  31.2 11.0 %all-to-all-done.k_ref.refs_1_ = bf16[32,272,128]{2,1,0:T(8,128)(2,1)S(1)} async-done(((bf16[32,272,128]{2,1,0:T(8,128)(2,1)}), bf16[32,272,128]{2,1,0:T(8,128)(2,1)S(1)}, u32[]{:S(2)}, u32[]{:S(2)}) %all-to-all-start) | async-done | bytes 2228256 | tf_op jit(solution)/shard_map/all_to_all | solution.py:297
  42.1 6.5 %shard_map.87 = (f32[8,8,512]{2,1,0:T(8,128)S(1)}, bf16[2,8,512,512]{3,2,1,0:T(8,128)(2,1)S(1)}, f32[2,8,8,512]{3,2,1,0:T(8,128)S(1)}) custom-call(bf16[32,272,128]{2,1,0:T(8,128)(2,1)S(1)} %all-to-all-done.k_ref.refs_1_, bf16[2,128,512]{2,1,0:T(8,128)(2,1)S(1)} %get-tuple-element.25.qt_ref, bf16[2,128,512]{2,1,0:T(8,128)(2,1)S(1)} %get-tuple-element.26.dt_ref.refs_4_), custom_call_target="tpu_custom_call" | custom-call | tf_op jit(solution)/shard_map/pallas_call | solution.py:310
  48.6 15.9 %all_to_all.15.refs_0_ = f32[8,8,512]{2,1,0:T(8,128)S(1)} all-to-all(f32[8,8,512]{2,1,0:T(8,128)S(1)} %get-tuple-element.27), channel_id=1, replica_groups=mesh['s'=4,'h'=2,'x'=4,'y'=4,'c'=2] {'h','s'}, dimensions={0} | all-to-all | bytes 262144 | tf_op jit(solution)/shard_map/all_to_all | solution.py:326
  64.5 9.5 %shard_map.88 = (bf16[32,256,128]{2,1,0:T(8,128)(2,1)}, bf16[64,128]{1,0:T(8,128)(2,1)S(1)}, bf16[64,128]{1,0:T(8,128)(2,1)S(1)}, bf16[64,128]{1,0:T(8,128)(2,1)...) custom-call(f32[8,8,512]{2,1,0:T(8,128)S(1)} %all_to_all.15.refs_0_,, ...), custom_call_target="tpu_custom_call" | custom-call | tf_op jit(solution)/shard_map/pallas_call | solution.py:327
  74.0 6.1 %all-to-all-start.2 = ((bf16[32,256,128]{2,1,0:T(8,128)(2,1)}), bf16[32,256,128]{2,1,0:T(8,128)(2,1)S(1)}, u32[]{:S(2)}, u32[]{:S(2)}) async-start(bf16[32,256,128]{2,1,0:T(8,128)(2,1)} %get-tuple-element.40), calls=%async_computation.2 | async-start | bytes 4194304 | tf_op jit(solution)/shard_map/all_to_all | solution.py:342
  80.0 0.4 collective-permute-start.7
  80.4 0.2 collective-permute-start.8
  80.6 2.0 %collective-permute-start.9 = (bf16[64,128]{1,0:T(8,128)(2,1)S(1)}, bf16[64,128]{1,0:T(8,128)(2,1)S(1)}, u32[]{:S(2)}, u32[]{:S(2)}) collective-permute-start(bf16[64,128]{1,0:T(8,128)(2,1)S(1)} %get-tuple-element.35), channel_id=1, source_target_pairs={{0,192},{64,32},{128,96},{192,160},{32,224},{96,0},{160,64},{224,1... | collective-permute-start | bytes 49160 | tf_op jit(solution)/shard_map/ppermute | solution.py:249
  82.6 3.5 %collective-permute-start.10 = (bf16[64,128]{1,0:T(8,128)(2,1)S(1)}, bf16[64,128]{1,0:T(8,128)(2,1)S(1)}, u32[]{:S(2)}, u32[]{:S(2)}) collective-permute-start(bf16[64,128]{1,0:T(8,128)(2,1)S(1)} %get-tuple-element.36), channel_id=1, source_target_pairs={{0,32},{64,96},{128,160},{192,224},{32,0},{96,64},{160,128},{224,1... | collective-permute-start | bytes 49160 | tf_op jit(solution)/shard_map/ppermute | solution.py:249
  86.1 1.4 %collective-permute-start.11 = (bf16[64,128]{1,0:T(8,128)(2,1)S(1)}, bf16[64,128]{1,0:T(8,128)(2,1)S(1)}, u32[]{:S(2)}, u32[]{:S(2)}) collective-permute-start(bf16[64,128]{1,0:T(8,128)(2,1)S(1)} %get-tuple-element.37), channel_id=1, source_target_pairs={{0,96},{64,160},{128,224},{192,0},{32,64},{96,128},{160,192},{224,... | collective-permute-start | bytes 49160 | tf_op jit(solution)/shard_map/ppermute | solution.py:249
  87.5 2.0 %collective-permute-start.12 = (bf16[64,128]{1,0:T(8,128)(2,1)S(1)}, bf16[64,128]{1,0:T(8,128)(2,1)S(1)}, u32[]{:S(2)}, u32[]{:S(2)}) collective-permute-start(bf16[64,128]{1,0:T(8,128)(2,1)S(1)} %get-tuple-element.38), channel_id=1, source_target_pairs={{0,160},{64,224},{128,0},{192,64},{32,128},{96,192},{160,32},{224,... | collective-permute-start | bytes 49160 | tf_op jit(solution)/shard_map/ppermute | solution.py:249
  89.4 0.5 collective-permute-start.13
  89.9 0.8 collective-permute-done.11
  90.8 1.5 %collective-permute-done.12 = bf16[64,128]{1,0:T(8,128)(2,1)S(1)} collective-permute-done((bf16[64,128]{1,0:T(8,128)(2,1)S(1)}, bf16[64,128]{1,0:T(8,128)(2,1)S(1)}, u32[]{:S(2)}, u32[]{:S(2)}) %collective-permute-start.12) | collective-permute-done | bytes 16416 | tf_op jit(solution)/shard_map/ppermute | solution.py:249
  92.2 0.6 collective-permute-done.13
  92.8 0.6 fusion
  93.5 15.0 %all-to-all-done.2.g_ref = bf16[32,256,128]{2,1,0:T(8,128)(2,1)S(1)} async-done(((bf16[32,256,128]{2,1,0:T(8,128)(2,1)}), bf16[32,256,128]{2,1,0:T(8,128)(2,1)S(1)}, u32[]{:S(2)}, u32[]{:S(2)}) %all-to-all-start.2) | async-done | bytes 2097184 | tf_op jit(solution)/shard_map/all_to_all | solution.py:342
  108.4 1.6 %shard_map.89 = (bf16[128,4096]{1,0:T(8,128)(2,1)}, bf16[128,4096]{1,0:T(8,128)(2,1)}) custom-call(bf16[32,256,128]{2,1,0:T(8,128)(2,1)S(1)} %all-to-all-done.2.g_ref), custom_call_target="tpu_custom_call" | custom-call | tf_op jit(solution)/shard_map/pallas_call | solution.py:346
  (9 shorter events, 0.0 us)
Async XLA Ops:
  3.8 8.6 %copy-start = (bf16[128,128]{1,0:T(8,128)(2,1)S(1)}, bf16[128,128]{1,0:T(8,128)(2,1)}, u32[]{:S(2)}) copy-start(bf16[128,128]{1,0:T(8,128)(2,1)} %get-tuple-element.24.refs_0_) | copy-start | bytes 98308
  3.8 38.3 %all-to-all-start = ((bf16[32,272,128]{2,1,0:T(8,128)(2,1)}), bf16[32,272,128]{2,1,0:T(8,128)(2,1)S(1)}, u32[]{:S(2)}, u32[]{:S(2)}) async-start(bf16[32,272,128]{2,1,0:T(8,128)(2,1)} %get-tuple-element.23), calls=%async_computation | async-start | bytes 4456448 | tf_op jit(solution)/shard_map/all_to_all | solution.py:297
  12.4 11.8 %collective-permute-start.6 = (bf16[128,128]{1,0:T(8,128)(2,1)S(1)}, bf16[128,128]{1,0:T(8,128)(2,1)S(1)}, u32[]{:S(2)}, u32[]{:S(2)}) collective-permute-start(bf16[128,128]{1,0:T(8,128)(2,1)S(1)} %copy-done), channel_id=1, source_target_pairs={{0,224},{64,0},{128,64},{192,128},{32,192},{96,32},{160,96},{224,1... | collective-permute-start | bytes 98312 | tf_op jit(solution)/shard_map/ppermute | solution.py:249
  18.1 8.3 %collective-permute-start.5 = (bf16[128,128]{1,0:T(8,128)(2,1)S(1)}, bf16[128,128]{1,0:T(8,128)(2,1)S(1)}, u32[]{:S(2)}, u32[]{:S(2)}) collective-permute-start(bf16[128,128]{1,0:T(8,128)(2,1)S(1)} %copy-done), channel_id=1, source_target_pairs={{0,160},{64,224},{128,0},{192,64},{32,128},{96,192},{160,32},{224,... | collective-permute-start | bytes 98312 | tf_op jit(solution)/shard_map/ppermute | solution.py:249
  19.3 8.5 %collective-permute-start.4 = (bf16[128,128]{1,0:T(8,128)(2,1)S(1)}, bf16[128,128]{1,0:T(8,128)(2,1)S(1)}, u32[]{:S(2)}, u32[]{:S(2)}) collective-permute-start(bf16[128,128]{1,0:T(8,128)(2,1)S(1)} %copy-done), channel_id=1, source_target_pairs={{0,96},{64,160},{128,224},{192,0},{32,64},{96,128},{160,192},{224,... | collective-permute-start | bytes 98312 | tf_op jit(solution)/shard_map/ppermute | solution.py:249
  19.7 8.0 %collective-permute-start.3 = (bf16[128,128]{1,0:T(8,128)(2,1)S(1)}, bf16[128,128]{1,0:T(8,128)(2,1)S(1)}, u32[]{:S(2)}, u32[]{:S(2)}) collective-permute-start(bf16[128,128]{1,0:T(8,128)(2,1)S(1)} %copy-done), channel_id=1, source_target_pairs={{0,32},{64,96},{128,160},{192,224},{32,0},{96,64},{160,128},{224,1... | collective-permute-start | bytes 98312 | tf_op jit(solution)/shard_map/ppermute | solution.py:249
  24.2 6.1 %collective-permute-start.2 = (bf16[128,128]{1,0:T(8,128)(2,1)S(1)}, bf16[128,128]{1,0:T(8,128)(2,1)S(1)}, u32[]{:S(2)}, u32[]{:S(2)}) collective-permute-start(bf16[128,128]{1,0:T(8,128)(2,1)S(1)} %copy-done), channel_id=1, source_target_pairs={{0,192},{64,32},{128,96},{192,160},{32,224},{96,0},{160,64},{224,1... | collective-permute-start | bytes 98312 | tf_op jit(solution)/shard_map/ppermute | solution.py:249
  24.2 6.7 %collective-permute-start.1 = (bf16[128,128]{1,0:T(8,128)(2,1)S(1)}, bf16[128,128]{1,0:T(8,128)(2,1)S(1)}, u32[]{:S(2)}, u32[]{:S(2)}) collective-permute-start(bf16[128,128]{1,0:T(8,128)(2,1)S(1)} %copy-done), channel_id=1, source_target_pairs={{0,128},{64,192},{128,32},{192,96},{32,160},{96,224},{160,0},{224,... | collective-permute-start | bytes 98312 | tf_op jit(solution)/shard_map/ppermute | solution.py:249
  26.4 4.5 %collective-permute-start = (bf16[128,128]{1,0:T(8,128)(2,1)S(1)}, bf16[128,128]{1,0:T(8,128)(2,1)S(1)}, u32[]{:S(2)}, u32[]{:S(2)}) collective-permute-start(bf16[128,128]{1,0:T(8,128)(2,1)S(1)} %copy-done), channel_id=1, source_target_pairs={{0,64},{64,128},{128,192},{192,32},{32,96},{96,160},{160,224},{224... | collective-permute-start | bytes 98312 | tf_op jit(solution)/shard_map/ppermute | solution.py:249
  74.0 34.4 %all-to-all-start.2 = ((bf16[32,256,128]{2,1,0:T(8,128)(2,1)}), bf16[32,256,128]{2,1,0:T(8,128)(2,1)S(1)}, u32[]{:S(2)}, u32[]{:S(2)}) async-start(bf16[32,256,128]{2,1,0:T(8,128)(2,1)} %get-tuple-element.40), calls=%async_computation.2 | async-start | bytes 4194304 | tf_op jit(solution)/shard_map/all_to_all | solution.py:342
  80.0 7.4 %collective-permute-start.7 = (bf16[64,128]{1,0:T(8,128)(2,1)S(1)}, bf16[64,128]{1,0:T(8,128)(2,1)S(1)}, u32[]{:S(2)}, u32[]{:S(2)}) collective-permute-start(bf16[64,128]{1,0:T(8,128)(2,1)S(1)} %get-tuple-element.33), channel_id=1, source_target_pairs={{0,64},{64,128},{128,192},{192,32},{32,96},{96,160},{160,224},{224... | collective-permute-start | bytes 49160 | tf_op jit(solution)/shard_map/ppermute | solution.py:249
  80.4 9.0 %collective-permute-start.8 = (bf16[64,128]{1,0:T(8,128)(2,1)S(1)}, bf16[64,128]{1,0:T(8,128)(2,1)S(1)}, u32[]{:S(2)}, u32[]{:S(2)}) collective-permute-start(bf16[64,128]{1,0:T(8,128)(2,1)S(1)} %get-tuple-element.34), channel_id=1, source_target_pairs={{0,128},{64,192},{128,32},{192,96},{32,160},{96,224},{160,0},{224,... | collective-permute-start | bytes 49160 | tf_op jit(solution)/shard_map/ppermute | solution.py:249
  80.6 9.3 %collective-permute-start.9 = (bf16[64,128]{1,0:T(8,128)(2,1)S(1)}, bf16[64,128]{1,0:T(8,128)(2,1)S(1)}, u32[]{:S(2)}, u32[]{:S(2)}) collective-permute-start(bf16[64,128]{1,0:T(8,128)(2,1)S(1)} %get-tuple-element.35), channel_id=1, source_target_pairs={{0,192},{64,32},{128,96},{192,160},{32,224},{96,0},{160,64},{224,1... | collective-permute-start | bytes 49160 | tf_op jit(solution)/shard_map/ppermute | solution.py:249
  82.6 7.3 %collective-permute-start.10 = (bf16[64,128]{1,0:T(8,128)(2,1)S(1)}, bf16[64,128]{1,0:T(8,128)(2,1)S(1)}, u32[]{:S(2)}, u32[]{:S(2)}) collective-permute-start(bf16[64,128]{1,0:T(8,128)(2,1)S(1)} %get-tuple-element.36), channel_id=1, source_target_pairs={{0,32},{64,96},{128,160},{192,224},{32,0},{96,64},{160,128},{224,1... | collective-permute-start | bytes 49160 | tf_op jit(solution)/shard_map/ppermute | solution.py:249
  86.1 4.7 %collective-permute-start.11 = (bf16[64,128]{1,0:T(8,128)(2,1)S(1)}, bf16[64,128]{1,0:T(8,128)(2,1)S(1)}, u32[]{:S(2)}, u32[]{:S(2)}) collective-permute-start(bf16[64,128]{1,0:T(8,128)(2,1)S(1)} %get-tuple-element.37), channel_id=1, source_target_pairs={{0,96},{64,160},{128,224},{192,0},{32,64},{96,128},{160,192},{224,... | collective-permute-start | bytes 49160 | tf_op jit(solution)/shard_map/ppermute | solution.py:249
  87.5 4.7 %collective-permute-start.12 = (bf16[64,128]{1,0:T(8,128)(2,1)S(1)}, bf16[64,128]{1,0:T(8,128)(2,1)S(1)}, u32[]{:S(2)}, u32[]{:S(2)}) collective-permute-start(bf16[64,128]{1,0:T(8,128)(2,1)S(1)} %get-tuple-element.38), channel_id=1, source_target_pairs={{0,160},{64,224},{128,0},{192,64},{32,128},{96,192},{160,32},{224,... | collective-permute-start | bytes 49160 | tf_op jit(solution)/shard_map/ppermute | solution.py:249
  89.4 3.4 %collective-permute-start.13 = (bf16[64,128]{1,0:T(8,128)(2,1)S(1)}, bf16[64,128]{1,0:T(8,128)(2,1)S(1)}, u32[]{:S(2)}, u32[]{:S(2)}) collective-permute-start(bf16[64,128]{1,0:T(8,128)(2,1)S(1)} %get-tuple-element.39), channel_id=1, source_target_pairs={{0,224},{64,0},{128,64},{192,128},{32,192},{96,32},{160,96},{224,1... | collective-permute-start | bytes 49160 | tf_op jit(solution)/shard_map/ppermute | solution.py:249

commit v5 on v4

--- a/solution.py
+++ b/solution.py
@@ -14,7 +14,9 @@
 TOKENS = 512
 ROWS = 128
 EXTRA = 16
-JOINED = 4
+JOINED = 2
+UNROLLED = 8
+MERGED = 4
 MIB = 1024 * 1024
 FACTOR = 1.0 / math.sqrt(HD)
 MASKED_BIAS = -1000000000.0
@@ -152,8 +154,9 @@
     z_s[...] = jnp.zeros(z_s.shape, f32)
     s_s[...] = jnp.zeros(s_s.shape, f32)
 
-    def one_pair(pair, carry):
-        for b in (2 * pair, 2 * pair + 1):
+    def one_step(step, carry):
+        for part in range(UNROLLED):
+            b = step * UNROLLED + part
             first = b * JOINED
             bias = bias_of(k_ref, first)
             keys = block_of(k_ref, first, JOINED, 0)
@@ -172,17 +175,18 @@
                 p_ref[head, b] = weights.reshape(FLAT).astype(bf16)
         return carry
 
-    lax.fori_loop(0, PEERS // JOINED // 2, one_pair, 0)
-    o_ref[...] = jnp.zeros(o_ref.shape, f32)
+    lax.fori_loop(0, PEERS // JOINED // UNROLLED, one_step, 0)
     for head in range(2):
         m = jnp.max(m_s[head], axis=0, keepdims=True)
         scale = jnp.exp(m_s[head] - m)
         z = jnp.sum(z_s[head] * scale, axis=0, keepdims=True)
         s = jnp.sum(s_s[head] * scale, axis=0, keepdims=True)
-        for layer in range(LAYERS):
-            o_ref[layer, head : head + 1, :] = m
-            o_ref[layer, 2 + head : 3 + head, :] = z
-            o_ref[layer, 4 + head : 5 + head, :] = s
+        for i, row in enumerate((m + jnp.log(z), s / z)):
+            for half in range(2):
+                at = 4 * i + 2 * head + half
+                part = row[:, half * (TOKENS // 2) : (half + 1) * (TOKENS // 2)]
+                for layer in range(LAYERS):
+                    o_ref[layer, at : at + 1, :] = part
 
 
 def grads_kernel(*refs):
@@ -190,35 +194,37 @@
     gq_refs, (l_s, r_s, acc_s, part_s, g_s, sems) = refs[8 : 8 + LAYERS], refs[8 + LAYERS :]
     acc_s[...] = jnp.zeros(acc_s.shape, f32)
     for head in range(2):
-        ms = [a_ref[i, head : head + 1, :] for i in range(LAYERS)]
-        m = functools.reduce(jnp.maximum, ms)
-        z = jnp.zeros_like(m)
-        s = jnp.zeros_like(m)
-        for i in range(LAYERS):
-            scale = jnp.exp(ms[i] - m)
-            z = z + scale * a_ref[i, 2 + head : 3 + head, :]
-            s = s + scale * a_ref[i, 4 + head : 5 + head, :]
-        l_s[head] = jnp.broadcast_to(m + jnp.log(z), (8, TOKENS))
-        r_s[head] = jnp.broadcast_to(s / z, (8, TOKENS))
-
-    count = 2 * JOINED
+        for half in range(2):
+            at = 2 * head + half
+            sums = [a_ref[i, at : at + 1, :] for i in range(LAYERS)]
+            inner = [a_ref[i, 4 + at : 5 + at, :] for i in range(LAYERS)]
+            m = functools.reduce(jnp.maximum, sums)
+            shares = [jnp.exp(part - m) for part in sums]
+            z = functools.reduce(jnp.add, shares)
+            s = functools.reduce(jnp.add, [x * y for x, y in zip(shares, inner)])
+            lanes = pl.ds(half * (TOKENS // 2), TOKENS // 2)
+            l_s[head, :, lanes] = jnp.broadcast_to(m + jnp.log(z), (8, TOKENS // 2))
+            r_s[head, :, lanes] = jnp.broadcast_to(s / z, (8, TOKENS // 2))
+
+    count = MERGED * JOINED
     flat = (count * ROWS, TOKENS)
-
-    def store_of(pair):
-        at = pl.ds(pair * count, count)
-        return pltpu.make_async_copy(g_s.at[at], g_ref.at[at], sems.at[pair])
-
-    def one_pair(pair, carry):
-        first = pair * count
+    parts = (MERGED,) + SPLIT
+
+    def store_of(step):
+        at = pl.ds(step * count, count)
+        return pltpu.make_async_copy(g_s.at[at], g_ref.at[at], sems.at[step])
+
+    def one_step(step, carry):
+        first = step * count
         keys_t = block_of(k_ref, first, count, 0).astype(f32).T.astype(bf16)
         values = block_of(k_ref, first, count, ROWS)
         gk = jnp.zeros(values.shape, f32)
         gv = jnp.zeros(values.shape, f32)
         for head in range(2):
-            blocks = pl.ds(2 * pair, 2)
+            blocks = pl.ds(MERGED * step, MERGED)
             scale = jnp.exp(b_ref[head, blocks] - l_s[head][None])
-            probs = dot(values, dt_ref[head]).reshape((2,) + SPLIT)
-            weights = p_ref[head, blocks].astype(f32).reshape((2,) + SPLIT) * scale[:, None]
+            probs = dot(values, dt_ref[head]).reshape(parts)
+            weights = p_ref[head, blocks].astype(f32).reshape(parts) * scale[:, None]
             grad = weights * (probs - r_s[head])
             weights = weights.reshape(flat).astype(bf16)
             grad = grad.reshape(flat).astype(bf16)
@@ -228,19 +234,19 @@
         shape = (count, ROWS, LANES)
         g_s[pl.ds(first, count), :ROWS, :] = gk.astype(bf16).reshape(shape)
         g_s[pl.ds(first, count), ROWS:, :] = gv.astype(bf16).reshape(shape)
-        store_of(pair).start()
+        store_of(step).start()
         return carry
 
-    pairs = PEERS // count
-    lax.fori_loop(0, pairs, one_pair, 0)
+    steps = PEERS // count
+    lax.fori_loop(0, steps, one_step, 0)
     for block in range(TOKENS // ROWS):
         for head in range(2):
             part = acc_s[head, :, block * ROWS : (block + 1) * ROWS] * FACTOR
             part_s[4 * head + block] = part.astype(bf16)
     for r in range(LAYERS):
         gq_refs[r][...] = part_s[lax.rem(layer_index() + r, LAYERS)]
-    for pair in range(pairs):
-        store_of(pair).wait()
+    for step in range(steps):
+        store_of(step).wait()
 
 
 def permuted(array, distance):
@@ -312,7 +318,7 @@
         in_specs=[vmem] * 3,
         out_specs=[vmem] * 3,
         out_shape=[
-            shape((LAYERS, 8, TOKENS), f32),
+            shape((LAYERS, 8, TOKENS // 2), f32),
             shape((2, blocks) + FLAT, bf16),
             shape((2, blocks, 8, TOKENS), f32),
         ],
@@ -335,7 +341,7 @@
             scratch(2, HD, TOKENS, dtype=f32),
             scratch(LAYERS, HD, ROWS),
             scratch(PEERS, 2 * ROWS, LANES),
-            dma((blocks // 2,)),
+            dma((blocks // MERGED,)),
         ],
         compiler_params=limit(32),
     )(all_stats, rows, q, d, dt, weights, maxima)

time: 111 us -> 109 us (0.982)
  no operation moved by 1% of the time
where the time goes in v5:
time: 109 us
  starting transfers between devices  39.9 us (37%)
  waiting for transfers between devices  32.1 us (29%)
  Pallas kernels  20.5 us (19%)
  blocking collectives  15.2 us (14%)
    ppermute x14, starting transfers between devices, permuted(): return lax.ppermute(array, ('s', 'h'), pairs)  25.1 us
    all_to_all x1, blocking collectives, per_device(): all_stats = exchange(stats, COLUMN)  15.2 us
    all_to_all x1, waiting for transfers between devices, per_device(): own_rows = exchange(grads, PLANE)  15 us
    all_to_all x1, waiting for transfers between devices, per_device(): rows = exchange(packed, PLANE)  11 us
    pallas_call x1, Pallas kernels, per_device(): pl.pallas_call(grads_kernel, in_specs=[vmem] * 7, out_specs=[hbm] + [vmem...  9.48 us
    all_to_all x1, starting transfers between devices, per_device(): rows = exchange(packed, PLANE)  8.6 us
    all_to_all x1, starting transfers between devices, per_device(): own_rows = exchange(grads, PLANE)  6.19 us
    ppermute x14, waiting for transfers between devices, permuted(): return lax.ppermute(array, ('s', 'h'), pairs)  6.16 us
  transfers between devices with their start and end apart: 16, of which 7 were waited for; matrix products, arithmetic and copies ran while one was open for 1% of the time, Pallas kernels for 0%

profile of v5, /device:TPU:1, one launch (start us, length us, event | category | flops | bytes accessed | tf_op | source)
XLA Modules:
  0.0 109.1 jit_solution(18064854837114175884)
XLA Ops:
  0.6 3.2 %shard_map.85 = (bf16[32,272,128]{2,1,0:T(8,128)(2,1)}, bf16[128,128]{1,0:T(8,128)(2,1)}) custom-call(bf16[128,4096]{1,0:T(8,128)(2,1)} %k_ref.1, bf16[128,4096]{1,0:T(8,128)(2,1)} %v_ref.1, s32[1,128]{1,0:T(1,128)} %bitcast.8, bf16[64,128]{1,0:T(8,128)(2,1)} %bitcast.6, bf16[64,128]{1,0:T(8,128)(2,1)} %bitcast.7, s32[1,128]{1,0:T(1,128)} %bitcast.9), custom_call_target="tpu_custom_call" | custom-call | tf_op jit(solution)/shard_map/pallas_call | solution.py:272
  3.8 0.0 copy-start
  3.8 8.6 %all-to-all-start = ((bf16[32,272,128]{2,1,0:T(8,128)(2,1)}), bf16[32,272,128]{2,1,0:T(8,128)(2,1)S(1)}, u32[]{:S(2)}, u32[]{:S(2)}) async-start(bf16[32,272,128]{2,1,0:T(8,128)(2,1)} %get-tuple-element.23), calls=%async_computation | async-start | bytes 4456448 | tf_op jit(solution)/shard_map/all_to_all | solution.py:303
  12.4 5.7 %collective-permute-start.6 = (bf16[128,128]{1,0:T(8,128)(2,1)S(1)}, bf16[128,128]{1,0:T(8,128)(2,1)S(1)}, u32[]{:S(2)}, u32[]{:S(2)}) collective-permute-start(bf16[128,128]{1,0:T(8,128)(2,1)S(1)} %copy-done), channel_id=1, source_target_pairs={{0,224},{64,0},{128,64},{192,128},{32,192},{96,32},{160,96},{224,1... | collective-permute-start | bytes 98312 | tf_op jit(solution)/shard_map/ppermute | solution.py:255
  18.1 1.2 %collective-permute-start.5 = (bf16[128,128]{1,0:T(8,128)(2,1)S(1)}, bf16[128,128]{1,0:T(8,128)(2,1)S(1)}, u32[]{:S(2)}, u32[]{:S(2)}) collective-permute-start(bf16[128,128]{1,0:T(8,128)(2,1)S(1)} %copy-done), channel_id=1, source_target_pairs={{0,160},{64,224},{128,0},{192,64},{32,128},{96,192},{160,32},{224,... | collective-permute-start | bytes 98312 | tf_op jit(solution)/shard_map/ppermute | solution.py:255
  19.3 0.4 collective-permute-start.4
  19.7 4.5 %collective-permute-start.3 = (bf16[128,128]{1,0:T(8,128)(2,1)S(1)}, bf16[128,128]{1,0:T(8,128)(2,1)S(1)}, u32[]{:S(2)}, u32[]{:S(2)}) collective-permute-start(bf16[128,128]{1,0:T(8,128)(2,1)S(1)} %copy-done), channel_id=1, source_target_pairs={{0,32},{64,96},{128,160},{192,224},{32,0},{96,64},{160,128},{224,1... | collective-permute-start | bytes 98312 | tf_op jit(solution)/shard_map/ppermute | solution.py:255
  24.2 0.0 collective-permute-start.2
  24.2 0.0 collective-permute-done.6.refs_7_
  24.2 2.2 %collective-permute-start.1 = (bf16[128,128]{1,0:T(8,128)(2,1)S(1)}, bf16[128,128]{1,0:T(8,128)(2,1)S(1)}, u32[]{:S(2)}, u32[]{:S(2)}) collective-permute-start(bf16[128,128]{1,0:T(8,128)(2,1)S(1)} %copy-done), channel_id=1, source_target_pairs={{0,128},{64,192},{128,32},{192,96},{32,160},{96,224},{160,0},{224,... | collective-permute-start | bytes 98312 | tf_op jit(solution)/shard_map/ppermute | solution.py:255
  26.4 1.4 %collective-permute-start = (bf16[128,128]{1,0:T(8,128)(2,1)S(1)}, bf16[128,128]{1,0:T(8,128)(2,1)S(1)}, u32[]{:S(2)}, u32[]{:S(2)}) collective-permute-start(bf16[128,128]{1,0:T(8,128)(2,1)S(1)} %copy-done), channel_id=1, source_target_pairs={{0,64},{64,128},{128,192},{192,32},{32,96},{96,160},{160,224},{224... | collective-permute-start | bytes 98312 | tf_op jit(solution)/shard_map/ppermute | solution.py:255
  27.7 2.5 %collective-permute-done.2.refs_3_ = bf16[128,128]{1,0:T(8,128)(2,1)S(1)} collective-permute-done((bf16[128,128]{1,0:T(8,128)(2,1)S(1)}, bf16[128,128]{1,0:T(8,128)(2,1)S(1)}, u32[]{:S(2)}, u32[]{:S(2)}) %collective-permute-start.2) | collective-permute-done | bytes 32800 | tf_op jit(solution)/shard_map/ppermute | solution.py:255
  30.3 0.6 collective-permute-done.1.refs_2_
  30.9 0.3 shard_map.86
  31.2 11.0 %all-to-all-done.k_ref.refs_1_ = bf16[32,272,128]{2,1,0:T(8,128)(2,1)S(1)} async-done(((bf16[32,272,128]{2,1,0:T(8,128)(2,1)}), bf16[32,272,128]{2,1,0:T(8,128)(2,1)S(1)}, u32[]{:S(2)}, u32[]{:S(2)}) %all-to-all-start) | async-done | bytes 2228256 | tf_op jit(solution)/shard_map/all_to_all | solution.py:303
  42.1 5.9 %shard_map.87 = (f32[8,8,256]{2,1,0:T(8,128)S(1)}, bf16[2,16,256,512]{3,2,1,0:T(8,128)(2,1)S(1)}, f32[2,16,8,512]{3,2,1,0:T(8,128)S(1)}) custom-call(bf16[32,272,128]{2,1,0:T(8,128)(2,1)S(1)} %all-to-all-done.k_ref.refs_1_, bf16[2,128,512]{2,1,0:T(8,128)(2,1)S(1)} %get-tuple-element.25.qt_ref, bf16[2,128,512]{2,1,0:T(8,128)(2,1)S(1)} %get-tuple-element.26.dt_ref.refs_4_), custom_call_target="tpu_custom_call" | custom-call | tf_op jit(solution)/shard_map/pallas_call | solution.py:316
  48.1 15.2 %all_to_all.15.refs_0_ = f32[8,8,256]{2,1,0:T(8,128)S(1)} all-to-all(f32[8,8,256]{2,1,0:T(8,128)S(1)} %get-tuple-element.27), channel_id=1, replica_groups=mesh['s'=4,'h'=2,'x'=4,'y'=4,'c'=2] {'h','s'}, dimensions={0} | all-to-all | bytes 131072 | tf_op jit(solution)/shard_map/all_to_all | solution.py:332
  63.3 9.5 %shard_map.88 = (bf16[32,256,128]{2,1,0:T(8,128)(2,1)}, bf16[64,128]{1,0:T(8,128)(2,1)S(1)}, bf16[64,128]{1,0:T(8,128)(2,1)S(1)}, bf16[64,128]{1,0:T(8,128)(2,1)...) custom-call(f32[8,8,256]{2,1,0:T(8,128)S(1)} %all_to_all.15.refs_0_,, ...), custom_call_target="tpu_custom_call" | custom-call | tf_op jit(solution)/shard_map/pallas_call | solution.py:333
  72.8 6.2 %all-to-all-start.2 = ((bf16[32,256,128]{2,1,0:T(8,128)(2,1)}), bf16[32,256,128]{2,1,0:T(8,128)(2,1)S(1)}, u32[]{:S(2)}, u32[]{:S(2)}) async-start(bf16[32,256,128]{2,1,0:T(8,128)(2,1)} %get-tuple-element.40), calls=%async_computation.2 | async-start | bytes 4194304 | tf_op jit(solution)/shard_map/all_to_all | solution.py:348
  79.0 0.4 collective-permute-start.7
  79.3 0.1 collective-permute-start.8
  79.5 2.1 %collective-permute-start.9 = (bf16[64,128]{1,0:T(8,128)(2,1)S(1)}, bf16[64,128]{1,0:T(8,128)(2,1)S(1)}, u32[]{:S(2)}, u32[]{:S(2)}) collective-permute-start(bf16[64,128]{1,0:T(8,128)(2,1)S(1)} %get-tuple-element.35), channel_id=1, source_target_pairs={{0,192},{64,32},{128,96},{192,160},{32,224},{96,0},{160,64},{224,1... | collective-permute-start | bytes 49160 | tf_op jit(solution)/shard_map/ppermute | solution.py:255
  81.6 3.4 %collective-permute-start.10 = (bf16[64,128]{1,0:T(8,128)(2,1)S(1)}, bf16[64,128]{1,0:T(8,128)(2,1)S(1)}, u32[]{:S(2)}, u32[]{:S(2)}) collective-permute-start(bf16[64,128]{1,0:T(8,128)(2,1)S(1)} %get-tuple-element.36), channel_id=1, source_target_pairs={{0,32},{64,96},{128,160},{192,224},{32,0},{96,64},{160,128},{224,1... | collective-permute-start | bytes 49160 | tf_op jit(solution)/shard_map/ppermute | solution.py:255
  84.9 1.8 %collective-permute-start.11 = (bf16[64,128]{1,0:T(8,128)(2,1)S(1)}, bf16[64,128]{1,0:T(8,128)(2,1)S(1)}, u32[]{:S(2)}, u32[]{:S(2)}) collective-permute-start(bf16[64,128]{1,0:T(8,128)(2,1)S(1)} %get-tuple-element.37), channel_id=1, source_target_pairs={{0,96},{64,160},{128,224},{192,0},{32,64},{96,128},{160,192},{224,... | collective-permute-start | bytes 49160 | tf_op jit(solution)/shard_map/ppermute | solution.py:255
  86.7 1.8 %collective-permute-start.12 = (bf16[64,128]{1,0:T(8,128)(2,1)S(1)}, bf16[64,128]{1,0:T(8,128)(2,1)S(1)}, u32[]{:S(2)}, u32[]{:S(2)}) collective-permute-start(bf16[64,128]{1,0:T(8,128)(2,1)S(1)} %get-tuple-element.38), channel_id=1, source_target_pairs={{0,160},{64,224},{128,0},{192,64},{32,128},{96,192},{160,32},{224,... | collective-permute-start | bytes 49160 | tf_op jit(solution)/shard_map/ppermute | solution.py:255
  88.5 0.3 collective-permute-start.13
  88.8 0.8 collective-permute-done.11
  89.6 1.7 %collective-permute-done.12 = bf16[64,128]{1,0:T(8,128)(2,1)S(1)} collective-permute-done((bf16[64,128]{1,0:T(8,128)(2,1)S(1)}, bf16[64,128]{1,0:T(8,128)(2,1)S(1)}, u32[]{:S(2)}, u32[]{:S(2)}) %collective-permute-start.12) | collective-permute-done | bytes 16416 | tf_op jit(solution)/shard_map/ppermute | solution.py:255
  91.3 0.5 collective-permute-done.13
  91.8 0.6 fusion
  92.4 15.0 %all-to-all-done.2.g_ref = bf16[32,256,128]{2,1,0:T(8,128)(2,1)S(1)} async-done(((bf16[32,256,128]{2,1,0:T(8,128)(2,1)}), bf16[32,256,128]{2,1,0:T(8,128)(2,1)S(1)}, u32[]{:S(2)}, u32[]{:S(2)}) %all-to-all-start.2) | async-done | bytes 2097184 | tf_op jit(solution)/shard_map/all_to_all | solution.py:348
  107.4 1.6 %shard_map.89 = (bf16[128,4096]{1,0:T(8,128)(2,1)}, bf16[128,4096]{1,0:T(8,128)(2,1)}) custom-call(bf16[32,256,128]{2,1,0:T(8,128)(2,1)S(1)} %all-to-all-done.2.g_ref), custom_call_target="tpu_custom_call" | custom-call | tf_op jit(solution)/shard_map/pallas_call | solution.py:352
  (9 shorter events, 0.0 us)
Async XLA Ops:
  3.8 8.6 %copy-start = (bf16[128,128]{1,0:T(8,128)(2,1)S(1)}, bf16[128,128]{1,0:T(8,128)(2,1)}, u32[]{:S(2)}) copy-start(bf16[128,128]{1,0:T(8,128)(2,1)} %get-tuple-element.24.refs_0_) | copy-start | bytes 98308
  3.8 38.3 %all-to-all-start = ((bf16[32,272,128]{2,1,0:T(8,128)(2,1)}), bf16[32,272,128]{2,1,0:T(8,128)(2,1)S(1)}, u32[]{:S(2)}, u32[]{:S(2)}) async-start(bf16[32,272,128]{2,1,0:T(8,128)(2,1)} %get-tuple-element.23), calls=%async_computation | async-start | bytes 4456448 | tf_op jit(solution)/shard_map/all_to_all | solution.py:303
  12.4 11.8 %collective-permute-start.6 = (bf16[128,128]{1,0:T(8,128)(2,1)S(1)}, bf16[128,128]{1,0:T(8,128)(2,1)S(1)}, u32[]{:S(2)}, u32[]{:S(2)}) collective-permute-start(bf16[128,128]{1,0:T(8,128)(2,1)S(1)} %copy-done), channel_id=1, source_target_pairs={{0,224},{64,0},{128,64},{192,128},{32,192},{96,32},{160,96},{224,1... | collective-permute-start | bytes 98312 | tf_op jit(solution)/shard_map/ppermute | solution.py:255
  18.1 8.3 %collective-permute-start.5 = (bf16[128,128]{1,0:T(8,128)(2,1)S(1)}, bf16[128,128]{1,0:T(8,128)(2,1)S(1)}, u32[]{:S(2)}, u32[]{:S(2)}) collective-permute-start(bf16[128,128]{1,0:T(8,128)(2,1)S(1)} %copy-done), channel_id=1, source_target_pairs={{0,160},{64,224},{128,0},{192,64},{32,128},{96,192},{160,32},{224,... | collective-permute-start | bytes 98312 | tf_op jit(solution)/shard_map/ppermute | solution.py:255
  19.3 8.5 %collective-permute-start.4 = (bf16[128,128]{1,0:T(8,128)(2,1)S(1)}, bf16[128,128]{1,0:T(8,128)(2,1)S(1)}, u32[]{:S(2)}, u32[]{:S(2)}) collective-permute-start(bf16[128,128]{1,0:T(8,128)(2,1)S(1)} %copy-done), channel_id=1, source_target_pairs={{0,96},{64,160},{128,224},{192,0},{32,64},{96,128},{160,192},{224,... | collective-permute-start | bytes 98312 | tf_op jit(solution)/shard_map/ppermute | solution.py:255
  19.7 8.0 %collective-permute-start.3 = (bf16[128,128]{1,0:T(8,128)(2,1)S(1)}, bf16[128,128]{1,0:T(8,128)(2,1)S(1)}, u32[]{:S(2)}, u32[]{:S(2)}) collective-permute-start(bf16[128,128]{1,0:T(8,128)(2,1)S(1)} %copy-done), channel_id=1, source_target_pairs={{0,32},{64,96},{128,160},{192,224},{32,0},{96,64},{160,128},{224,1... | collective-permute-start | bytes 98312 | tf_op jit(solution)/shard_map/ppermute | solution.py:255
  24.2 6.1 %collective-permute-start.2 = (bf16[128,128]{1,0:T(8,128)(2,1)S(1)}, bf16[128,128]{1,0:T(8,128)(2,1)S(1)}, u32[]{:S(2)}, u32[]{:S(2)}) collective-permute-start(bf16[128,128]{1,0:T(8,128)(2,1)S(1)} %copy-done), channel_id=1, source_target_pairs={{0,192},{64,32},{128,96},{192,160},{32,224},{96,0},{160,64},{224,1... | collective-permute-start | bytes 98312 | tf_op jit(solution)/shard_map/ppermute | solution.py:255
  24.2 6.7 %collective-permute-start.1 = (bf16[128,128]{1,0:T(8,128)(2,1)S(1)}, bf16[128,128]{1,0:T(8,128)(2,1)S(1)}, u32[]{:S(2)}, u32[]{:S(2)}) collective-permute-start(bf16[128,128]{1,0:T(8,128)(2,1)S(1)} %copy-done), channel_id=1, source_target_pairs={{0,128},{64,192},{128,32},{192,96},{32,160},{96,224},{160,0},{224,... | collective-permute-start | bytes 98312 | tf_op jit(solution)/shard_map/ppermute | solution.py:255
  26.4 4.5 %collective-permute-start = (bf16[128,128]{1,0:T(8,128)(2,1)S(1)}, bf16[128,128]{1,0:T(8,128)(2,1)S(1)}, u32[]{:S(2)}, u32[]{:S(2)}) collective-permute-start(bf16[128,128]{1,0:T(8,128)(2,1)S(1)} %copy-done), channel_id=1, source_target_pairs={{0,64},{64,128},{128,192},{192,32},{32,96},{96,160},{160,224},{224... | collective-permute-start | bytes 98312 | tf_op jit(solution)/shard_map/ppermute | solution.py:255
  72.8 34.6 %all-to-all-start.2 = ((bf16[32,256,128]{2,1,0:T(8,128)(2,1)}), bf16[32,256,128]{2,1,0:T(8,128)(2,1)S(1)}, u32[]{:S(2)}, u32[]{:S(2)}) async-start(bf16[32,256,128]{2,1,0:T(8,128)(2,1)} %get-tuple-element.40), calls=%async_computation.2 | async-start | bytes 4194304 | tf_op jit(solution)/shard_map/all_to_all | solution.py:348
  79.0 7.8 %collective-permute-start.7 = (bf16[64,128]{1,0:T(8,128)(2,1)S(1)}, bf16[64,128]{1,0:T(8,128)(2,1)S(1)}, u32[]{:S(2)}, u32[]{:S(2)}) collective-permute-start(bf16[64,128]{1,0:T(8,128)(2,1)S(1)} %get-tuple-element.33), channel_id=1, source_target_pairs={{0,64},{64,128},{128,192},{192,32},{32,96},{96,160},{160,224},{224... | collective-permute-start | bytes 49160 | tf_op jit(solution)/shard_map/ppermute | solution.py:255
  79.3 9.2 %collective-permute-start.8 = (bf16[64,128]{1,0:T(8,128)(2,1)S(1)}, bf16[64,128]{1,0:T(8,128)(2,1)S(1)}, u32[]{:S(2)}, u32[]{:S(2)}) collective-permute-start(bf16[64,128]{1,0:T(8,128)(2,1)S(1)} %get-tuple-element.34), channel_id=1, source_target_pairs={{0,128},{64,192},{128,32},{192,96},{32,160},{96,224},{160,0},{224,... | collective-permute-start | bytes 49160 | tf_op jit(solution)/shard_map/ppermute | solution.py:255
  79.5 9.3 %collective-permute-start.9 = (bf16[64,128]{1,0:T(8,128)(2,1)S(1)}, bf16[64,128]{1,0:T(8,128)(2,1)S(1)}, u32[]{:S(2)}, u32[]{:S(2)}) collective-permute-start(bf16[64,128]{1,0:T(8,128)(2,1)S(1)} %get-tuple-element.35), channel_id=1, source_target_pairs={{0,192},{64,32},{128,96},{192,160},{32,224},{96,0},{160,64},{224,1... | collective-permute-start | bytes 49160 | tf_op jit(solution)/shard_map/ppermute | solution.py:255
  81.6 7.2 %collective-permute-start.10 = (bf16[64,128]{1,0:T(8,128)(2,1)S(1)}, bf16[64,128]{1,0:T(8,128)(2,1)S(1)}, u32[]{:S(2)}, u32[]{:S(2)}) collective-permute-start(bf16[64,128]{1,0:T(8,128)(2,1)S(1)} %get-tuple-element.36), channel_id=1, source_target_pairs={{0,32},{64,96},{128,160},{192,224},{32,0},{96,64},{160,128},{224,1... | collective-permute-start | bytes 49160 | tf_op jit(solution)/shard_map/ppermute | solution.py:255
  84.9 4.7 %collective-permute-start.11 = (bf16[64,128]{1,0:T(8,128)(2,1)S(1)}, bf16[64,128]{1,0:T(8,128)(2,1)S(1)}, u32[]{:S(2)}, u32[]{:S(2)}) collective-permute-start(bf16[64,128]{1,0:T(8,128)(2,1)S(1)} %get-tuple-element.37), channel_id=1, source_target_pairs={{0,96},{64,160},{128,224},{192,0},{32,64},{96,128},{160,192},{224,... | collective-permute-start | bytes 49160 | tf_op jit(solution)/shard_map/ppermute | solution.py:255
  86.7 4.5 %collective-permute-start.12 = (bf16[64,128]{1,0:T(8,128)(2,1)S(1)}, bf16[64,128]{1,0:T(8,128)(2,1)S(1)}, u32[]{:S(2)}, u32[]{:S(2)}) collective-permute-start(bf16[64,128]{1,0:T(8,128)(2,1)S(1)} %get-tuple-element.38), channel_id=1, source_target_pairs={{0,160},{64,224},{128,0},{192,64},{32,128},{96,192},{160,32},{224,... | collective-permute-start | bytes 49160 | tf_op jit(solution)/shard_map/ppermute | solution.py:255
  88.5 3.3 %collective-permute-start.13 = (bf16[64,128]{1,0:T(8,128)(2,1)S(1)}, bf16[64,128]{1,0:T(8,128)(2,1)S(1)}, u32[]{:S(2)}, u32[]{:S(2)}) collective-permute-start(bf16[64,128]{1,0:T(8,128)(2,1)S(1)} %get-tuple-element.39), channel_id=1, source_target_pairs={{0,224},{64,0},{128,64},{192,128},{32,192},{96,32},{160,96},{224,1... | collective-permute-start | bytes 49160 | tf_op jit(solution)/shard_map/ppermute | solution.py:255

commit v6 on v5

--- a/solution.py
+++ b/solution.py
@@ -190,9 +190,8 @@
 
 
 def grads_kernel(*refs):
-    a_ref, k_ref, q_ref, d_ref, dt_ref, p_ref, b_ref, g_ref = refs[:8]
-    gq_refs, (l_s, r_s, acc_s, part_s, g_s, sems) = refs[8 : 8 + LAYERS], refs[8 + LAYERS :]
-    acc_s[...] = jnp.zeros(acc_s.shape, f32)
+    a_ref, k_ref, q_ref, d_ref, dt_ref, p_ref, b_ref, g_ref, gl_ref, kt_ref = refs[:10]
+    l_s, r_s, gl_s, kt_s, g_s, sems = refs[10:]
     for head in range(2):
         for half in range(2):
             at = 2 * head + half
@@ -210,16 +209,20 @@
     flat = (count * ROWS, TOKENS)
     parts = (MERGED,) + SPLIT
 
-    def store_of(step):
+    def stores_of(step):
         at = pl.ds(step * count, count)
-        return pltpu.make_async_copy(g_s.at[at], g_ref.at[at], sems.at[step])
+        pairs = [(gl_s.at[head, step], gl_ref.at[head, step]) for head in range(2)]
+        pairs += [(kt_s.at[step], kt_ref.at[step]), (g_s.at[at], g_ref.at[at])]
+        copy = pltpu.make_async_copy
+        return [copy(src, dst, sems.at[step, i]) for i, (src, dst) in enumerate(pairs)]
 
     def one_step(step, carry):
         first = step * count
-        keys_t = block_of(k_ref, first, count, 0).astype(f32).T.astype(bf16)
+        stores = stores_of(step)
+        kt_s[step] = block_of(k_ref, first, count, 0).astype(f32).T.astype(bf16)
+        stores[2].start()
         values = block_of(k_ref, first, count, ROWS)
-        gk = jnp.zeros(values.shape, f32)
-        gv = jnp.zeros(values.shape, f32)
+        both_weights, both_grads = [], []
         for head in range(2):
             blocks = pl.ds(MERGED * step, MERGED)
             scale = jnp.exp(b_ref[head, blocks] - l_s[head][None])
@@ -228,25 +231,49 @@
             grad = weights * (probs - r_s[head])
             weights = weights.reshape(flat).astype(bf16)
             grad = grad.reshape(flat).astype(bf16)
-            gv = gv + dot(weights, d_ref[head])
-            gk = gk + dot(grad, q_ref[head])
-            acc_s[head] += dot(keys_t[head * HD : (head + 1) * HD, :], grad)
+            gl_s[head, step] = grad
+            stores[head].start()
+            both_weights.append(weights)
+            both_grads.append(grad)
+        gv = dot(jnp.concatenate(both_weights, axis=1), d_ref[...].reshape(2 * TOKENS, LANES))
+        gk = dot(jnp.concatenate(both_grads, axis=1), q_ref[...].reshape(2 * TOKENS, LANES))
         shape = (count, ROWS, LANES)
         g_s[pl.ds(first, count), :ROWS, :] = gk.astype(bf16).reshape(shape)
         g_s[pl.ds(first, count), ROWS:, :] = gv.astype(bf16).reshape(shape)
-        store_of(step).start()
+        stores[3].start()
         return carry
 
     steps = PEERS // count
     lax.fori_loop(0, steps, one_step, 0)
+    for step in range(steps):
+        for store in stores_of(step):
+            store.wait()
+
+
+def query_kernel(gl_ref, kt_ref, *refs):
+    gq_refs, (gl_s, kt_s, part_s, sems) = refs[:LAYERS], refs[LAYERS:]
+    steps = sems.shape[0]
+    copy = pltpu.make_async_copy
+    loads = []
+    for step in range(steps):
+        pairs = [(gl_ref.at[head, step], gl_s.at[head, step]) for head in range(2)]
+        pairs += [(kt_ref.at[step], kt_s.at[step])]
+        loads.append([copy(src, dst, sems.at[step, i]) for i, (src, dst) in enumerate(pairs)])
+    for load in sum(loads, []):
+        load.start()
+    sums = [0.0, 0.0]
+    for step in range(steps):
+        for load in loads[step]:
+            load.wait()
+        for head in range(2):
+            mine = kt_s[step, head * HD : (head + 1) * HD, :]
+            sums[head] = sums[head] + dot(mine, gl_s[head, step])
     for block in range(TOKENS // ROWS):
         for head in range(2):
-            part = acc_s[head, :, block * ROWS : (block + 1) * ROWS] * FACTOR
+            part = sums[head][:, block * ROWS : (block + 1) * ROWS] * FACTOR
             part_s[4 * head + block] = part.astype(bf16)
     for r in range(LAYERS):
         gq_refs[r][...] = part_s[lax.rem(layer_index() + r, LAYERS)]
-    for step in range(steps):
-        store_of(step).wait()
 
 
 def permuted(array, distance):
@@ -330,22 +357,44 @@
         compiler_params=limit(24),
     )(rows, qt, dt)
     all_stats = exchange(stats, COLUMN)
-    grads, *query_parts = pl.pallas_call(
+    steps = blocks // MERGED
+    merged = MERGED * JOINED * ROWS
+    grads, grad_logits, keys_t = pl.pallas_call(
         grads_kernel,
         in_specs=[vmem] * 7,
-        out_specs=[hbm] + [vmem] * LAYERS,
-        out_shape=[pltpu.HBM((PEERS, 2 * ROWS, LANES), bf16)] + [shape((HD, ROWS), bf16)] * LAYERS,
+        out_specs=[hbm] * 3,
+        out_shape=[
+            pltpu.HBM((PEERS, 2 * ROWS, LANES), bf16),
+            pltpu.HBM((2, steps, merged, TOKENS), bf16),
+            pltpu.HBM((steps, LANES, merged), bf16),
+        ],
         scratch_shapes=[
             scratch(2, 8, TOKENS, dtype=f32),
             scratch(2, 8, TOKENS, dtype=f32),
-            scratch(2, HD, TOKENS, dtype=f32),
-            scratch(LAYERS, HD, ROWS),
+            scratch(2, steps, merged, TOKENS),
+            scratch(steps, LANES, merged),
             scratch(PEERS, 2 * ROWS, LANES),
-            dma((blocks // MERGED,)),
-        ],
-        compiler_params=limit(32),
+            dma((steps, 4)),
+        ],
+        compiler_params=limit(38),
     )(all_stats, rows, q, d, dt, weights, maxima)
     own_rows = exchange(grads, PLANE)
+    query_parts = pl.pallas_call(
+        query_kernel,
+        in_specs=[hbm] * 2,
+        out_specs=[vmem] * LAYERS,
+        out_shape=[shape((HD, ROWS), bf16)] * LAYERS,
+        scratch_shapes=[
+            scratch(2, steps, merged, TOKENS),
+            scratch(steps, LANES, merged),
+            scratch(LAYERS, HD, ROWS),
+            dma((steps, 3)),
+        ],
+        compiler_params=limit(48),
+        cost_estimate=pl.CostEstimate(
+            flops=4 * PEERS * ROWS * HD * TOKENS, bytes_accessed=9 * MIB, transcendentals=0
+        ),
+    )(grad_logits, keys_t)
     own_parts = permuted_parts(query_parts)
     total = functools.reduce(jnp.add, [part.astype(f32) for part in own_parts])
     grad_queries = total.astype(bf16).T

time: 109 us -> 109 us (level)
  waiting for transfers between devices: 32.1 us -> 28 us
  Pallas kernels: 20.5 us -> 23.9 us
    all_to_all x1, waiting for transfers between devices: 15 us -> 10.9 us  [per_device(): own_rows = exchange(grads, PLANE)]
    pallas_call x1 -> x2, Pallas kernels: 9.48 us -> 13 us  [the longest x1 8.94 us: per_device(): pl.pallas_call(grads_kernel, in_specs=[vmem] * 7, out_specs=[hbm] * 3, ou...]
  transfers between devices with their start and end apart: 16 -> 16, of which waited for: 7 -> 7; matrix products, arithmetic and copies ran while one was open for 1% -> 1% of each run, Pallas kernels for 0% -> 4%
where the time goes in v6:
time: 109 us
  starting transfers between devices  40 us (37%)
  waiting for transfers between devices  28 us (26%)
  Pallas kernels  23.9 us (22%)
  blocking collectives  15.2 us (14%)
    ppermute x14, starting transfers between devices, permuted(): return lax.ppermute(array, ('s', 'h'), pairs)  25.1 us
    all_to_all x1, blocking collectives, per_device(): all_stats = exchange(stats, COLUMN)  15.2 us
    all_to_all x1, waiting for transfers between devices, per_device(): rows = exchange(packed, PLANE)  11 us
    all_to_all x1, waiting for transfers between devices, per_device(): own_rows = exchange(grads, PLANE)  10.9 us
    pallas_call x1, Pallas kernels, per_device(): pl.pallas_call(grads_kernel, in_specs=[vmem] * 7, out_specs=[hbm] * 3, ou...  8.94 us
    all_to_all x1, starting transfers between devices, per_device(): rows = exchange(packed, PLANE)  8.6 us
    all_to_all x1, starting transfers between devices, per_device(): own_rows = exchange(grads, PLANE)  6.32 us
    ppermute x14, waiting for transfers between devices, permuted(): return lax.ppermute(array, ('s', 'h'), pairs)  6.14 us
  transfers between devices with their start and end apart: 16, of which 7 were waited for; matrix products, arithmetic and copies ran while one was open for 1% of the time, Pallas kernels for 4%

profile of v6, /device:TPU:1, one launch (start us, length us, event | category | flops | bytes accessed | tf_op | source)
XLA Modules:
  0.0 108.7 jit_solution(4108780214605633162)
XLA Ops:
  0.6 3.1 %shard_map.85 = (bf16[32,272,128]{2,1,0:T(8,128)(2,1)}, bf16[128,128]{1,0:T(8,128)(2,1)}) custom-call(bf16[128,4096]{1,0:T(8,128)(2,1)} %k_ref.1, bf16[128,4096]{1,0:T(8,128)(2,1)} %v_ref.1, s32[1,128]{1,0:T(1,128)} %bitcast.8, bf16[64,128]{1,0:T(8,128)(2,1)} %bitcast.6, bf16[64,128]{1,0:T(8,128)(2,1)} %bitcast.7, s32[1,128]{1,0:T(1,128)} %bitcast.9), custom_call_target="tpu_custom_call" | custom-call | tf_op jit(solution)/shard_map/pallas_call | solution.py:299
  3.8 0.0 copy-start.1
  3.8 8.6 %all-to-all-start = ((bf16[32,272,128]{2,1,0:T(8,128)(2,1)}), bf16[32,272,128]{2,1,0:T(8,128)(2,1)S(1)}, u32[]{:S(2)}, u32[]{:S(2)}) async-start(bf16[32,272,128]{2,1,0:T(8,128)(2,1)} %get-tuple-element.25), calls=%async_computation | async-start | bytes 4456448 | tf_op jit(solution)/shard_map/all_to_all | solution.py:330
  12.4 5.7 %collective-permute-start.6 = (bf16[128,128]{1,0:T(8,128)(2,1)S(1)}, bf16[128,128]{1,0:T(8,128)(2,1)S(1)}, u32[]{:S(2)}, u32[]{:S(2)}) collective-permute-start(bf16[128,128]{1,0:T(8,128)(2,1)S(1)} %copy-done.1), channel_id=1, source_target_pairs={{0,224},{64,0},{128,64},{192,128},{32,192},{96,32},{160,96},{224,1... | collective-permute-start | bytes 98312 | tf_op jit(solution)/shard_map/ppermute | solution.py:282
  18.0 1.2 %collective-permute-start.5 = (bf16[128,128]{1,0:T(8,128)(2,1)S(1)}, bf16[128,128]{1,0:T(8,128)(2,1)S(1)}, u32[]{:S(2)}, u32[]{:S(2)}) collective-permute-start(bf16[128,128]{1,0:T(8,128)(2,1)S(1)} %copy-done.1), channel_id=1, source_target_pairs={{0,160},{64,224},{128,0},{192,64},{32,128},{96,192},{160,32},{224,... | collective-permute-start | bytes 98312 | tf_op jit(solution)/shard_map/ppermute | solution.py:282
  19.2 0.4 collective-permute-start.4
  19.7 4.5 %collective-permute-start.3 = (bf16[128,128]{1,0:T(8,128)(2,1)S(1)}, bf16[128,128]{1,0:T(8,128)(2,1)S(1)}, u32[]{:S(2)}, u32[]{:S(2)}) collective-permute-start(bf16[128,128]{1,0:T(8,128)(2,1)S(1)} %copy-done.1), channel_id=1, source_target_pairs={{0,32},{64,96},{128,160},{192,224},{32,0},{96,64},{160,128},{224,1... | collective-permute-start | bytes 98312 | tf_op jit(solution)/shard_map/ppermute | solution.py:282
  24.2 2.2 %collective-permute-start.1 = (bf16[128,128]{1,0:T(8,128)(2,1)S(1)}, bf16[128,128]{1,0:T(8,128)(2,1)S(1)}, u32[]{:S(2)}, u32[]{:S(2)}) collective-permute-start(bf16[128,128]{1,0:T(8,128)(2,1)S(1)} %copy-done.1), channel_id=1, source_target_pairs={{0,128},{64,192},{128,32},{192,96},{32,160},{96,224},{160,0},{224,... | collective-permute-start | bytes 98312 | tf_op jit(solution)/shard_map/ppermute | solution.py:282
  26.3 1.4 %collective-permute-start = (bf16[128,128]{1,0:T(8,128)(2,1)S(1)}, bf16[128,128]{1,0:T(8,128)(2,1)S(1)}, u32[]{:S(2)}, u32[]{:S(2)}) collective-permute-start(bf16[128,128]{1,0:T(8,128)(2,1)S(1)} %copy-done.1), channel_id=1, source_target_pairs={{0,64},{64,128},{128,192},{192,32},{32,96},{96,160},{160,224},{224... | collective-permute-start | bytes 98312 | tf_op jit(solution)/shard_map/ppermute | solution.py:282
  27.7 2.5 %collective-permute-done.2.refs_3_ = bf16[128,128]{1,0:T(8,128)(2,1)S(1)} collective-permute-done((bf16[128,128]{1,0:T(8,128)(2,1)S(1)}, bf16[128,128]{1,0:T(8,128)(2,1)S(1)}, u32[]{:S(2)}, u32[]{:S(2)}) %collective-permute-start.2) | collective-permute-done | bytes 32800 | tf_op jit(solution)/shard_map/ppermute | solution.py:282
  30.2 0.6 collective-permute-done.1.refs_2_
  30.9 0.3 shard_map.86
  31.1 11.0 %all-to-all-done.k_ref.refs_1_ = bf16[32,272,128]{2,1,0:T(8,128)(2,1)S(1)} async-done(((bf16[32,272,128]{2,1,0:T(8,128)(2,1)}), bf16[32,272,128]{2,1,0:T(8,128)(2,1)S(1)}, u32[]{:S(2)}, u32[]{:S(2)}) %all-to-all-start) | async-done | bytes 2228256 | tf_op jit(solution)/shard_map/all_to_all | solution.py:330
  42.1 6.0 %shard_map.87 = (f32[8,8,256]{2,1,0:T(8,128)S(1)}, bf16[2,16,256,512]{3,2,1,0:T(8,128)(2,1)S(1)}, f32[2,16,8,512]{3,2,1,0:T(8,128)S(1)}) custom-call(bf16[32,272,128]{2,1,0:T(8,128)(2,1)S(1)} %all-to-all-done.k_ref.refs_1_, bf16[2,128,512]{2,1,0:T(8,128)(2,1)S(1)} %get-tuple-element.27.qt_ref, bf16[2,128,512]{2,1,0:T(8,128)(2,1)S(1)} %get-tuple-element.28.dt_ref.refs_4_), custom_call_target="tpu_custom_call" | custom-call | tf_op jit(solution)/shard_map/pallas_call | solution.py:343
  48.1 15.2 %all_to_all.15.refs_0_ = f32[8,8,256]{2,1,0:T(8,128)S(1)} all-to-all(f32[8,8,256]{2,1,0:T(8,128)S(1)} %get-tuple-element.29), channel_id=1, replica_groups=mesh['s'=4,'h'=2,'x'=4,'y'=4,'c'=2] {'h','s'}, dimensions={0} | all-to-all | bytes 131072 | tf_op jit(solution)/shard_map/all_to_all | solution.py:359
  63.3 8.9 %shard_map.88 = (bf16[32,256,128]{2,1,0:T(8,128)(2,1)}, bf16[2,4,1024,512]{3,2,1,0:T(8,128)(2,1)}, bf16[4,128,1024]{2,1,0:T(8,128)(2,1)}) custom-call(f32[8,8,256]{2,1,0:T(8,128)S(1)} %all_to_all.15.refs_0_, bf16[32,272,128]{2,1,0:T(8,128)(2,1)S(1)} %all-to-all-done.k_ref.refs_1_, bf16[2,512,128]{2,1,0:T(8,128)(2,1)S(1)} %get-tuple-element.30.refs_2_, ...), custom_call_target="tpu_custom_call" | custom-call | tf_op jit(solution)/shard_map/pallas_call | solution.py:362
  72.2 0.0 copy-start
  72.2 6.3 %all-to-all-start.2 = ((bf16[32,256,128]{2,1,0:T(8,128)(2,1)}), bf16[32,256,128]{2,1,0:T(8,128)(2,1)S(1)}, u32[]{:S(2)}, u32[]{:S(2)}) async-start(bf16[32,256,128]{2,1,0:T(8,128)(2,1)} %get-tuple-element.44), calls=%async_computation.2 | async-start | bytes 4194304 | tf_op jit(solution)/shard_map/all_to_all | solution.py:381
  78.6 4.0 %shard_map.89 = (bf16[64,128]{1,0:T(8,128)(2,1)S(1)}, bf16[64,128]{1,0:T(8,128)(2,1)S(1)}, bf16[64,128]{1,0:T(8,128)(2,1)S(1)}, bf16[64,128]{1,0:T(8,128)(2,1)S(...) custom-call(bf16[2,4,1024,512]{3,2,1,0:T(8,128)(2,1)} %get-tuple-ele, ...), custom_call_target="tpu_custom_call" | custom-call | flops 536870912 | bytes 9437184 | tf_op jit(solution)/shard_map/pallas_call | solution.py:382
  82.6 0.3 collective-permute-start.7
  82.9 0.2 collective-permute-start.8
  83.1 2.1 %collective-permute-start.9 = (bf16[64,128]{1,0:T(8,128)(2,1)S(1)}, bf16[64,128]{1,0:T(8,128)(2,1)S(1)}, u32[]{:S(2)}, u32[]{:S(2)}) collective-permute-start(bf16[64,128]{1,0:T(8,128)(2,1)S(1)} %get-tuple-element.39), channel_id=1, source_target_pairs={{0,192},{64,32},{128,96},{192,160},{32,224},{96,0},{160,64},{224,1... | collective-permute-start | bytes 49160 | tf_op jit(solution)/shard_map/ppermute | solution.py:282
  85.2 3.3 %collective-permute-start.10 = (bf16[64,128]{1,0:T(8,128)(2,1)S(1)}, bf16[64,128]{1,0:T(8,128)(2,1)S(1)}, u32[]{:S(2)}, u32[]{:S(2)}) collective-permute-start(bf16[64,128]{1,0:T(8,128)(2,1)S(1)} %get-tuple-element.40), channel_id=1, source_target_pairs={{0,32},{64,96},{128,160},{192,224},{32,0},{96,64},{160,128},{224,1... | collective-permute-start | bytes 49160 | tf_op jit(solution)/shard_map/ppermute | solution.py:282
  88.5 1.8 %collective-permute-start.11 = (bf16[64,128]{1,0:T(8,128)(2,1)S(1)}, bf16[64,128]{1,0:T(8,128)(2,1)S(1)}, u32[]{:S(2)}, u32[]{:S(2)}) collective-permute-start(bf16[64,128]{1,0:T(8,128)(2,1)S(1)} %get-tuple-element.41), channel_id=1, source_target_pairs={{0,96},{64,160},{128,224},{192,0},{32,64},{96,128},{160,192},{224,... | collective-permute-start | bytes 49160 | tf_op jit(solution)/shard_map/ppermute | solution.py:282
  90.3 1.8 %collective-permute-start.12 = (bf16[64,128]{1,0:T(8,128)(2,1)S(1)}, bf16[64,128]{1,0:T(8,128)(2,1)S(1)}, u32[]{:S(2)}, u32[]{:S(2)}) collective-permute-start(bf16[64,128]{1,0:T(8,128)(2,1)S(1)} %get-tuple-element.42), channel_id=1, source_target_pairs={{0,160},{64,224},{128,0},{192,64},{32,128},{96,192},{160,32},{224,... | collective-permute-start | bytes 49160 | tf_op jit(solution)/shard_map/ppermute | solution.py:282
  92.1 0.3 collective-permute-start.13
  92.4 0.8 collective-permute-done.11
  93.2 1.7 %collective-permute-done.12 = bf16[64,128]{1,0:T(8,128)(2,1)S(1)} collective-permute-done((bf16[64,128]{1,0:T(8,128)(2,1)S(1)}, bf16[64,128]{1,0:T(8,128)(2,1)S(1)}, u32[]{:S(2)}, u32[]{:S(2)}) %collective-permute-start.12) | collective-permute-done | bytes 16416 | tf_op jit(solution)/shard_map/ppermute | solution.py:282
  94.9 0.5 collective-permute-done.13
  95.4 0.6 fusion
  96.0 10.9 %all-to-all-done.2.g_ref = bf16[32,256,128]{2,1,0:T(8,128)(2,1)S(1)} async-done(((bf16[32,256,128]{2,1,0:T(8,128)(2,1)}), bf16[32,256,128]{2,1,0:T(8,128)(2,1)S(1)}, u32[]{:S(2)}, u32[]{:S(2)}) %all-to-all-start.2) | async-done | bytes 2097184 | tf_op jit(solution)/shard_map/all_to_all | solution.py:381
  106.9 1.6 %shard_map.90 = (bf16[128,4096]{1,0:T(8,128)(2,1)}, bf16[128,4096]{1,0:T(8,128)(2,1)}) custom-call(bf16[32,256,128]{2,1,0:T(8,128)(2,1)S(1)} %all-to-all-done.2.g_ref), custom_call_target="tpu_custom_call" | custom-call | tf_op jit(solution)/shard_map/pallas_call | solution.py:401
  (12 shorter events, 0.0 us)
Async XLA Ops:
  3.8 8.6 %copy-start.1 = (bf16[128,128]{1,0:T(8,128)(2,1)S(1)}, bf16[128,128]{1,0:T(8,128)(2,1)}, u32[]{:S(2)}) copy-start(bf16[128,128]{1,0:T(8,128)(2,1)} %get-tuple-element.26.refs_0_) | copy-start | bytes 98308
  3.8 38.3 %all-to-all-start = ((bf16[32,272,128]{2,1,0:T(8,128)(2,1)}), bf16[32,272,128]{2,1,0:T(8,128)(2,1)S(1)}, u32[]{:S(2)}, u32[]{:S(2)}) async-start(bf16[32,272,128]{2,1,0:T(8,128)(2,1)} %get-tuple-element.25), calls=%async_computation | async-start | bytes 4456448 | tf_op jit(solution)/shard_map/all_to_all | solution.py:330
  12.4 11.8 %collective-permute-start.6 = (bf16[128,128]{1,0:T(8,128)(2,1)S(1)}, bf16[128,128]{1,0:T(8,128)(2,1)S(1)}, u32[]{:S(2)}, u32[]{:S(2)}) collective-permute-start(bf16[128,128]{1,0:T(8,128)(2,1)S(1)} %copy-done.1), channel_id=1, source_target_pairs={{0,224},{64,0},{128,64},{192,128},{32,192},{96,32},{160,96},{224,1... | collective-permute-start | bytes 98312 | tf_op jit(solution)/shard_map/ppermute | solution.py:282
  18.0 8.3 %collective-permute-start.5 = (bf16[128,128]{1,0:T(8,128)(2,1)S(1)}, bf16[128,128]{1,0:T(8,128)(2,1)S(1)}, u32[]{:S(2)}, u32[]{:S(2)}) collective-permute-start(bf16[128,128]{1,0:T(8,128)(2,1)S(1)} %copy-done.1), channel_id=1, source_target_pairs={{0,160},{64,224},{128,0},{192,64},{32,128},{96,192},{160,32},{224,... | collective-permute-start | bytes 98312 | tf_op jit(solution)/shard_map/ppermute | solution.py:282
  19.2 8.5 %collective-permute-start.4 = (bf16[128,128]{1,0:T(8,128)(2,1)S(1)}, bf16[128,128]{1,0:T(8,128)(2,1)S(1)}, u32[]{:S(2)}, u32[]{:S(2)}) collective-permute-start(bf16[128,128]{1,0:T(8,128)(2,1)S(1)} %copy-done.1), channel_id=1, source_target_pairs={{0,96},{64,160},{128,224},{192,0},{32,64},{96,128},{160,192},{224,... | collective-permute-start | bytes 98312 | tf_op jit(solution)/shard_map/ppermute | solution.py:282
  19.7 8.0 %collective-permute-start.3 = (bf16[128,128]{1,0:T(8,128)(2,1)S(1)}, bf16[128,128]{1,0:T(8,128)(2,1)S(1)}, u32[]{:S(2)}, u32[]{:S(2)}) collective-permute-start(bf16[128,128]{1,0:T(8,128)(2,1)S(1)} %copy-done.1), channel_id=1, source_target_pairs={{0,32},{64,96},{128,160},{192,224},{32,0},{96,64},{160,128},{224,1... | collective-permute-start | bytes 98312 | tf_op jit(solution)/shard_map/ppermute | solution.py:282
  24.1 6.1 %collective-permute-start.2 = (bf16[128,128]{1,0:T(8,128)(2,1)S(1)}, bf16[128,128]{1,0:T(8,128)(2,1)S(1)}, u32[]{:S(2)}, u32[]{:S(2)}) collective-permute-start(bf16[128,128]{1,0:T(8,128)(2,1)S(1)} %copy-done.1), channel_id=1, source_target_pairs={{0,192},{64,32},{128,96},{192,160},{32,224},{96,0},{160,64},{224,1... | collective-permute-start | bytes 98312 | tf_op jit(solution)/shard_map/ppermute | solution.py:282
  24.2 6.7 %collective-permute-start.1 = (bf16[128,128]{1,0:T(8,128)(2,1)S(1)}, bf16[128,128]{1,0:T(8,128)(2,1)S(1)}, u32[]{:S(2)}, u32[]{:S(2)}) collective-permute-start(bf16[128,128]{1,0:T(8,128)(2,1)S(1)} %copy-done.1), channel_id=1, source_target_pairs={{0,128},{64,192},{128,32},{192,96},{32,160},{96,224},{160,0},{224,... | collective-permute-start | bytes 98312 | tf_op jit(solution)/shard_map/ppermute | solution.py:282
  26.3 4.5 %collective-permute-start = (bf16[128,128]{1,0:T(8,128)(2,1)S(1)}, bf16[128,128]{1,0:T(8,128)(2,1)S(1)}, u32[]{:S(2)}, u32[]{:S(2)}) collective-permute-start(bf16[128,128]{1,0:T(8,128)(2,1)S(1)} %copy-done.1), channel_id=1, source_target_pairs={{0,64},{64,128},{128,192},{192,32},{32,96},{96,160},{160,224},{224... | collective-permute-start | bytes 98312 | tf_op jit(solution)/shard_map/ppermute | solution.py:282
  72.2 6.3 %copy-start = (bf16[4,128,1024]{2,1,0:T(8,128)(2,1)S(1)}, bf16[4,128,1024]{2,1,0:T(8,128)(2,1)}, u32[]{:S(2)}) copy-start(bf16[4,128,1024]{2,1,0:T(8,128)(2,1)} %get-tuple-element.35.kt_ref) | copy-start | bytes 3145732
  72.2 34.7 %all-to-all-start.2 = ((bf16[32,256,128]{2,1,0:T(8,128)(2,1)}), bf16[32,256,128]{2,1,0:T(8,128)(2,1)S(1)}, u32[]{:S(2)}, u32[]{:S(2)}) async-start(bf16[32,256,128]{2,1,0:T(8,128)(2,1)} %get-tuple-element.44), calls=%async_computation.2 | async-start | bytes 4194304 | tf_op jit(solution)/shard_map/all_to_all | solution.py:381
  82.6 7.8 %collective-permute-start.7 = (bf16[64,128]{1,0:T(8,128)(2,1)S(1)}, bf16[64,128]{1,0:T(8,128)(2,1)S(1)}, u32[]{:S(2)}, u32[]{:S(2)}) collective-permute-start(bf16[64,128]{1,0:T(8,128)(2,1)S(1)} %get-tuple-element.37), channel_id=1, source_target_pairs={{0,64},{64,128},{128,192},{192,32},{32,96},{96,160},{160,224},{224... | collective-permute-start | bytes 49160 | tf_op jit(solution)/shard_map/ppermute | solution.py:282
  82.9 9.2 %collective-permute-start.8 = (bf16[64,128]{1,0:T(8,128)(2,1)S(1)}, bf16[64,128]{1,0:T(8,128)(2,1)S(1)}, u32[]{:S(2)}, u32[]{:S(2)}) collective-permute-start(bf16[64,128]{1,0:T(8,128)(2,1)S(1)} %get-tuple-element.38), channel_id=1, source_target_pairs={{0,128},{64,192},{128,32},{192,96},{32,160},{96,224},{160,0},{224,... | collective-permute-start | bytes 49160 | tf_op jit(solution)/shard_map/ppermute | solution.py:282
  83.1 9.3 %collective-permute-start.9 = (bf16[64,128]{1,0:T(8,128)(2,1)S(1)}, bf16[64,128]{1,0:T(8,128)(2,1)S(1)}, u32[]{:S(2)}, u32[]{:S(2)}) collective-permute-start(bf16[64,128]{1,0:T(8,128)(2,1)S(1)} %get-tuple-element.39), channel_id=1, source_target_pairs={{0,192},{64,32},{128,96},{192,160},{32,224},{96,0},{160,64},{224,1... | collective-permute-start | bytes 49160 | tf_op jit(solution)/shard_map/ppermute | solution.py:282
  85.2 7.2 %collective-permute-start.10 = (bf16[64,128]{1,0:T(8,128)(2,1)S(1)}, bf16[64,128]{1,0:T(8,128)(2,1)S(1)}, u32[]{:S(2)}, u32[]{:S(2)}) collective-permute-start(bf16[64,128]{1,0:T(8,128)(2,1)S(1)} %get-tuple-element.40), channel_id=1, source_target_pairs={{0,32},{64,96},{128,160},{192,224},{32,0},{96,64},{160,128},{224,1... | collective-permute-start | bytes 49160 | tf_op jit(solution)/shard_map/ppermute | solution.py:282
  88.5 4.7 %collective-permute-start.11 = (bf16[64,128]{1,0:T(8,128)(2,1)S(1)}, bf16[64,128]{1,0:T(8,128)(2,1)S(1)}, u32[]{:S(2)}, u32[]{:S(2)}) collective-permute-start(bf16[64,128]{1,0:T(8,128)(2,1)S(1)} %get-tuple-element.41), channel_id=1, source_target_pairs={{0,96},{64,160},{128,224},{192,0},{32,64},{96,128},{160,192},{224,... | collective-permute-start | bytes 49160 | tf_op jit(solution)/shard_map/ppermute | solution.py:282
  90.3 4.5 %collective-permute-start.12 = (bf16[64,128]{1,0:T(8,128)(2,1)S(1)}, bf16[64,128]{1,0:T(8,128)(2,1)S(1)}, u32[]{:S(2)}, u32[]{:S(2)}) collective-permute-start(bf16[64,128]{1,0:T(8,128)(2,1)S(1)} %get-tuple-element.42), channel_id=1, source_target_pairs={{0,160},{64,224},{128,0},{192,64},{32,128},{96,192},{160,32},{224,... | collective-permute-start | bytes 49160 | tf_op jit(solution)/shard_map/ppermute | solution.py:282
  92.1 3.3 %collective-permute-start.13 = (bf16[64,128]{1,0:T(8,128)(2,1)S(1)}, bf16[64,128]{1,0:T(8,128)(2,1)S(1)}, u32[]{:S(2)}, u32[]{:S(2)}) collective-permute-start(bf16[64,128]{1,0:T(8,128)(2,1)S(1)} %get-tuple-element.43), channel_id=1, source_target_pairs={{0,224},{64,0},{128,64},{192,128},{32,192},{96,32},{160,96},{224,1... | collective-permute-start | bytes 49160 | tf_op jit(solution)/shard_map/ppermute | solution.py:282

commit v7 on v6

--- a/solution.py
+++ b/solution.py
@@ -15,7 +15,7 @@
 ROWS = 128
 EXTRA = 16
 JOINED = 2
-UNROLLED = 8
+UNROLLED = 16
 MERGED = 4
 MIB = 1024 * 1024
 FACTOR = 1.0 / math.sqrt(HD)
@@ -190,8 +190,8 @@
 
 
 def grads_kernel(*refs):
-    a_ref, k_ref, q_ref, d_ref, dt_ref, p_ref, b_ref, g_ref, gl_ref, kt_ref = refs[:10]
-    l_s, r_s, gl_s, kt_s, g_s, sems = refs[10:]
+    a_ref, k_ref, q_ref, d_ref, dt_ref, p_ref, b_ref, g_ref, gl_ref, kt_ref, sum_ref = refs[:11]
+    l_s, r_s, gl_s, kt_s, g_s, sum_s, sems = refs[11:]
     for head in range(2):
         for half in range(2):
             at = 2 * head + half
@@ -209,18 +209,27 @@
     flat = (count * ROWS, TOKENS)
     parts = (MERGED,) + SPLIT
 
-    def stores_of(step):
+    steps = PEERS // count
+    last = steps - 1
+
+    def stores_of(step, is_last=False):
         at = pl.ds(step * count, count)
-        pairs = [(gl_s.at[head, step], gl_ref.at[head, step]) for head in range(2)]
-        pairs += [(kt_s.at[step], kt_ref.at[step]), (g_s.at[at], g_ref.at[at])]
+        if is_last:
+            pairs = [(sum_s, sum_ref)]
+        else:
+            pairs = [(gl_s.at[head, step], gl_ref.at[head, step]) for head in range(2)]
+            pairs += [(kt_s.at[step], kt_ref.at[step])]
+        pairs += [(g_s.at[at], g_ref.at[at])]
         copy = pltpu.make_async_copy
         return [copy(src, dst, sems.at[step, i]) for i, (src, dst) in enumerate(pairs)]
 
-    def one_step(step, carry):
+    def one_step(step, is_last=False):
         first = step * count
-        stores = stores_of(step)
-        kt_s[step] = block_of(k_ref, first, count, 0).astype(f32).T.astype(bf16)
-        stores[2].start()
+        stores = stores_of(step, is_last)
+        keys_t = block_of(k_ref, first, count, 0).astype(f32).T.astype(bf16)
+        if not is_last:
+            kt_s[step] = keys_t
+            stores[2].start()
         values = block_of(k_ref, first, count, ROWS)
         both_weights, both_grads = [], []
         for head in range(2):
@@ -231,27 +240,35 @@
             grad = weights * (probs - r_s[head])
             weights = weights.reshape(flat).astype(bf16)
             grad = grad.reshape(flat).astype(bf16)
-            gl_s[head, step] = grad
-            stores[head].start()
+            if is_last:
+                sum_s[head] = dot(keys_t[head * HD : (head + 1) * HD, :], grad)
+            else:
+                gl_s[head, step] = grad
+                stores[head].start()
             both_weights.append(weights)
             both_grads.append(grad)
+        if is_last:
+            stores[0].start()
         gv = dot(jnp.concatenate(both_weights, axis=1), d_ref[...].reshape(2 * TOKENS, LANES))
         gk = dot(jnp.concatenate(both_grads, axis=1), q_ref[...].reshape(2 * TOKENS, LANES))
         shape = (count, ROWS, LANES)
         g_s[pl.ds(first, count), :ROWS, :] = gk.astype(bf16).reshape(shape)
         g_s[pl.ds(first, count), ROWS:, :] = gv.astype(bf16).reshape(shape)
-        stores[3].start()
+        stores[-1].start()
+
+    def middle_step(step, carry):
+        one_step(step)
         return carry
 
-    steps = PEERS // count
-    lax.fori_loop(0, steps, one_step, 0)
-    for step in range(steps):
-        for store in stores_of(step):
+    lax.fori_loop(0, last, middle_step, 0)
+    one_step(last, True)
+    for step in range(steps):
+        for store in stores_of(step, step == last):
             store.wait()
 
 
-def query_kernel(gl_ref, kt_ref, *refs):
-    gq_refs, (gl_s, kt_s, part_s, sems) = refs[:LAYERS], refs[LAYERS:]
+def query_kernel(gl_ref, kt_ref, sum_ref, *refs):
+    gq_refs, (gl_s, kt_s, sum_s, part_s, sems, sum_sem) = refs[:LAYERS], refs[LAYERS:]
     steps = sems.shape[0]
     copy = pltpu.make_async_copy
     loads = []
@@ -259,9 +276,11 @@
         pairs = [(gl_ref.at[head, step], gl_s.at[head, step]) for head in range(2)]
         pairs += [(kt_ref.at[step], kt_s.at[step])]
         loads.append([copy(src, dst, sems.at[step, i]) for i, (src, dst) in enumerate(pairs)])
-    for load in sum(loads, []):
+    rest = copy(sum_ref, sum_s, sum_sem)
+    for load in [rest] + sum(loads, []):
         load.start()
-    sums = [0.0, 0.0]
+    rest.wait()
+    sums = [sum_s[0], sum_s[1]]
     for step in range(steps):
         for load in loads[step]:
             load.wait()
@@ -359,21 +378,23 @@
     all_stats = exchange(stats, COLUMN)
     steps = blocks // MERGED
     merged = MERGED * JOINED * ROWS
-    grads, grad_logits, keys_t = pl.pallas_call(
+    grads, grad_logits, keys_t, query_rest = pl.pallas_call(
         grads_kernel,
         in_specs=[vmem] * 7,
-        out_specs=[hbm] * 3,
+        out_specs=[hbm] * 4,
         out_shape=[
             pltpu.HBM((PEERS, 2 * ROWS, LANES), bf16),
-            pltpu.HBM((2, steps, merged, TOKENS), bf16),
-            pltpu.HBM((steps, LANES, merged), bf16),
+            pltpu.HBM((2, steps - 1, merged, TOKENS), bf16),
+            pltpu.HBM((steps - 1, LANES, merged), bf16),
+            pltpu.HBM((2, HD, TOKENS), f32),
         ],
         scratch_shapes=[
             scratch(2, 8, TOKENS, dtype=f32),
             scratch(2, 8, TOKENS, dtype=f32),
-            scratch(2, steps, merged, TOKENS),
-            scratch(steps, LANES, merged),
+            scratch(2, steps - 1, merged, TOKENS),
+            scratch(steps - 1, LANES, merged),
             scratch(PEERS, 2 * ROWS, LANES),
+            scratch(2, HD, TOKENS, dtype=f32),
             dma((steps, 4)),
         ],
         compiler_params=limit(38),
@@ -381,20 +402,22 @@
     own_rows = exchange(grads, PLANE)
     query_parts = pl.pallas_call(
         query_kernel,
-        in_specs=[hbm] * 2,
+        in_specs=[hbm] * 3,
         out_specs=[vmem] * LAYERS,
         out_shape=[shape((HD, ROWS), bf16)] * LAYERS,
         scratch_shapes=[
-            scratch(2, steps, merged, TOKENS),
-            scratch(steps, LANES, merged),
+            scratch(2, steps - 1, merged, TOKENS),
+            scratch(steps - 1, LANES, merged),
+            scratch(2, HD, TOKENS, dtype=f32),
             scratch(LAYERS, HD, ROWS),
-            dma((steps, 3)),
+            dma((steps - 1, 3)),
+            dma,
         ],
         compiler_params=limit(48),
         cost_estimate=pl.CostEstimate(
             flops=4 * PEERS * ROWS * HD * TOKENS, bytes_accessed=9 * MIB, transcendentals=0
         ),
-    )(grad_logits, keys_t)
+    )(grad_logits, keys_t, query_rest)
     own_parts = permuted_parts(query_parts)
     total = functools.reduce(jnp.add, [part.astype(f32) for part in own_parts])
     grad_queries = total.astype(bf16).T

time: 109 us -> 109 us (level)
  transfers between devices with their start and end apart: 16 -> 16, of which waited for: 7 -> 7; matrix products, arithmetic and copies ran while one was open for 1% -> 1% of each run, Pallas kernels for 4% -> 3%
where the time goes in v7:
time: 109 us
  starting transfers between devices  40.1 us (37%)
  waiting for transfers between devices  28.4 us (26%)
  Pallas kernels  23.5 us (22%)
  blocking collectives  15.2 us (14%)
    ppermute x14, starting transfers between devices, permuted(): return lax.ppermute(array, ('s', 'h'), pairs)  25.3 us
    all_to_all x1, blocking collectives, per_device(): all_stats = exchange(stats, COLUMN)  15.2 us
    all_to_all x1, waiting for transfers between devices, per_device(): own_rows = exchange(grads, PLANE)  11.3 us
    all_to_all x1, waiting for transfers between devices, per_device(): rows = exchange(packed, PLANE)  11 us
    pallas_call x1, Pallas kernels, per_device(): pl.pallas_call(grads_kernel, in_specs=[vmem] * 7, out_specs=[hbm] * 4, ou...  9.25 us
    all_to_all x1, starting transfers between devices, per_device(): rows = exchange(packed, PLANE)  8.6 us
    all_to_all x1, starting transfers between devices, per_device(): own_rows = exchange(grads, PLANE)  6.18 us
    ppermute x14, waiting for transfers between devices, permuted(): return lax.ppermute(array, ('s', 'h'), pairs)  6.16 us
  transfers between devices with their start and end apart: 16, of which 7 were waited for; matrix products, arithmetic and copies ran while one was open for 1% of the time, Pallas kernels for 3%

profile of v7, /device:TPU:1, one launch (start us, length us, event | category | flops | bytes accessed | tf_op | source)
XLA Modules:
  0.0 108.7 jit_solution(3600790108219645216)
XLA Ops:
  0.6 3.1 %shard_map.85 = (bf16[32,272,128]{2,1,0:T(8,128)(2,1)}, bf16[128,128]{1,0:T(8,128)(2,1)}) custom-call(bf16[128,4096]{1,0:T(8,128)(2,1)} %k_ref.1, bf16[128,4096]{1,0:T(8,128)(2,1)} %v_ref.1, s32[1,128]{1,0:T(1,128)} %bitcast.8, bf16[64,128]{1,0:T(8,128)(2,1)} %bitcast.6, bf16[64,128]{1,0:T(8,128)(2,1)} %bitcast.7, s32[1,128]{1,0:T(1,128)} %bitcast.9), custom_call_target="tpu_custom_call" | custom-call | tf_op jit(solution)/shard_map/pallas_call | solution.py:318
  3.7 0.0 copy-start.2
  3.7 8.6 %all-to-all-start = ((bf16[32,272,128]{2,1,0:T(8,128)(2,1)}), bf16[32,272,128]{2,1,0:T(8,128)(2,1)S(1)}, u32[]{:S(2)}, u32[]{:S(2)}) async-start(bf16[32,272,128]{2,1,0:T(8,128)(2,1)} %get-tuple-element.26), calls=%async_computation | async-start | bytes 4456448 | tf_op jit(solution)/shard_map/all_to_all | solution.py:349
  12.4 5.7 %collective-permute-start.6 = (bf16[128,128]{1,0:T(8,128)(2,1)S(1)}, bf16[128,128]{1,0:T(8,128)(2,1)S(1)}, u32[]{:S(2)}, u32[]{:S(2)}) collective-permute-start(bf16[128,128]{1,0:T(8,128)(2,1)S(1)} %copy-done.2), channel_id=1, source_target_pairs={{0,224},{64,0},{128,64},{192,128},{32,192},{96,32},{160,96},{224,1... | collective-permute-start | bytes 98312 | tf_op jit(solution)/shard_map/ppermute | solution.py:301
  18.0 1.2 %collective-permute-start.5 = (bf16[128,128]{1,0:T(8,128)(2,1)S(1)}, bf16[128,128]{1,0:T(8,128)(2,1)S(1)}, u32[]{:S(2)}, u32[]{:S(2)}) collective-permute-start(bf16[128,128]{1,0:T(8,128)(2,1)S(1)} %copy-done.2), channel_id=1, source_target_pairs={{0,160},{64,224},{128,0},{192,64},{32,128},{96,192},{160,32},{224,... | collective-permute-start | bytes 98312 | tf_op jit(solution)/shard_map/ppermute | solution.py:301
  19.2 0.4 collective-permute-start.4
  19.6 4.5 %collective-permute-start.3 = (bf16[128,128]{1,0:T(8,128)(2,1)S(1)}, bf16[128,128]{1,0:T(8,128)(2,1)S(1)}, u32[]{:S(2)}, u32[]{:S(2)}) collective-permute-start(bf16[128,128]{1,0:T(8,128)(2,1)S(1)} %copy-done.2), channel_id=1, source_target_pairs={{0,32},{64,96},{128,160},{192,224},{32,0},{96,64},{160,128},{224,1... | collective-permute-start | bytes 98312 | tf_op jit(solution)/shard_map/ppermute | solution.py:301
  24.1 2.2 %collective-permute-start.1 = (bf16[128,128]{1,0:T(8,128)(2,1)S(1)}, bf16[128,128]{1,0:T(8,128)(2,1)S(1)}, u32[]{:S(2)}, u32[]{:S(2)}) collective-permute-start(bf16[128,128]{1,0:T(8,128)(2,1)S(1)} %copy-done.2), channel_id=1, source_target_pairs={{0,128},{64,192},{128,32},{192,96},{32,160},{96,224},{160,0},{224,... | collective-permute-start | bytes 98312 | tf_op jit(solution)/shard_map/ppermute | solution.py:301
  26.3 1.4 %collective-permute-start = (bf16[128,128]{1,0:T(8,128)(2,1)S(1)}, bf16[128,128]{1,0:T(8,128)(2,1)S(1)}, u32[]{:S(2)}, u32[]{:S(2)}) collective-permute-start(bf16[128,128]{1,0:T(8,128)(2,1)S(1)} %copy-done.2), channel_id=1, source_target_pairs={{0,64},{64,128},{128,192},{192,32},{32,96},{96,160},{160,224},{224... | collective-permute-start | bytes 98312 | tf_op jit(solution)/shard_map/ppermute | solution.py:301
  27.7 2.5 %collective-permute-done.2.refs_3_ = bf16[128,128]{1,0:T(8,128)(2,1)S(1)} collective-permute-done((bf16[128,128]{1,0:T(8,128)(2,1)S(1)}, bf16[128,128]{1,0:T(8,128)(2,1)S(1)}, u32[]{:S(2)}, u32[]{:S(2)}) %collective-permute-start.2) | collective-permute-done | bytes 32800 | tf_op jit(solution)/shard_map/ppermute | solution.py:301
  30.2 0.6 collective-permute-done.1.refs_2_
  30.8 0.3 shard_map.86
  31.1 11.0 %all-to-all-done.k_ref.refs_1_ = bf16[32,272,128]{2,1,0:T(8,128)(2,1)S(1)} async-done(((bf16[32,272,128]{2,1,0:T(8,128)(2,1)}), bf16[32,272,128]{2,1,0:T(8,128)(2,1)S(1)}, u32[]{:S(2)}, u32[]{:S(2)}) %all-to-all-start) | async-done | bytes 2228256 | tf_op jit(solution)/shard_map/all_to_all | solution.py:349
  42.1 5.9 %shard_map.87 = (f32[8,8,256]{2,1,0:T(8,128)S(1)}, bf16[2,16,256,512]{3,2,1,0:T(8,128)(2,1)S(1)}, f32[2,16,8,512]{3,2,1,0:T(8,128)S(1)}) custom-call(bf16[32,272,128]{2,1,0:T(8,128)(2,1)S(1)} %all-to-all-done.k_ref.refs_1_, bf16[2,128,512]{2,1,0:T(8,128)(2,1)S(1)} %get-tuple-element.28.qt_ref, bf16[2,128,512]{2,1,0:T(8,128)(2,1)S(1)} %get-tuple-element.29.dt_ref.refs_4_), custom_call_target="tpu_custom_call" | custom-call | tf_op jit(solution)/shard_map/pallas_call | solution.py:362
  47.9 15.2 %all_to_all.15.refs_0_ = f32[8,8,256]{2,1,0:T(8,128)S(1)} all-to-all(f32[8,8,256]{2,1,0:T(8,128)S(1)} %get-tuple-element.30), channel_id=1, replica_groups=mesh['s'=4,'h'=2,'x'=4,'y'=4,'c'=2] {'h','s'}, dimensions={0} | all-to-all | bytes 131072 | tf_op jit(solution)/shard_map/all_to_all | solution.py:378
  63.1 9.2 %shard_map.88 = (bf16[32,256,128]{2,1,0:T(8,128)(2,1)}, bf16[2,3,1024,512]{3,2,1,0:T(8,128)(2,1)}, bf16[3,128,1024]{2,1,0:T(8,128)(2,1)}, f32[2,64,512]{2,1,0:T(8,128)}) custom-call(f32[8,8,256]{2,1,0:T(8,128)S(1)} %all_to_all.15.refs_0_, bf16[32,272,128]{2,1,0:T(8,128)(2,1)S(1)} %all-to-all-done.k_ref.refs_1_, ...), custom_call_target="tpu_custom_call" | custom-call | tf_op jit(solution)/shard_map/pallas_call | solution.py:381
  72.4 0.0 copy-start
  72.4 6.2 %all-to-all-start.2 = ((bf16[32,256,128]{2,1,0:T(8,128)(2,1)}), bf16[32,256,128]{2,1,0:T(8,128)(2,1)S(1)}, u32[]{:S(2)}, u32[]{:S(2)}) async-start(bf16[32,256,128]{2,1,0:T(8,128)(2,1)} %get-tuple-element.46), calls=%async_computation.2 | async-start | bytes 4194304 | tf_op jit(solution)/shard_map/all_to_all | solution.py:402
  78.6 3.4 %shard_map.89 = (bf16[64,128]{1,0:T(8,128)(2,1)S(1)}, bf16[64,128]{1,0:T(8,128)(2,1)S(1)}, bf16[64,128]{1,0:T(8,128)(2,1)S(1)}, bf16[64,128]{1,0:T(8,128)(2,1)S(...) custom-call(bf16[2,3,1024,512]{3,2,1,0:T(8,128)(2,1)} %get-tuple-ele, ...), custom_call_target="tpu_custom_call" | custom-call | flops 536870912 | bytes 9437184 | tf_op jit(solution)/shard_map/pallas_call | solution.py:403
  82.0 0.6 collective-permute-start.7
  82.6 0.1 collective-permute-start.8
  82.7 2.1 %collective-permute-start.9 = (bf16[64,128]{1,0:T(8,128)(2,1)S(1)}, bf16[64,128]{1,0:T(8,128)(2,1)S(1)}, u32[]{:S(2)}, u32[]{:S(2)}) collective-permute-start(bf16[64,128]{1,0:T(8,128)(2,1)S(1)} %get-tuple-element.41), channel_id=1, source_target_pairs={{0,192},{64,32},{128,96},{192,160},{32,224},{96,0},{160,64},{224,1... | collective-permute-start | bytes 49160 | tf_op jit(solution)/shard_map/ppermute | solution.py:301
  84.8 3.4 %collective-permute-start.10 = (bf16[64,128]{1,0:T(8,128)(2,1)S(1)}, bf16[64,128]{1,0:T(8,128)(2,1)S(1)}, u32[]{:S(2)}, u32[]{:S(2)}) collective-permute-start(bf16[64,128]{1,0:T(8,128)(2,1)S(1)} %get-tuple-element.42), channel_id=1, source_target_pairs={{0,32},{64,96},{128,160},{192,224},{32,0},{96,64},{160,128},{224,1... | collective-permute-start | bytes 49160 | tf_op jit(solution)/shard_map/ppermute | solution.py:301
  88.2 1.8 %collective-permute-start.11 = (bf16[64,128]{1,0:T(8,128)(2,1)S(1)}, bf16[64,128]{1,0:T(8,128)(2,1)S(1)}, u32[]{:S(2)}, u32[]{:S(2)}) collective-permute-start(bf16[64,128]{1,0:T(8,128)(2,1)S(1)} %get-tuple-element.43), channel_id=1, source_target_pairs={{0,96},{64,160},{128,224},{192,0},{32,64},{96,128},{160,192},{224,... | collective-permute-start | bytes 49160 | tf_op jit(solution)/shard_map/ppermute | solution.py:301
  90.0 1.8 %collective-permute-start.12 = (bf16[64,128]{1,0:T(8,128)(2,1)S(1)}, bf16[64,128]{1,0:T(8,128)(2,1)S(1)}, u32[]{:S(2)}, u32[]{:S(2)}) collective-permute-start(bf16[64,128]{1,0:T(8,128)(2,1)S(1)} %get-tuple-element.44), channel_id=1, source_target_pairs={{0,160},{64,224},{128,0},{192,64},{32,128},{96,192},{160,32},{224,... | collective-permute-start | bytes 49160 | tf_op jit(solution)/shard_map/ppermute | solution.py:301
  91.7 0.3 collective-permute-start.13
  92.1 0.8 collective-permute-done.11
  92.9 1.6 %collective-permute-done.12 = bf16[64,128]{1,0:T(8,128)(2,1)S(1)} collective-permute-done((bf16[64,128]{1,0:T(8,128)(2,1)S(1)}, bf16[64,128]{1,0:T(8,128)(2,1)S(1)}, u32[]{:S(2)}, u32[]{:S(2)}) %collective-permute-start.12) | collective-permute-done | bytes 16416 | tf_op jit(solution)/shard_map/ppermute | solution.py:301
  94.5 0.5 collective-permute-done.13
  95.0 0.6 fusion
  95.7 11.3 %all-to-all-done.2.g_ref = bf16[32,256,128]{2,1,0:T(8,128)(2,1)S(1)} async-done(((bf16[32,256,128]{2,1,0:T(8,128)(2,1)}), bf16[32,256,128]{2,1,0:T(8,128)(2,1)S(1)}, u32[]{:S(2)}, u32[]{:S(2)}) %all-to-all-start.2) | async-done | bytes 2097184 | tf_op jit(solution)/shard_map/all_to_all | solution.py:402
  107.0 1.6 %shard_map.90 = (bf16[128,4096]{1,0:T(8,128)(2,1)}, bf16[128,4096]{1,0:T(8,128)(2,1)}) custom-call(bf16[32,256,128]{2,1,0:T(8,128)(2,1)S(1)} %all-to-all-done.2.g_ref), custom_call_target="tpu_custom_call" | custom-call | tf_op jit(solution)/shard_map/pallas_call | solution.py:424
  (14 shorter events, 0.0 us)
Async XLA Ops:
  3.7 8.6 %copy-start.2 = (bf16[128,128]{1,0:T(8,128)(2,1)S(1)}, bf16[128,128]{1,0:T(8,128)(2,1)}, u32[]{:S(2)}) copy-start(bf16[128,128]{1,0:T(8,128)(2,1)} %get-tuple-element.27.refs_0_) | copy-start | bytes 98308
  3.7 38.3 %all-to-all-start = ((bf16[32,272,128]{2,1,0:T(8,128)(2,1)}), bf16[32,272,128]{2,1,0:T(8,128)(2,1)S(1)}, u32[]{:S(2)}, u32[]{:S(2)}) async-start(bf16[32,272,128]{2,1,0:T(8,128)(2,1)} %get-tuple-element.26), calls=%async_computation | async-start | bytes 4456448 | tf_op jit(solution)/shard_map/all_to_all | solution.py:349
  12.4 11.8 %collective-permute-start.6 = (bf16[128,128]{1,0:T(8,128)(2,1)S(1)}, bf16[128,128]{1,0:T(8,128)(2,1)S(1)}, u32[]{:S(2)}, u32[]{:S(2)}) collective-permute-start(bf16[128,128]{1,0:T(8,128)(2,1)S(1)} %copy-done.2), channel_id=1, source_target_pairs={{0,224},{64,0},{128,64},{192,128},{32,192},{96,32},{160,96},{224,1... | collective-permute-start | bytes 98312 | tf_op jit(solution)/shard_map/ppermute | solution.py:301
  18.0 8.3 %collective-permute-start.5 = (bf16[128,128]{1,0:T(8,128)(2,1)S(1)}, bf16[128,128]{1,0:T(8,128)(2,1)S(1)}, u32[]{:S(2)}, u32[]{:S(2)}) collective-permute-start(bf16[128,128]{1,0:T(8,128)(2,1)S(1)} %copy-done.2), channel_id=1, source_target_pairs={{0,160},{64,224},{128,0},{192,64},{32,128},{96,192},{160,32},{224,... | collective-permute-start | bytes 98312 | tf_op jit(solution)/shard_map/ppermute | solution.py:301
  19.2 8.5 %collective-permute-start.4 = (bf16[128,128]{1,0:T(8,128)(2,1)S(1)}, bf16[128,128]{1,0:T(8,128)(2,1)S(1)}, u32[]{:S(2)}, u32[]{:S(2)}) collective-permute-start(bf16[128,128]{1,0:T(8,128)(2,1)S(1)} %copy-done.2), channel_id=1, source_target_pairs={{0,96},{64,160},{128,224},{192,0},{32,64},{96,128},{160,192},{224,... | collective-permute-start | bytes 98312 | tf_op jit(solution)/shard_map/ppermute | solution.py:301
  19.6 8.0 %collective-permute-start.3 = (bf16[128,128]{1,0:T(8,128)(2,1)S(1)}, bf16[128,128]{1,0:T(8,128)(2,1)S(1)}, u32[]{:S(2)}, u32[]{:S(2)}) collective-permute-start(bf16[128,128]{1,0:T(8,128)(2,1)S(1)} %copy-done.2), channel_id=1, source_target_pairs={{0,32},{64,96},{128,160},{192,224},{32,0},{96,64},{160,128},{224,1... | collective-permute-start | bytes 98312 | tf_op jit(solution)/shard_map/ppermute | solution.py:301
  24.1 6.1 %collective-permute-start.2 = (bf16[128,128]{1,0:T(8,128)(2,1)S(1)}, bf16[128,128]{1,0:T(8,128)(2,1)S(1)}, u32[]{:S(2)}, u32[]{:S(2)}) collective-permute-start(bf16[128,128]{1,0:T(8,128)(2,1)S(1)} %copy-done.2), channel_id=1, source_target_pairs={{0,192},{64,32},{128,96},{192,160},{32,224},{96,0},{160,64},{224,1... | collective-permute-start | bytes 98312 | tf_op jit(solution)/shard_map/ppermute | solution.py:301
  24.1 6.7 %collective-permute-start.1 = (bf16[128,128]{1,0:T(8,128)(2,1)S(1)}, bf16[128,128]{1,0:T(8,128)(2,1)S(1)}, u32[]{:S(2)}, u32[]{:S(2)}) collective-permute-start(bf16[128,128]{1,0:T(8,128)(2,1)S(1)} %copy-done.2), channel_id=1, source_target_pairs={{0,128},{64,192},{128,32},{192,96},{32,160},{96,224},{160,0},{224,... | collective-permute-start | bytes 98312 | tf_op jit(solution)/shard_map/ppermute | solution.py:301
  26.3 4.5 %collective-permute-start = (bf16[128,128]{1,0:T(8,128)(2,1)S(1)}, bf16[128,128]{1,0:T(8,128)(2,1)S(1)}, u32[]{:S(2)}, u32[]{:S(2)}) collective-permute-start(bf16[128,128]{1,0:T(8,128)(2,1)S(1)} %copy-done.2), channel_id=1, source_target_pairs={{0,64},{64,128},{128,192},{192,32},{32,96},{96,160},{160,224},{224... | collective-permute-start | bytes 98312 | tf_op jit(solution)/shard_map/ppermute | solution.py:301
  72.4 6.2 %copy-start = (bf16[3,128,1024]{2,1,0:T(8,128)(2,1)S(1)}, bf16[3,128,1024]{2,1,0:T(8,128)(2,1)}, u32[]{:S(2)}) copy-start(bf16[3,128,1024]{2,1,0:T(8,128)(2,1)} %get-tuple-element.36.kt_ref) | copy-start | bytes 2359300
  72.4 6.2 %copy-start.1 = (f32[2,64,512]{2,1,0:T(8,128)S(1)}, f32[2,64,512]{2,1,0:T(8,128)}, u32[]{:S(2)}) copy-start(f32[2,64,512]{2,1,0:T(8,128)} %get-tuple-element.37.sum_ref) | copy-start | bytes 786436
  72.4 34.6 %all-to-all-start.2 = ((bf16[32,256,128]{2,1,0:T(8,128)(2,1)}), bf16[32,256,128]{2,1,0:T(8,128)(2,1)S(1)}, u32[]{:S(2)}, u32[]{:S(2)}) async-start(bf16[32,256,128]{2,1,0:T(8,128)(2,1)} %get-tuple-element.46), calls=%async_computation.2 | async-start | bytes 4194304 | tf_op jit(solution)/shard_map/all_to_all | solution.py:402
  82.0 7.9 %collective-permute-start.7 = (bf16[64,128]{1,0:T(8,128)(2,1)S(1)}, bf16[64,128]{1,0:T(8,128)(2,1)S(1)}, u32[]{:S(2)}, u32[]{:S(2)}) collective-permute-start(bf16[64,128]{1,0:T(8,128)(2,1)S(1)} %get-tuple-element.39), channel_id=1, source_target_pairs={{0,64},{64,128},{128,192},{192,32},{32,96},{96,160},{160,224},{224... | collective-permute-start | bytes 49160 | tf_op jit(solution)/shard_map/ppermute | solution.py:301
  82.6 9.1 %collective-permute-start.8 = (bf16[64,128]{1,0:T(8,128)(2,1)S(1)}, bf16[64,128]{1,0:T(8,128)(2,1)S(1)}, u32[]{:S(2)}, u32[]{:S(2)}) collective-permute-start(bf16[64,128]{1,0:T(8,128)(2,1)S(1)} %get-tuple-element.40), channel_id=1, source_target_pairs={{0,128},{64,192},{128,32},{192,96},{32,160},{96,224},{160,0},{224,... | collective-permute-start | bytes 49160 | tf_op jit(solution)/shard_map/ppermute | solution.py:301
  82.7 9.3 %collective-permute-start.9 = (bf16[64,128]{1,0:T(8,128)(2,1)S(1)}, bf16[64,128]{1,0:T(8,128)(2,1)S(1)}, u32[]{:S(2)}, u32[]{:S(2)}) collective-permute-start(bf16[64,128]{1,0:T(8,128)(2,1)S(1)} %get-tuple-element.41), channel_id=1, source_target_pairs={{0,192},{64,32},{128,96},{192,160},{32,224},{96,0},{160,64},{224,1... | collective-permute-start | bytes 49160 | tf_op jit(solution)/shard_map/ppermute | solution.py:301
  84.8 7.2 %collective-permute-start.10 = (bf16[64,128]{1,0:T(8,128)(2,1)S(1)}, bf16[64,128]{1,0:T(8,128)(2,1)S(1)}, u32[]{:S(2)}, u32[]{:S(2)}) collective-permute-start(bf16[64,128]{1,0:T(8,128)(2,1)S(1)} %get-tuple-element.42), channel_id=1, source_target_pairs={{0,32},{64,96},{128,160},{192,224},{32,0},{96,64},{160,128},{224,1... | collective-permute-start | bytes 49160 | tf_op jit(solution)/shard_map/ppermute | solution.py:301
  88.2 4.7 %collective-permute-start.11 = (bf16[64,128]{1,0:T(8,128)(2,1)S(1)}, bf16[64,128]{1,0:T(8,128)(2,1)S(1)}, u32[]{:S(2)}, u32[]{:S(2)}) collective-permute-start(bf16[64,128]{1,0:T(8,128)(2,1)S(1)} %get-tuple-element.43), channel_id=1, source_target_pairs={{0,96},{64,160},{128,224},{192,0},{32,64},{96,128},{160,192},{224,... | collective-permute-start | bytes 49160 | tf_op jit(solution)/shard_map/ppermute | solution.py:301
  90.0 4.5 %collective-permute-start.12 = (bf16[64,128]{1,0:T(8,128)(2,1)S(1)}, bf16[64,128]{1,0:T(8,128)(2,1)S(1)}, u32[]{:S(2)}, u32[]{:S(2)}) collective-permute-start(bf16[64,128]{1,0:T(8,128)(2,1)S(1)} %get-tuple-element.44), channel_id=1, source_target_pairs={{0,160},{64,224},{128,0},{192,64},{32,128},{96,192},{160,32},{224,... | collective-permute-start | bytes 49160 | tf_op jit(solution)/shard_map/ppermute | solution.py:301
  91.7 3.3 %collective-permute-start.13 = (bf16[64,128]{1,0:T(8,128)(2,1)S(1)}, bf16[64,128]{1,0:T(8,128)(2,1)S(1)}, u32[]{:S(2)}, u32[]{:S(2)}) collective-permute-start(bf16[64,128]{1,0:T(8,128)(2,1)S(1)} %get-tuple-element.45), channel_id=1, source_target_pairs={{0,224},{64,0},{128,64},{192,128},{32,192},{96,32},{160,96},{224,1... | collective-permute-start | bytes 49160 | tf_op jit(solution)/shard_map/ppermute | solution.py:301

commit v8 on v6

--- a/solution.py
+++ b/solution.py
@@ -15,7 +15,7 @@
 ROWS = 128
 EXTRA = 16
 JOINED = 2
-UNROLLED = 8
+UNROLLED = 16
 MERGED = 4
 MIB = 1024 * 1024
 FACTOR = 1.0 / math.sqrt(HD)

time: 109 us -> 109 us (level)
  no operation moved by 1% of the time
where the time goes in v8:
time: 109 us; the launch traced here: 108 us
  starting transfers between devices  39.8 us (37%)
  waiting for transfers between devices  28.1 us (26%)
  Pallas kernels  23.8 us (22%)
  blocking collectives  15.2 us (14%)
    ppermute x14, starting transfers between devices, permuted(): return lax.ppermute(array, ('s', 'h'), pairs)  25.1 us
    all_to_all x1, blocking collectives, per_device(): all_stats = exchange(stats, COLUMN)  15.2 us
    all_to_all x1, waiting for transfers between devices, per_device(): rows = exchange(packed, PLANE)  11 us
    all_to_all x1, waiting for transfers between devices, per_device(): own_rows = exchange(grads, PLANE)  10.9 us
    pallas_call x1, Pallas kernels, per_device(): pl.pallas_call(grads_kernel, in_specs=[vmem] * 7, out_specs=[hbm] * 3, ou...  8.94 us
    all_to_all x1, starting transfers between devices, per_device(): rows = exchange(packed, PLANE)  8.6 us
    ppermute x14, waiting for transfers between devices, permuted(): return lax.ppermute(array, ('s', 'h'), pairs)  6.16 us
    all_to_all x1, starting transfers between devices, per_device(): own_rows = exchange(grads, PLANE)  6.15 us
  transfers between devices with their start and end apart: 16, of which 7 were waited for; matrix products, arithmetic and copies ran while one was open for 1% of the time, Pallas kernels for 4%

profile of v8, /device:TPU:1, one launch (start us, length us, event | category | flops | bytes accessed | tf_op | source)
XLA Modules:
  0.0 108.4 jit_solution(13252964223946818371)
XLA Ops:
  0.6 3.1 %shard_map.85 = (bf16[32,272,128]{2,1,0:T(8,128)(2,1)}, bf16[128,128]{1,0:T(8,128)(2,1)}) custom-call(bf16[128,4096]{1,0:T(8,128)(2,1)} %k_ref.1, bf16[128,4096]{1,0:T(8,128)(2,1)} %v_ref.1, s32[1,128]{1,0:T(1,128)} %bitcast.8, bf16[64,128]{1,0:T(8,128)(2,1)} %bitcast.6, bf16[64,128]{1,0:T(8,128)(2,1)} %bitcast.7, s32[1,128]{1,0:T(1,128)} %bitcast.9), custom_call_target="tpu_custom_call" | custom-call | tf_op jit(solution)/shard_map/pallas_call | solution.py:299
  3.8 0.0 copy-start.1
  3.8 8.6 %all-to-all-start = ((bf16[32,272,128]{2,1,0:T(8,128)(2,1)}), bf16[32,272,128]{2,1,0:T(8,128)(2,1)S(1)}, u32[]{:S(2)}, u32[]{:S(2)}) async-start(bf16[32,272,128]{2,1,0:T(8,128)(2,1)} %get-tuple-element.25), calls=%async_computation | async-start | bytes 4456448 | tf_op jit(solution)/shard_map/all_to_all | solution.py:330
  12.4 5.7 %collective-permute-start.6 = (bf16[128,128]{1,0:T(8,128)(2,1)S(1)}, bf16[128,128]{1,0:T(8,128)(2,1)S(1)}, u32[]{:S(2)}, u32[]{:S(2)}) collective-permute-start(bf16[128,128]{1,0:T(8,128)(2,1)S(1)} %copy-done.1), channel_id=1, source_target_pairs={{0,224},{64,0},{128,64},{192,128},{32,192},{96,32},{160,96},{224,1... | collective-permute-start | bytes 98312 | tf_op jit(solution)/shard_map/ppermute | solution.py:282
  18.0 1.2 %collective-permute-start.5 = (bf16[128,128]{1,0:T(8,128)(2,1)S(1)}, bf16[128,128]{1,0:T(8,128)(2,1)S(1)}, u32[]{:S(2)}, u32[]{:S(2)}) collective-permute-start(bf16[128,128]{1,0:T(8,128)(2,1)S(1)} %copy-done.1), channel_id=1, source_target_pairs={{0,160},{64,224},{128,0},{192,64},{32,128},{96,192},{160,32},{224,... | collective-permute-start | bytes 98312 | tf_op jit(solution)/shard_map/ppermute | solution.py:282
  19.2 0.4 collective-permute-start.4
  19.7 4.5 %collective-permute-start.3 = (bf16[128,128]{1,0:T(8,128)(2,1)S(1)}, bf16[128,128]{1,0:T(8,128)(2,1)S(1)}, u32[]{:S(2)}, u32[]{:S(2)}) collective-permute-start(bf16[128,128]{1,0:T(8,128)(2,1)S(1)} %copy-done.1), channel_id=1, source_target_pairs={{0,32},{64,96},{128,160},{192,224},{32,0},{96,64},{160,128},{224,1... | collective-permute-start | bytes 98312 | tf_op jit(solution)/shard_map/ppermute | solution.py:282
  24.2 2.2 %collective-permute-start.1 = (bf16[128,128]{1,0:T(8,128)(2,1)S(1)}, bf16[128,128]{1,0:T(8,128)(2,1)S(1)}, u32[]{:S(2)}, u32[]{:S(2)}) collective-permute-start(bf16[128,128]{1,0:T(8,128)(2,1)S(1)} %copy-done.1), channel_id=1, source_target_pairs={{0,128},{64,192},{128,32},{192,96},{32,160},{96,224},{160,0},{224,... | collective-permute-start | bytes 98312 | tf_op jit(solution)/shard_map/ppermute | solution.py:282
  26.3 1.4 %collective-permute-start = (bf16[128,128]{1,0:T(8,128)(2,1)S(1)}, bf16[128,128]{1,0:T(8,128)(2,1)S(1)}, u32[]{:S(2)}, u32[]{:S(2)}) collective-permute-start(bf16[128,128]{1,0:T(8,128)(2,1)S(1)} %copy-done.1), channel_id=1, source_target_pairs={{0,64},{64,128},{128,192},{192,32},{32,96},{96,160},{160,224},{224... | collective-permute-start | bytes 98312 | tf_op jit(solution)/shard_map/ppermute | solution.py:282
  27.7 2.5 %collective-permute-done.2.refs_3_ = bf16[128,128]{1,0:T(8,128)(2,1)S(1)} collective-permute-done((bf16[128,128]{1,0:T(8,128)(2,1)S(1)}, bf16[128,128]{1,0:T(8,128)(2,1)S(1)}, u32[]{:S(2)}, u32[]{:S(2)}) %collective-permute-start.2) | collective-permute-done | bytes 32800 | tf_op jit(solution)/shard_map/ppermute | solution.py:282
  30.2 0.6 collective-permute-done.1.refs_2_
  30.9 0.3 shard_map.86
  31.1 11.0 %all-to-all-done.k_ref.refs_1_ = bf16[32,272,128]{2,1,0:T(8,128)(2,1)S(1)} async-done(((bf16[32,272,128]{2,1,0:T(8,128)(2,1)}), bf16[32,272,128]{2,1,0:T(8,128)(2,1)S(1)}, u32[]{:S(2)}, u32[]{:S(2)}) %all-to-all-start) | async-done | bytes 2228256 | tf_op jit(solution)/shard_map/all_to_all | solution.py:330
  42.1 5.9 %shard_map.87 = (f32[8,8,256]{2,1,0:T(8,128)S(1)}, bf16[2,16,256,512]{3,2,1,0:T(8,128)(2,1)S(1)}, f32[2,16,8,512]{3,2,1,0:T(8,128)S(1)}) custom-call(bf16[32,272,128]{2,1,0:T(8,128)(2,1)S(1)} %all-to-all-done.k_ref.refs_1_, bf16[2,128,512]{2,1,0:T(8,128)(2,1)S(1)} %get-tuple-element.27.qt_ref, bf16[2,128,512]{2,1,0:T(8,128)(2,1)S(1)} %get-tuple-element.28.dt_ref.refs_4_), custom_call_target="tpu_custom_call" | custom-call | tf_op jit(solution)/shard_map/pallas_call | solution.py:343
  48.0 15.2 %all_to_all.15.refs_0_ = f32[8,8,256]{2,1,0:T(8,128)S(1)} all-to-all(f32[8,8,256]{2,1,0:T(8,128)S(1)} %get-tuple-element.29), channel_id=1, replica_groups=mesh['s'=4,'h'=2,'x'=4,'y'=4,'c'=2] {'h','s'}, dimensions={0} | all-to-all | bytes 131072 | tf_op jit(solution)/shard_map/all_to_all | solution.py:359
  63.2 8.9 %shard_map.88 = (bf16[32,256,128]{2,1,0:T(8,128)(2,1)}, bf16[2,4,1024,512]{3,2,1,0:T(8,128)(2,1)}, bf16[4,128,1024]{2,1,0:T(8,128)(2,1)}) custom-call(f32[8,8,256]{2,1,0:T(8,128)S(1)} %all_to_all.15.refs_0_, bf16[32,272,128]{2,1,0:T(8,128)(2,1)S(1)} %all-to-all-done.k_ref.refs_1_, bf16[2,512,128]{2,1,0:T(8,128)(2,1)S(1)} %get-tuple-element.30.refs_2_, ...), custom_call_target="tpu_custom_call" | custom-call | tf_op jit(solution)/shard_map/pallas_call | solution.py:362
  72.1 0.0 copy-start
  72.1 6.1 %all-to-all-start.2 = ((bf16[32,256,128]{2,1,0:T(8,128)(2,1)}), bf16[32,256,128]{2,1,0:T(8,128)(2,1)S(1)}, u32[]{:S(2)}, u32[]{:S(2)}) async-start(bf16[32,256,128]{2,1,0:T(8,128)(2,1)} %get-tuple-element.44), calls=%async_computation.2 | async-start | bytes 4194304 | tf_op jit(solution)/shard_map/all_to_all | solution.py:381
  78.3 4.0 %shard_map.89 = (bf16[64,128]{1,0:T(8,128)(2,1)S(1)}, bf16[64,128]{1,0:T(8,128)(2,1)S(1)}, bf16[64,128]{1,0:T(8,128)(2,1)S(1)}, bf16[64,128]{1,0:T(8,128)(2,1)S(...) custom-call(bf16[2,4,1024,512]{3,2,1,0:T(8,128)(2,1)} %get-tuple-ele, ...), custom_call_target="tpu_custom_call" | custom-call | flops 536870912 | bytes 9437184 | tf_op jit(solution)/shard_map/pallas_call | solution.py:382
  82.3 0.3 collective-permute-start.7
  82.7 0.1 collective-permute-start.8
  82.8 2.1 %collective-permute-start.9 = (bf16[64,128]{1,0:T(8,128)(2,1)S(1)}, bf16[64,128]{1,0:T(8,128)(2,1)S(1)}, u32[]{:S(2)}, u32[]{:S(2)}) collective-permute-start(bf16[64,128]{1,0:T(8,128)(2,1)S(1)} %get-tuple-element.39), channel_id=1, source_target_pairs={{0,192},{64,32},{128,96},{192,160},{32,224},{96,0},{160,64},{224,1... | collective-permute-start | bytes 49160 | tf_op jit(solution)/shard_map/ppermute | solution.py:282
  84.9 3.3 %collective-permute-start.10 = (bf16[64,128]{1,0:T(8,128)(2,1)S(1)}, bf16[64,128]{1,0:T(8,128)(2,1)S(1)}, u32[]{:S(2)}, u32[]{:S(2)}) collective-permute-start(bf16[64,128]{1,0:T(8,128)(2,1)S(1)} %get-tuple-element.40), channel_id=1, source_target_pairs={{0,32},{64,96},{128,160},{192,224},{32,0},{96,64},{160,128},{224,1... | collective-permute-start | bytes 49160 | tf_op jit(solution)/shard_map/ppermute | solution.py:282
  88.2 1.8 %collective-permute-start.11 = (bf16[64,128]{1,0:T(8,128)(2,1)S(1)}, bf16[64,128]{1,0:T(8,128)(2,1)S(1)}, u32[]{:S(2)}, u32[]{:S(2)}) collective-permute-start(bf16[64,128]{1,0:T(8,128)(2,1)S(1)} %get-tuple-element.41), channel_id=1, source_target_pairs={{0,96},{64,160},{128,224},{192,0},{32,64},{96,128},{160,192},{224,... | collective-permute-start | bytes 49160 | tf_op jit(solution)/shard_map/ppermute | solution.py:282
  90.0 1.8 %collective-permute-start.12 = (bf16[64,128]{1,0:T(8,128)(2,1)S(1)}, bf16[64,128]{1,0:T(8,128)(2,1)S(1)}, u32[]{:S(2)}, u32[]{:S(2)}) collective-permute-start(bf16[64,128]{1,0:T(8,128)(2,1)S(1)} %get-tuple-element.42), channel_id=1, source_target_pairs={{0,160},{64,224},{128,0},{192,64},{32,128},{96,192},{160,32},{224,... | collective-permute-start | bytes 49160 | tf_op jit(solution)/shard_map/ppermute | solution.py:282
  91.8 0.3 collective-permute-start.13
  92.1 0.8 collective-permute-done.11
  92.9 1.6 %collective-permute-done.12 = bf16[64,128]{1,0:T(8,128)(2,1)S(1)} collective-permute-done((bf16[64,128]{1,0:T(8,128)(2,1)S(1)}, bf16[64,128]{1,0:T(8,128)(2,1)S(1)}, u32[]{:S(2)}, u32[]{:S(2)}) %collective-permute-start.12) | collective-permute-done | bytes 16416 | tf_op jit(solution)/shard_map/ppermute | solution.py:282
  94.6 0.5 collective-permute-done.13
  95.1 0.6 fusion
  95.7 10.9 %all-to-all-done.2.g_ref = bf16[32,256,128]{2,1,0:T(8,128)(2,1)S(1)} async-done(((bf16[32,256,128]{2,1,0:T(8,128)(2,1)}), bf16[32,256,128]{2,1,0:T(8,128)(2,1)S(1)}, u32[]{:S(2)}, u32[]{:S(2)}) %all-to-all-start.2) | async-done | bytes 2097184 | tf_op jit(solution)/shard_map/all_to_all | solution.py:381
  106.7 1.6 %shard_map.90 = (bf16[128,4096]{1,0:T(8,128)(2,1)}, bf16[128,4096]{1,0:T(8,128)(2,1)}) custom-call(bf16[32,256,128]{2,1,0:T(8,128)(2,1)S(1)} %all-to-all-done.2.g_ref), custom_call_target="tpu_custom_call" | custom-call | tf_op jit(solution)/shard_map/pallas_call | solution.py:401
  (12 shorter events, 0.0 us)
Async XLA Ops:
  3.8 8.6 %copy-start.1 = (bf16[128,128]{1,0:T(8,128)(2,1)S(1)}, bf16[128,128]{1,0:T(8,128)(2,1)}, u32[]{:S(2)}) copy-start(bf16[128,128]{1,0:T(8,128)(2,1)} %get-tuple-element.26.refs_0_) | copy-start | bytes 98308
  3.8 38.3 %all-to-all-start = ((bf16[32,272,128]{2,1,0:T(8,128)(2,1)}), bf16[32,272,128]{2,1,0:T(8,128)(2,1)S(1)}, u32[]{:S(2)}, u32[]{:S(2)}) async-start(bf16[32,272,128]{2,1,0:T(8,128)(2,1)} %get-tuple-element.25), calls=%async_computation | async-start | bytes 4456448 | tf_op jit(solution)/shard_map/all_to_all | solution.py:330
  12.4 11.8 %collective-permute-start.6 = (bf16[128,128]{1,0:T(8,128)(2,1)S(1)}, bf16[128,128]{1,0:T(8,128)(2,1)S(1)}, u32[]{:S(2)}, u32[]{:S(2)}) collective-permute-start(bf16[128,128]{1,0:T(8,128)(2,1)S(1)} %copy-done.1), channel_id=1, source_target_pairs={{0,224},{64,0},{128,64},{192,128},{32,192},{96,32},{160,96},{224,1... | collective-permute-start | bytes 98312 | tf_op jit(solution)/shard_map/ppermute | solution.py:282
  18.0 8.3 %collective-permute-start.5 = (bf16[128,128]{1,0:T(8,128)(2,1)S(1)}, bf16[128,128]{1,0:T(8,128)(2,1)S(1)}, u32[]{:S(2)}, u32[]{:S(2)}) collective-permute-start(bf16[128,128]{1,0:T(8,128)(2,1)S(1)} %copy-done.1), channel_id=1, source_target_pairs={{0,160},{64,224},{128,0},{192,64},{32,128},{96,192},{160,32},{224,... | collective-permute-start | bytes 98312 | tf_op jit(solution)/shard_map/ppermute | solution.py:282
  19.2 8.5 %collective-permute-start.4 = (bf16[128,128]{1,0:T(8,128)(2,1)S(1)}, bf16[128,128]{1,0:T(8,128)(2,1)S(1)}, u32[]{:S(2)}, u32[]{:S(2)}) collective-permute-start(bf16[128,128]{1,0:T(8,128)(2,1)S(1)} %copy-done.1), channel_id=1, source_target_pairs={{0,96},{64,160},{128,224},{192,0},{32,64},{96,128},{160,192},{224,... | collective-permute-start | bytes 98312 | tf_op jit(solution)/shard_map/ppermute | solution.py:282
  19.7 8.0 %collective-permute-start.3 = (bf16[128,128]{1,0:T(8,128)(2,1)S(1)}, bf16[128,128]{1,0:T(8,128)(2,1)S(1)}, u32[]{:S(2)}, u32[]{:S(2)}) collective-permute-start(bf16[128,128]{1,0:T(8,128)(2,1)S(1)} %copy-done.1), channel_id=1, source_target_pairs={{0,32},{64,96},{128,160},{192,224},{32,0},{96,64},{160,128},{224,1... | collective-permute-start | bytes 98312 | tf_op jit(solution)/shard_map/ppermute | solution.py:282
  24.1 6.1 %collective-permute-start.2 = (bf16[128,128]{1,0:T(8,128)(2,1)S(1)}, bf16[128,128]{1,0:T(8,128)(2,1)S(1)}, u32[]{:S(2)}, u32[]{:S(2)}) collective-permute-start(bf16[128,128]{1,0:T(8,128)(2,1)S(1)} %copy-done.1), channel_id=1, source_target_pairs={{0,192},{64,32},{128,96},{192,160},{32,224},{96,0},{160,64},{224,1... | collective-permute-start | bytes 98312 | tf_op jit(solution)/shard_map/ppermute | solution.py:282
  24.2 6.7 %collective-permute-start.1 = (bf16[128,128]{1,0:T(8,128)(2,1)S(1)}, bf16[128,128]{1,0:T(8,128)(2,1)S(1)}, u32[]{:S(2)}, u32[]{:S(2)}) collective-permute-start(bf16[128,128]{1,0:T(8,128)(2,1)S(1)} %copy-done.1), channel_id=1, source_target_pairs={{0,128},{64,192},{128,32},{192,96},{32,160},{96,224},{160,0},{224,... | collective-permute-start | bytes 98312 | tf_op jit(solution)/shard_map/ppermute | solution.py:282
  26.3 4.5 %collective-permute-start = (bf16[128,128]{1,0:T(8,128)(2,1)S(1)}, bf16[128,128]{1,0:T(8,128)(2,1)S(1)}, u32[]{:S(2)}, u32[]{:S(2)}) collective-permute-start(bf16[128,128]{1,0:T(8,128)(2,1)S(1)} %copy-done.1), channel_id=1, source_target_pairs={{0,64},{64,128},{128,192},{192,32},{32,96},{96,160},{160,224},{224... | collective-permute-start | bytes 98312 | tf_op jit(solution)/shard_map/ppermute | solution.py:282
  72.1 6.2 %copy-start = (bf16[4,128,1024]{2,1,0:T(8,128)(2,1)S(1)}, bf16[4,128,1024]{2,1,0:T(8,128)(2,1)}, u32[]{:S(2)}) copy-start(bf16[4,128,1024]{2,1,0:T(8,128)(2,1)} %get-tuple-element.35.kt_ref) | copy-start | bytes 3145732
  72.1 34.5 %all-to-all-start.2 = ((bf16[32,256,128]{2,1,0:T(8,128)(2,1)}), bf16[32,256,128]{2,1,0:T(8,128)(2,1)S(1)}, u32[]{:S(2)}, u32[]{:S(2)}) async-start(bf16[32,256,128]{2,1,0:T(8,128)(2,1)} %get-tuple-element.44), calls=%async_computation.2 | async-start | bytes 4194304 | tf_op jit(solution)/shard_map/all_to_all | solution.py:381
  82.3 7.7 %collective-permute-start.7 = (bf16[64,128]{1,0:T(8,128)(2,1)S(1)}, bf16[64,128]{1,0:T(8,128)(2,1)S(1)}, u32[]{:S(2)}, u32[]{:S(2)}) collective-permute-start(bf16[64,128]{1,0:T(8,128)(2,1)S(1)} %get-tuple-element.37), channel_id=1, source_target_pairs={{0,64},{64,128},{128,192},{192,32},{32,96},{96,160},{160,224},{224... | collective-permute-start | bytes 49160 | tf_op jit(solution)/shard_map/ppermute | solution.py:282
  82.7 9.2 %collective-permute-start.8 = (bf16[64,128]{1,0:T(8,128)(2,1)S(1)}, bf16[64,128]{1,0:T(8,128)(2,1)S(1)}, u32[]{:S(2)}, u32[]{:S(2)}) collective-permute-start(bf16[64,128]{1,0:T(8,128)(2,1)S(1)} %get-tuple-element.38), channel_id=1, source_target_pairs={{0,128},{64,192},{128,32},{192,96},{32,160},{96,224},{160,0},{224,... | collective-permute-start | bytes 49160 | tf_op jit(solution)/shard_map/ppermute | solution.py:282
  82.8 9.3 %collective-permute-start.9 = (bf16[64,128]{1,0:T(8,128)(2,1)S(1)}, bf16[64,128]{1,0:T(8,128)(2,1)S(1)}, u32[]{:S(2)}, u32[]{:S(2)}) collective-permute-start(bf16[64,128]{1,0:T(8,128)(2,1)S(1)} %get-tuple-element.39), channel_id=1, source_target_pairs={{0,192},{64,32},{128,96},{192,160},{32,224},{96,0},{160,64},{224,1... | collective-permute-start | bytes 49160 | tf_op jit(solution)/shard_map/ppermute | solution.py:282
  84.9 7.2 %collective-permute-start.10 = (bf16[64,128]{1,0:T(8,128)(2,1)S(1)}, bf16[64,128]{1,0:T(8,128)(2,1)S(1)}, u32[]{:S(2)}, u32[]{:S(2)}) collective-permute-start(bf16[64,128]{1,0:T(8,128)(2,1)S(1)} %get-tuple-element.40), channel_id=1, source_target_pairs={{0,32},{64,96},{128,160},{192,224},{32,0},{96,64},{160,128},{224,1... | collective-permute-start | bytes 49160 | tf_op jit(solution)/shard_map/ppermute | solution.py:282
  88.2 4.7 %collective-permute-start.11 = (bf16[64,128]{1,0:T(8,128)(2,1)S(1)}, bf16[64,128]{1,0:T(8,128)(2,1)S(1)}, u32[]{:S(2)}, u32[]{:S(2)}) collective-permute-start(bf16[64,128]{1,0:T(8,128)(2,1)S(1)} %get-tuple-element.41), channel_id=1, source_target_pairs={{0,96},{64,160},{128,224},{192,0},{32,64},{96,128},{160,192},{224,... | collective-permute-start | bytes 49160 | tf_op jit(solution)/shard_map/ppermute | solution.py:282
  90.0 4.5 %collective-permute-start.12 = (bf16[64,128]{1,0:T(8,128)(2,1)S(1)}, bf16[64,128]{1,0:T(8,128)(2,1)S(1)}, u32[]{:S(2)}, u32[]{:S(2)}) collective-permute-start(bf16[64,128]{1,0:T(8,128)(2,1)S(1)} %get-tuple-element.42), channel_id=1, source_target_pairs={{0,160},{64,224},{128,0},{192,64},{32,128},{96,192},{160,32},{224,... | collective-permute-start | bytes 49160 | tf_op jit(solution)/shard_map/ppermute | solution.py:282
  91.8 3.3 %collective-permute-start.13 = (bf16[64,128]{1,0:T(8,128)(2,1)S(1)}, bf16[64,128]{1,0:T(8,128)(2,1)S(1)}, u32[]{:S(2)}, u32[]{:S(2)}) collective-permute-start(bf16[64,128]{1,0:T(8,128)(2,1)S(1)} %get-tuple-element.43), channel_id=1, source_target_pairs={{0,224},{64,0},{128,64},{192,128},{32,192},{96,32},{160,96},{224,1... | collective-permute-start | bytes 49160 | tf_op jit(solution)/shard_map/ppermute | solution.py:282
